TPU v7x, 512 devices: a whole 4x8x8 slice. The times are simulated.
512 devices in a mesh: leaf: 512 (over z, x, y, core).
Axes of the slice: x: 4, y: 8, z: 8, core: 2. Of those that a mesh axis runs over, the one named last changes fastest.
Arguments:
- embeddings: bfloat16 [1048576, 256], P('leaf'), may hold values from -12 to 12
- rhs: bfloat16 [1048576, 64], P('leaf'), may hold values from -6 to 6
- item_order: int32 [1048576], P('leaf'), may hold values from 0 to 2047, as said below
- leaf_basis: bfloat16 [1048576, 32], P('leaf'), may hold values from -0.375 to 0.375
- leaf_skel: int32 [4096, 32], P('leaf'), may hold values from 0 to 255, as said below
- local_transfer: bfloat16 [7680, 32, 32], P('leaf'), may hold values from -0.875 to 0.875
- local_pick: int32 [3584, 32], P('leaf'), may hold values from 0 to 63, as said below
- upper_transfer: bfloat16 [512, 32, 32], replicated, may hold values from -0.875 to 0.875
- upper_pick: int32 [512, 32], replicated, may hold values from 0 to 63, as said below
Outputs:
- product: bfloat16 [1048576, 64], P('leaf')
Inputs may be any that keep to these rules, and one draw needn't show every extreme that they name: `item_order`: each block of 2048 entries is a permutation of 0 to 2047. `leaf_skel`: each row holds 32 different numbers. `local_pick`: each row holds 32 different numbers. `upper_pick`: each row holds 32 different numbers.
All inputs are finite; a program needn't handle non-finite values.
Results may differ from a plain program's by a relative error of at most 0.0043.
Values may be sent and summed in bfloat16 or wider, within the bound.
No kernel may reach another device: no remote copies, remote signals or barrier semaphores. Data moves between devices by JAX's collectives and lax.ppermute only.
A program may use at most 64 MiB of HBM per device.

v0:
```python
import jax
import jax.numpy as jnp
from jax import lax
from jax.sharding import PartitionSpec as P

RIDGE = 1.0
HIGHEST = lax.Precision.HIGHEST


def swapped(array, axis, stride):
    return lax.ppermute(array, axis, [(i, i ^ 1 << stride) for i in range(lax.axis_size(axis))])


def kernel_block(left, right):
    gram = jnp.einsum("nme,nke->nmk", left, right, preferred_element_type=jnp.float32)
    left_norm = jnp.einsum("nme,nme->nm", left, left, preferred_element_type=jnp.float32)
    right_norm = jnp.einsum("nke,nke->nk", right, right, preferred_element_type=jnp.float32)
    distance = jnp.maximum(left_norm[:, :, None] + right_norm[:, None, :] - 2.0 * gram, 0.0)
    return 1.0 / jnp.sqrt(1.0 + distance / left.shape[-1])


def lift(transfer, weights):
    return jnp.einsum("nab,nac->nbc", transfer.astype(jnp.float32), weights, precision=HIGHEST)


def lower(transfer, field):
    return jnp.einsum("nab,nbc->nac", transfer.astype(jnp.float32), field, precision=HIGHEST)


def couple(own_points, sibling_points, sibling_weights):
    return jnp.einsum(
        "nmk,nkc->nmc", kernel_block(own_points, sibling_points), sibling_weights, precision=HIGHEST
    )


def pair_total(terms):
    paired = terms.reshape((-1, 2) + terms.shape[1:])
    return paired[:, 0] + paired[:, 1]


def pair_select(points, selection):
    joined = points.reshape(-1, 2 * points.shape[1], points.shape[2])
    return jnp.take_along_axis(joined, selection[:, :, None], axis=1)


def swap_pairs(values):
    paired = values.reshape((-1, 2) + values.shape[1:])
    return paired[:, ::-1].reshape(values.shape)


def descend(point_levels, weight_levels, transfer_levels, field):
    for height in reversed(range(len(weight_levels))):
        points = point_levels[height]
        term = couple(points, swap_pairs(points), swap_pairs(weight_levels[height]))
        term = term + lower(transfer_levels[height], jnp.repeat(field, 2, axis=0))
        field = term
    return field


def local(
    embeddings,
    rhs,
    item_order,
    leaf_basis,
    leaf_skel,
    local_transfer,
    local_pick,
    upper_transfer,
    upper_pick,
):
    leaf_count, rank = leaf_skel.shape
    leaf_size = rhs.shape[0] // leaf_count
    feats = embeddings[item_order].reshape(leaf_count, leaf_size, -1)
    weights = rhs[item_order].reshape(leaf_count, leaf_size, -1)
    kernel = kernel_block(feats, feats) + RIDGE * jnp.eye(leaf_size, dtype=jnp.float32)
    near = jnp.einsum(
        "lij,ljc->lic", kernel.astype(jnp.bfloat16), weights, preferred_element_type=jnp.float32
    )
    basis = leaf_basis.reshape(leaf_count, leaf_size, rank)
    leaf_weights = jnp.einsum("lia,lic->lac", basis, weights, preferred_element_type=jnp.float32)
    leaf_points = jnp.take_along_axis(feats, leaf_skel[:, :, None], axis=1)
    depth = leaf_count.bit_length() - 1
    weight_levels = [leaf_weights]
    point_levels = [leaf_points]
    transfer_levels = []
    for height in range(depth):
        transfer_levels.append(
            local_transfer[(leaf_count >> height) - 1 : (2 * leaf_count >> height) - 1]
        )
        weight_levels.append(pair_total(lift(transfer_levels[-1], weight_levels[-1])))
        upper_lo = (leaf_count >> height + 1) - 1
        upper_hi = (2 * leaf_count >> height + 1) - 1
        point_levels.append(pair_select(point_levels[-1], local_pick[upper_lo:upper_hi]))
    devices = lax.axis_size("leaf")
    levels = devices.bit_length() - 1
    my_index = lax.axis_index("leaf")
    current_weights = weight_levels[-1][0]
    current_points = point_levels[-1][0]
    device_transfer = local_transfer[0]
    saved = []
    for level in range(levels):
        heap_index = devices + my_index >> level
        node_transfer = device_transfer if level == 0 else upper_transfer[heap_index]
        own_share = lift(node_transfer[None], current_weights[None])[0]
        received = swapped(jnp.stack([current_weights, own_share]), "leaf", level)
        sibling_points = swapped(current_points, "leaf", level)
        saved.append((current_points, sibling_points, received[0], node_transfer))
        if level + 1 < levels:
            current_weights = own_share + received[1]
            on_left = my_index >> level & 1 == 0
            left_points = jnp.where(on_left, current_points, sibling_points)
            right_points = jnp.where(on_left, sibling_points, current_points)
            joined = jnp.concatenate([left_points, right_points], axis=0)
            current_points = jnp.take(joined, upper_pick[heap_index >> 1], axis=0)
    down_field = None
    for level in reversed(range(len(saved))):
        own_points, sibling_points, sibling_weights, node_transfer = saved[level]
        term = couple(own_points[None], sibling_points[None], sibling_weights[None])[0]
        if down_field is not None:
            term = term + lower(node_transfer[None], down_field[None])[0]
        down_field = term
    field = descend(point_levels[:depth], weight_levels[:depth], transfer_levels, down_field[None])
    far = jnp.einsum("lia,lac->lic", basis.astype(jnp.float32), field, precision=HIGHEST)
    result = (near + far).astype(jnp.bfloat16).reshape(rhs.shape)
    return jnp.zeros_like(result).at[item_order].set(result)


def solution(mesh):
    return jax.shard_map(
        local,
        mesh=mesh,
        in_specs=(
            P("leaf", None),
            P("leaf", None),
            P("leaf"),
            P("leaf", None),
            P("leaf", None),
            P("leaf", None, None),
            P("leaf", None),
            P(),
            P(),
        ),
        out_specs=P("leaf", None),
        check_vma=False,
    )
```

profile of v0, /device:TPU:8, one launch (start us, length us, event | category | flops | bytes accessed | tf_op | source)
XLA Modules:
  0.0 151.7 jit_solution(7690359175759355629)
XLA Ops:
  0.0 1.4 broadcast_clamp_fusion
  1.4 1.2 copy.24
  2.6 6.2 %gather_fusion.1 = bf16[2048,64]{1,0:T(8,128)(2,1)S(1)} fusion(bf16[2048,64]{1,0:T(8,128)(2,1)S(1)} %copy.24, s32[2048]{0:T(1024)S(1)} %get-tuple-element.58), kind=kCustom, calls=%fused_computation.9 | custom fusion | bytes 532480 | tf_op jit(solution)/shard_map/gather | solution.py:74
  10.0 0.6 pad_maximum_fusion
  10.6 1.9 %collective-permute-start.1 = (f32[2,32,64]{2,1,0:T(8,128)}, f32[2,32,64]{2,1,0:T(8,128)}, u32[]{:S(2)}, u32[]{:S(2)}) collective-permute-start(f32[2,32,64]{2,1,0:T(8,128)} %pad_maximum_fusion), channel_id=1, source_target_pairs={{0,1},{1,0},{2,3},{3,2},{4,5},{5,4},{6,7},{7,6},{8,9},{9,8},{10,11... | collective-permute-start | bytes 49160 | tf_op jit(solution)/shard_map/ppermute | solution.py:11
  12.7 7.5 %gather_fusion = bf16[2048,256]{1,0:T(8,128)(2,1)S(1)} fusion(bf16[2048,256]{1,0:T(8,128)(2,1)S(1)} %copy-done, s32[2048]{0:T(1024)S(1)} %get-tuple-element.58), kind=kCustom, calls=%fused_computation.8 | custom fusion | bytes 2105344 | tf_op jit(solution)/shard_map/gather | solution.py:73
  20.7 1.7 %gather_fusion.3 = bf16[256,256]{1,0:T(8,128)(2,1)S(1)} fusion(bf16[8,256,256]{2,1,0:T(8,128)(2,1)S(1)} %bitcast.273, s32[256]{0:T(256)S(1)} %reshape.860), kind=kCustom, calls=%fused_computation.11 | custom fusion | bytes 264192 | tf_op jit(solution)/shard_map/jit(take_along_axis)/gather | solution.py:81
  22.5 1.1 gather_fusion.4
  23.7 0.8 gather_fusion.5
  24.6 0.6 gather_fusion.2
  25.3 1.3 fusion.68
  26.6 2.4 %collective-permute-start = (bf16[32,256]{1,0:T(8,128)(2,1)}, bf16[32,256]{1,0:T(8,128)(2,1)}, u32[]{:S(2)}, u32[]{:S(2)}) collective-permute-start(bf16[32,256]{1,0:T(8,128)(2,1)} %get-tuple-element.17), channel_id=1, source_target_pairs={{0,1},{1,0},{2,3},{3,2},{4,5},{5,4},{6,7},{7,6},{8,9},{9,8},{10,11... | collective-permute-start | bytes 49160 | tf_op jit(solution)/shard_map/ppermute | solution.py:11
  29.0 0.7 fusion.32
  30.5 0.6 compare_and_fusion.7
  31.6 0.6 compare_and_fusion.3
  32.2 0.6 compare_and_fusion.1
  32.7 0.6 compare_select_fusion.4
  34.2 0.6 pad_clamp_fusion.7
  34.8 0.6 pad_clamp_fusion.6
  35.4 0.6 pad_clamp_fusion.5
  36.0 0.6 pad_clamp_fusion.4
  36.6 0.6 pad_clamp_fusion.3
  37.2 0.6 pad_clamp_fusion.2
  37.7 0.6 pad_clamp_fusion.1
  38.5 2.8 %fusion.1 = f32[8,256,64]{1,2,0:T(8,128)} fusion(bf16[8,256,64]{2,1,0:T(8,128)(2,1)S(1)} %bitcast.277, bf16[8,256,256]{2,1,0:T(8,128)(2,1)S(1)} %bitcast.275, f32[256,256]{1,0:T(8,128)} %fusion.32, f32[8,256]{1,0:T(8,128)S(1)} %fusion), kind=kOutput, calls=%fused_computation.18 | convolution fusion | flops 339738624 | bytes 2105344 | tf_op jit(solution)/shard_map/lij,ljc->lic/dot_general | solution.py:76
  42.1 0.8 fusion.257
  42.9 0.7 fusion.20
  43.7 1.6 %constant_dynamic-slice_fusion = (bf16[1,32,32]{0,2,1:T(8,128)(2,1)S(1)}, bf16[1,32,32]{0,2,1:T(8,128)(2,1)S(1)}, bf16[1,32,32]{0,2,1:T(8,128)(2,1)S(1)}, bf16[1...) fusion(bf16[512,32,32]{0,2,1:T(8,128)(2,1)S(1)} %copy-done.1, ...), kind=kLoop, calls=%fused_computation.392 | loop fusion | bytes 32800 | tf_op jit(solution)/shard_map/dynamic_slice | solution.py:103
  45.2 1.2 copy.162
  46.4 1.2 copy.163
  47.6 1.2 copy.164
  50.3 0.7 slice_add_fusion.8
  51.0 0.9 fusion.80
  51.9 7.7 %collective-permute-start.3 = (f32[2,32,64]{2,1,0:T(8,128)S(1)}, f32[2,32,64]{2,1,0:T(8,128)S(1)}, u32[]{:S(2)}, u32[]{:S(2)}) collective-permute-start(f32[2,32,64]{2,1,0:T(8,128)S(1)} %pad_maximum_fusion.2), channel_id=1, source_target_pairs={{0,2},{1,3},{2,0},{3,1},{4,6},{5,7},{6,4},{7,5},{8,10},{9,11},{10,... | collective-permute-start | bytes 49160 | tf_op jit(solution)/shard_map/ppermute | solution.py:11
  59.7 0.7 broadcast_select_fusion.33
  60.4 0.7 gather_fusion.6
  61.4 1.9 %collective-permute-start.2 = (bf16[32,256]{1,0:T(8,128)(2,1)S(1)}, bf16[32,256]{1,0:T(8,128)(2,1)S(1)}, u32[]{:S(2)}, u32[]{:S(2)}) collective-permute-start(bf16[32,256]{1,0:T(8,128)(2,1)S(1)} %get-tuple-element.19), channel_id=1, source_target_pairs={{0,2},{1,3},{2,0},{3,1},{4,6},{5,7},{6,4},{7,5},{8,10},{9,11},{10,... | collective-permute-start | bytes 49160 | tf_op jit(solution)/shard_map/ppermute | solution.py:11
  63.3 0.9 convolution_multiply_fusion.11
  64.1 0.8 fusion.67
  65.2 1.9 %collective-permute-start.5 = (f32[2,32,64]{2,1,0:T(8,128)S(1)}, f32[2,32,64]{2,1,0:T(8,128)S(1)}, u32[]{:S(2)}, u32[]{:S(2)}) collective-permute-start(f32[2,32,64]{2,1,0:T(8,128)S(1)} %pad_maximum_fusion.4), channel_id=1, source_target_pairs={{0,4},{1,5},{2,6},{3,7},{4,0},{5,1},{6,2},{7,3},{8,12},{9,13},{10,... | collective-permute-start | bytes 49160 | tf_op jit(solution)/shard_map/ppermute | solution.py:11
  67.2 0.7 gather_fusion.7
  68.1 4.8 %collective-permute-start.4 = (bf16[32,256]{1,0:T(8,128)(2,1)S(1)}, bf16[32,256]{1,0:T(8,128)(2,1)S(1)}, u32[]{:S(2)}, u32[]{:S(2)}) collective-permute-start(bf16[32,256]{1,0:T(8,128)(2,1)S(1)} %get-tuple-element.21), channel_id=1, source_target_pairs={{0,4},{1,5},{2,6},{3,7},{4,0},{5,1},{6,2},{7,3},{8,12},{9,13},{10,... | collective-permute-start | bytes 49160 | tf_op jit(solution)/shard_map/ppermute | solution.py:11
  73.4 3.0 %collective-permute-start.7 = (f32[2,32,64]{2,1,0:T(8,128)S(1)}, f32[2,32,64]{2,1,0:T(8,128)S(1)}, u32[]{:S(2)}, u32[]{:S(2)}) collective-permute-start(f32[2,32,64]{2,1,0:T(8,128)S(1)} %pad_maximum_fusion.6), channel_id=1, source_target_pairs={{0,8},{1,9},{2,10},{3,11},{4,12},{5,13},{6,14},{7,15},{8,0},{9,1},... | collective-permute-start | bytes 49160 | tf_op jit(solution)/shard_map/ppermute | solution.py:11
  76.5 0.7 gather_fusion.8
  77.5 6.7 %collective-permute-start.6 = (bf16[32,256]{1,0:T(8,128)(2,1)S(1)}, bf16[32,256]{1,0:T(8,128)(2,1)S(1)}, u32[]{:S(2)}, u32[]{:S(2)}) collective-permute-start(bf16[32,256]{1,0:T(8,128)(2,1)S(1)} %get-tuple-element.23), channel_id=1, source_target_pairs={{0,8},{1,9},{2,10},{3,11},{4,12},{5,13},{6,14},{7,15},{8,0},{9,1},... | collective-permute-start | bytes 49160 | tf_op jit(solution)/shard_map/ppermute | solution.py:11
  84.7 1.9 %collective-permute-start.9 = (f32[2,32,64]{2,1,0:T(8,128)S(1)}, f32[2,32,64]{2,1,0:T(8,128)S(1)}, u32[]{:S(2)}, u32[]{:S(2)}) collective-permute-start(f32[2,32,64]{2,1,0:T(8,128)S(1)} %pad_maximum_fusion.8), channel_id=1, source_target_pairs={{0,16},{1,17},{2,18},{3,19},{4,20},{5,21},{6,22},{7,23},{8,24},{9,... | collective-permute-start | bytes 49160 | tf_op jit(solution)/shard_map/ppermute | solution.py:11
  87.0 0.7 gather_fusion.9
  87.9 3.5 %collective-permute-start.8 = (bf16[32,256]{1,0:T(8,128)(2,1)S(1)}, bf16[32,256]{1,0:T(8,128)(2,1)S(1)}, u32[]{:S(2)}, u32[]{:S(2)}) collective-permute-start(bf16[32,256]{1,0:T(8,128)(2,1)S(1)} %get-tuple-element.25), channel_id=1, source_target_pairs={{0,16},{1,17},{2,18},{3,19},{4,20},{5,21},{6,22},{7,23},{8,24},{9,... | collective-permute-start | bytes 49160 | tf_op jit(solution)/shard_map/ppermute | solution.py:11
  92.0 4.5 %collective-permute-start.11 = (f32[2,32,64]{2,1,0:T(8,128)S(1)}, f32[2,32,64]{2,1,0:T(8,128)S(1)}, u32[]{:S(2)}, u32[]{:S(2)}) collective-permute-start(f32[2,32,64]{2,1,0:T(8,128)S(1)} %pad_maximum_fusion.10), channel_id=1, source_target_pairs={{0,32},{1,33},{2,34},{3,35},{4,36},{5,37},{6,38},{7,39},{8,40},{9,... | collective-permute-start | bytes 49160 | tf_op jit(solution)/shard_map/ppermute | solution.py:11
  96.5 0.7 gather_fusion.10
  97.5 2.9 %collective-permute-start.10 = (bf16[32,256]{1,0:T(8,128)(2,1)S(1)}, bf16[32,256]{1,0:T(8,128)(2,1)S(1)}, u32[]{:S(2)}, u32[]{:S(2)}) collective-permute-start(bf16[32,256]{1,0:T(8,128)(2,1)S(1)} %get-tuple-element.27), channel_id=1, source_target_pairs={{0,32},{1,33},{2,34},{3,35},{4,36},{5,37},{6,38},{7,39},{8,40},{9,... | collective-permute-start | bytes 49160 | tf_op jit(solution)/shard_map/ppermute | solution.py:11
  100.8 4.1 %collective-permute-start.13 = (f32[2,32,64]{2,1,0:T(8,128)S(1)}, f32[2,32,64]{2,1,0:T(8,128)S(1)}, u32[]{:S(2)}, u32[]{:S(2)}) collective-permute-start(f32[2,32,64]{2,1,0:T(8,128)S(1)} %pad_maximum_fusion.12), channel_id=1, source_target_pairs={{0,64},{1,65},{2,66},{3,67},{4,68},{5,69},{6,70},{7,71},{8,72},{9,... | collective-permute-start | bytes 49160 | tf_op jit(solution)/shard_map/ppermute | solution.py:11
  105.0 0.7 gather_fusion.11
  105.9 3.9 %collective-permute-start.12 = (bf16[32,256]{1,0:T(8,128)(2,1)S(1)}, bf16[32,256]{1,0:T(8,128)(2,1)S(1)}, u32[]{:S(2)}, u32[]{:S(2)}) collective-permute-start(bf16[32,256]{1,0:T(8,128)(2,1)S(1)} %get-tuple-element.29), channel_id=1, source_target_pairs={{0,64},{1,65},{2,66},{3,67},{4,68},{5,69},{6,70},{7,71},{8,72},{9,... | collective-permute-start | bytes 49160 | tf_op jit(solution)/shard_map/ppermute | solution.py:11
  110.4 6.1 %collective-permute-start.15 = (f32[2,32,64]{2,1,0:T(8,128)S(1)}, f32[2,32,64]{2,1,0:T(8,128)S(1)}, u32[]{:S(2)}, u32[]{:S(2)}) collective-permute-start(f32[2,32,64]{2,1,0:T(8,128)S(1)} %pad_maximum_fusion.14), channel_id=1, source_target_pairs={{0,128},{1,129},{2,130},{3,131},{4,132},{5,133},{6,134},{7,135},{8... | collective-permute-start | bytes 49160 | tf_op jit(solution)/shard_map/ppermute | solution.py:11
  116.5 0.9 gather_fusion.12
  117.6 1.9 %collective-permute-start.14 = (bf16[32,256]{1,0:T(8,128)(2,1)S(1)}, bf16[32,256]{1,0:T(8,128)(2,1)S(1)}, u32[]{:S(2)}, u32[]{:S(2)}) collective-permute-start(bf16[32,256]{1,0:T(8,128)(2,1)S(1)} %get-tuple-element.31), channel_id=1, source_target_pairs={{0,128},{1,129},{2,130},{3,131},{4,132},{5,133},{6,134},{7,135},{8... | collective-permute-start | bytes 49160 | tf_op jit(solution)/shard_map/ppermute | solution.py:11
  120.0 8.8 %collective-permute-start.17 = (f32[2,32,64]{2,1,0:T(8,128)S(1)}, f32[2,32,64]{2,1,0:T(8,128)S(1)}, u32[]{:S(2)}, u32[]{:S(2)}) collective-permute-start(f32[2,32,64]{2,1,0:T(8,128)S(1)} %pad_maximum_fusion.16), channel_id=1, source_target_pairs={{0,256},{1,257},{2,258},{3,259},{4,260},{5,261},{6,262},{7,263},{8... | collective-permute-start | bytes 49160 | tf_op jit(solution)/shard_map/ppermute | solution.py:11
  128.8 0.6 gather_fusion.13
  129.6 4.2 %collective-permute-start.16 = (bf16[32,256]{1,0:T(8,128)(2,1)S(1)}, bf16[32,256]{1,0:T(8,128)(2,1)S(1)}, u32[]{:S(2)}, u32[]{:S(2)}) collective-permute-start(bf16[32,256]{1,0:T(8,128)(2,1)S(1)} %get-tuple-element.33), channel_id=1, source_target_pairs={{0,256},{1,257},{2,258},{3,259},{4,260},{5,261},{6,262},{7,263},{8... | collective-permute-start | bytes 49160 | tf_op jit(solution)/shard_map/ppermute | solution.py:11
  134.0 5.1 %collective-permute-done.16 = bf16[32,256]{1,0:T(8,128)(2,1)S(1)} collective-permute-done((bf16[32,256]{1,0:T(8,128)(2,1)S(1)}, bf16[32,256]{1,0:T(8,128)(2,1)S(1)}, u32[]{:S(2)}, u32[]{:S(2)}) %collective-permute-start.16) | collective-permute-done | bytes 16416 | tf_op jit(solution)/shard_map/ppermute | solution.py:11
  142.3 0.9 convolution_add_fusion.8
  144.8 6.0 %scatter_custom_fusion = bf16[2048,64]{1,0:T(8,128)(2,1)S(1)} fusion(s32[2048]{0:T(1024)} %get-tuple-element.59, bf16[2048,64]{1,0:T(8,128)(2,1)S(1)} %bitcast.290, bf16[]{:T(256)} %constant.39.clone.1), kind=kCustom, calls=%fused_computation.79 | custom fusion | bytes 262656 | tf_op jit(solution)/shard_map/scatter | solution.py:125
  150.7 0.9 copy.48
  (208 shorter events, 15.9 us)
Async XLA Ops:
  0.0 12.7 %copy-start = (bf16[2048,256]{1,0:T(8,128)(2,1)S(1)}, bf16[2048,256]{1,0:T(8,128)(2,1)}, u32[]{:S(2)}) copy-start(bf16[2048,256]{1,0:T(8,128)(2,1)} %param.11) | copy-start | bytes 3145732
  2.6 6.2 %copy-start.3 = (bf16[2048,32]{0,1:T(8,128)(2,1)S(1)}, bf16[2048,32]{0,1:T(8,128)(2,1)}, u32[]{:S(2)}) copy-start(bf16[2048,32]{0,1:T(8,128)(2,1)} %param.14) | copy-start | bytes 393220
  2.6 6.4 %copy-start.5 = (bf16[15,32,32]{2,1,0:T(8,128)(2,1)S(1)}, bf16[15,32,32]{2,1,0:T(8,128)(2,1)}, u32[]{:S(2)}) copy-start(bf16[15,32,32]{2,1,0:T(8,128)(2,1)} %param.16) | copy-start | bytes 92164
  8.8 3.7 %copy-start.12 = (s32[8,32]{1,0:T(8,128)S(1)}, s32[8,32]{1,0:T(8,128)}, u32[]{:S(2)}) copy-start(s32[8,32]{1,0:T(8,128)} %param.15) | copy-start | bytes 3076
  8.8 3.8 %copy-start.13 = (s32[7,32]{1,0:T(8,128)S(1)}, s32[7,32]{1,0:T(8,128)}, u32[]{:S(2)}) copy-start(s32[7,32]{1,0:T(8,128)} %param.17) | copy-start | bytes 2692
  9.6 10.6 %copy-start.9 = (f32[4,64,32]{1,2,0:T(8,128)}, f32[4,64,32]{1,2,0:T(8,128)S(1)}, u32[]{:S(2)}) copy-start(f32[4,64,32]{1,2,0:T(8,128)S(1)} %fusion.41) | copy-start | bytes 98308
  10.6 39.6 %collective-permute-start.1 = (f32[2,32,64]{2,1,0:T(8,128)}, f32[2,32,64]{2,1,0:T(8,128)}, u32[]{:S(2)}, u32[]{:S(2)}) collective-permute-start(f32[2,32,64]{2,1,0:T(8,128)} %pad_maximum_fusion), channel_id=1, source_target_pairs={{0,1},{1,0},{2,3},{3,2},{4,5},{5,4},{6,7},{7,6},{8,9},{9,8},{10,11... | collective-permute-start | bytes 49160 | tf_op jit(solution)/shard_map/ppermute | solution.py:11
  23.6 6.5 %copy-start.8 = (s32[512,32]{0,1:T(8,128)S(1)}, s32[512,32]{0,1:T(8,128)}, u32[]{:S(2)}) copy-start(s32[512,32]{0,1:T(8,128)} %param.19) | copy-start | bytes 196612
  26.6 33.1 %collective-permute-start = (bf16[32,256]{1,0:T(8,128)(2,1)}, bf16[32,256]{1,0:T(8,128)(2,1)}, u32[]{:S(2)}, u32[]{:S(2)}) collective-permute-start(bf16[32,256]{1,0:T(8,128)(2,1)} %get-tuple-element.17), channel_id=1, source_target_pairs={{0,1},{1,0},{2,3},{3,2},{4,5},{5,4},{6,7},{7,6},{8,9},{9,8},{10,11... | collective-permute-start | bytes 49160 | tf_op jit(solution)/shard_map/ppermute | solution.py:11
  41.4 2.3 %copy-start.1 = (bf16[512,32,32]{0,2,1:T(8,128)(2,1)S(1)}, bf16[512,32,32]{0,2,1:T(8,128)(2,1)}, u32[]{:S(2)}) copy-start(bf16[512,32,32]{0,2,1:T(8,128)(2,1)} %param.18) | copy-start | bytes 3145732
  43.6 1.6 %copy-start.23 = (s32[32]{0:T(128)S(1)}, s32[32]{0:T(128)}, u32[]{:S(2)}) copy-start(s32[32]{0:T(128)} %compare_select_fusion.4) | copy-start | bytes 388
  47.6 13.5 %copy-start.22 = (pred[32]{0:T(512)(128)(4,1)S(1)}, pred[32]{0:T(512)(128)(4,1)}, u32[]{:S(2)}) copy-start(pred[32]{0:T(512)(128)(4,1)} %get-tuple-element.67) | copy-start | bytes 100
  49.1 18.8 %copy-start.21 = (pred[32]{0:T(512)(128)(4,1)S(1)}, pred[32]{0:T(512)(128)(4,1)}, u32[]{:S(2)}) copy-start(pred[32]{0:T(512)(128)(4,1)} %get-tuple-element.66) | copy-start | bytes 100
  49.7 27.6 %copy-start.20 = (pred[32]{0:T(512)(128)(4,1)S(1)}, pred[32]{0:T(512)(128)(4,1)}, u32[]{:S(2)}) copy-start(pred[32]{0:T(512)(128)(4,1)} %get-tuple-element.65) | copy-start | bytes 100
  51.0 36.8 %copy-start.19 = (pred[32]{0:T(512)(128)(4,1)S(1)}, pred[32]{0:T(512)(128)(4,1)}, u32[]{:S(2)}) copy-start(pred[32]{0:T(512)(128)(4,1)} %get-tuple-element.64) | copy-start | bytes 100
  51.9 13.1 %collective-permute-start.3 = (f32[2,32,64]{2,1,0:T(8,128)S(1)}, f32[2,32,64]{2,1,0:T(8,128)S(1)}, u32[]{:S(2)}, u32[]{:S(2)}) collective-permute-start(f32[2,32,64]{2,1,0:T(8,128)S(1)} %pad_maximum_fusion.2), channel_id=1, source_target_pairs={{0,2},{1,3},{2,0},{3,1},{4,6},{5,7},{6,4},{7,5},{8,10},{9,11},{10,... | collective-permute-start | bytes 49160 | tf_op jit(solution)/shard_map/ppermute | solution.py:11
  61.4 5.8 %collective-permute-start.2 = (bf16[32,256]{1,0:T(8,128)(2,1)S(1)}, bf16[32,256]{1,0:T(8,128)(2,1)S(1)}, u32[]{:S(2)}, u32[]{:S(2)}) collective-permute-start(bf16[32,256]{1,0:T(8,128)(2,1)S(1)} %get-tuple-element.19), channel_id=1, source_target_pairs={{0,2},{1,3},{2,0},{3,1},{4,6},{5,7},{6,4},{7,5},{8,10},{9,11},{10,... | collective-permute-start | bytes 49160 | tf_op jit(solution)/shard_map/ppermute | solution.py:11
  65.0 32.3 %copy-start.18 = (pred[32]{0:T(512)(128)(4,1)S(1)}, pred[32]{0:T(512)(128)(4,1)}, u32[]{:S(2)}) copy-start(pred[32]{0:T(512)(128)(4,1)} %get-tuple-element.63) | copy-start | bytes 100
  65.2 8.0 %collective-permute-start.5 = (f32[2,32,64]{2,1,0:T(8,128)S(1)}, f32[2,32,64]{2,1,0:T(8,128)S(1)}, u32[]{:S(2)}, u32[]{:S(2)}) collective-permute-start(f32[2,32,64]{2,1,0:T(8,128)S(1)} %pad_maximum_fusion.4), channel_id=1, source_target_pairs={{0,4},{1,5},{2,6},{3,7},{4,0},{5,1},{6,2},{7,3},{8,12},{9,13},{10,... | collective-permute-start | bytes 49160 | tf_op jit(solution)/shard_map/ppermute | solution.py:11
  68.1 8.3 %collective-permute-start.4 = (bf16[32,256]{1,0:T(8,128)(2,1)S(1)}, bf16[32,256]{1,0:T(8,128)(2,1)S(1)}, u32[]{:S(2)}, u32[]{:S(2)}) collective-permute-start(bf16[32,256]{1,0:T(8,128)(2,1)S(1)} %get-tuple-element.21), channel_id=1, source_target_pairs={{0,4},{1,5},{2,6},{3,7},{4,0},{5,1},{6,2},{7,3},{8,12},{9,13},{10,... | collective-permute-start | bytes 49160 | tf_op jit(solution)/shard_map/ppermute | solution.py:11
  73.2 32.5 %copy-start.17 = (pred[32]{0:T(512)(128)(4,1)S(1)}, pred[32]{0:T(512)(128)(4,1)}, u32[]{:S(2)}) copy-start(pred[32]{0:T(512)(128)(4,1)} %get-tuple-element.62) | copy-start | bytes 100
  73.4 11.0 %collective-permute-start.7 = (f32[2,32,64]{2,1,0:T(8,128)S(1)}, f32[2,32,64]{2,1,0:T(8,128)S(1)}, u32[]{:S(2)}, u32[]{:S(2)}) collective-permute-start(f32[2,32,64]{2,1,0:T(8,128)S(1)} %pad_maximum_fusion.6), channel_id=1, source_target_pairs={{0,8},{1,9},{2,10},{3,11},{4,12},{5,13},{6,14},{7,15},{8,0},{9,1},... | collective-permute-start | bytes 49160 | tf_op jit(solution)/shard_map/ppermute | solution.py:11
  77.5 9.5 %collective-permute-start.6 = (bf16[32,256]{1,0:T(8,128)(2,1)S(1)}, bf16[32,256]{1,0:T(8,128)(2,1)S(1)}, u32[]{:S(2)}, u32[]{:S(2)}) collective-permute-start(bf16[32,256]{1,0:T(8,128)(2,1)S(1)} %get-tuple-element.23), channel_id=1, source_target_pairs={{0,8},{1,9},{2,10},{3,11},{4,12},{5,13},{6,14},{7,15},{8,0},{9,1},... | collective-permute-start | bytes 49160 | tf_op jit(solution)/shard_map/ppermute | solution.py:11
  84.4 32.9 %copy-start.16 = (pred[32]{0:T(512)(128)(4,1)S(1)}, pred[32]{0:T(512)(128)(4,1)}, u32[]{:S(2)}) copy-start(pred[32]{0:T(512)(128)(4,1)} %get-tuple-element.61) | copy-start | bytes 100
  84.7 7.1 %collective-permute-start.9 = (f32[2,32,64]{2,1,0:T(8,128)S(1)}, f32[2,32,64]{2,1,0:T(8,128)S(1)}, u32[]{:S(2)}, u32[]{:S(2)}) collective-permute-start(f32[2,32,64]{2,1,0:T(8,128)S(1)} %pad_maximum_fusion.8), channel_id=1, source_target_pairs={{0,16},{1,17},{2,18},{3,19},{4,20},{5,21},{6,22},{7,23},{8,24},{9,... | collective-permute-start | bytes 49160 | tf_op jit(solution)/shard_map/ppermute | solution.py:11
  87.9 8.5 %collective-permute-start.8 = (bf16[32,256]{1,0:T(8,128)(2,1)S(1)}, bf16[32,256]{1,0:T(8,128)(2,1)S(1)}, u32[]{:S(2)}, u32[]{:S(2)}) collective-permute-start(bf16[32,256]{1,0:T(8,128)(2,1)S(1)} %get-tuple-element.25), channel_id=1, source_target_pairs={{0,16},{1,17},{2,18},{3,19},{4,20},{5,21},{6,22},{7,23},{8,24},{9,... | collective-permute-start | bytes 49160 | tf_op jit(solution)/shard_map/ppermute | solution.py:11
  91.8 37.6 %copy-start.15 = (pred[32]{0:T(512)(128)(4,1)S(1)}, pred[32]{0:T(512)(128)(4,1)}, u32[]{:S(2)}) copy-start(pred[32]{0:T(512)(128)(4,1)} %get-tuple-element.60) | copy-start | bytes 100
  92.0 8.6 %collective-permute-start.11 = (f32[2,32,64]{2,1,0:T(8,128)S(1)}, f32[2,32,64]{2,1,0:T(8,128)S(1)}, u32[]{:S(2)}, u32[]{:S(2)}) collective-permute-start(f32[2,32,64]{2,1,0:T(8,128)S(1)} %pad_maximum_fusion.10), channel_id=1, source_target_pairs={{0,32},{1,33},{2,34},{3,35},{4,36},{5,37},{6,38},{7,39},{8,40},{9,... | collective-permute-start | bytes 49160 | tf_op jit(solution)/shard_map/ppermute | solution.py:11
  97.5 7.5 %collective-permute-start.10 = (bf16[32,256]{1,0:T(8,128)(2,1)S(1)}, bf16[32,256]{1,0:T(8,128)(2,1)S(1)}, u32[]{:S(2)}, u32[]{:S(2)}) collective-permute-start(bf16[32,256]{1,0:T(8,128)(2,1)S(1)} %get-tuple-element.27), channel_id=1, source_target_pairs={{0,32},{1,33},{2,34},{3,35},{4,36},{5,37},{6,38},{7,39},{8,40},{9,... | collective-permute-start | bytes 49160 | tf_op jit(solution)/shard_map/ppermute | solution.py:11
  100.8 9.3 %collective-permute-start.13 = (f32[2,32,64]{2,1,0:T(8,128)S(1)}, f32[2,32,64]{2,1,0:T(8,128)S(1)}, u32[]{:S(2)}, u32[]{:S(2)}) collective-permute-start(f32[2,32,64]{2,1,0:T(8,128)S(1)} %pad_maximum_fusion.12), channel_id=1, source_target_pairs={{0,64},{1,65},{2,66},{3,67},{4,68},{5,69},{6,70},{7,71},{8,72},{9,... | collective-permute-start | bytes 49160 | tf_op jit(solution)/shard_map/ppermute | solution.py:11
  105.7 36.4 %copy-start.6 = (bf16[15,32,32]{2,1,0:T(8,128)(2,1)S(1)}, bf16[15,32,32]{2,1,0:T(8,128)(2,1)}, u32[]{:S(2)}) copy-start(bf16[15,32,32]{2,1,0:T(8,128)(2,1)} %param.16) | copy-start | bytes 92164
  105.9 36.4 %copy-start.14 = (f32[32]{0:T(128)S(1)}, f32[32]{0:T(128)}, u32[]{:S(2)}) copy-start(f32[32]{0:T(128)} %get-tuple-element.16) | copy-start | bytes 388
  105.9 10.5 %collective-permute-start.12 = (bf16[32,256]{1,0:T(8,128)(2,1)S(1)}, bf16[32,256]{1,0:T(8,128)(2,1)S(1)}, u32[]{:S(2)}, u32[]{:S(2)}) collective-permute-start(bf16[32,256]{1,0:T(8,128)(2,1)S(1)} %get-tuple-element.29), channel_id=1, source_target_pairs={{0,64},{1,65},{2,66},{3,67},{4,68},{5,69},{6,70},{7,71},{8,72},{9,... | collective-permute-start | bytes 49160 | tf_op jit(solution)/shard_map/ppermute | solution.py:11
  110.1 33.3 %copy-start.10 = (f32[4,64,32]{1,2,0:T(8,128)S(1)}, f32[4,64,32]{1,2,0:T(8,128)}, u32[]{:S(2)}) copy-start(f32[4,64,32]{1,2,0:T(8,128)} %copy-done.9) | copy-start | bytes 98308
  110.1 33.3 %copy-start.11 = (f32[2,32,32]{2,1,0:T(8,128)S(1)}, f32[2,32,32]{2,1,0:T(8,128)}, u32[]{:S(2)}) copy-start(f32[2,32,32]{2,1,0:T(8,128)} %fusion.20) | copy-start | bytes 24580
  110.4 9.4 %collective-permute-start.15 = (f32[2,32,64]{2,1,0:T(8,128)S(1)}, f32[2,32,64]{2,1,0:T(8,128)S(1)}, u32[]{:S(2)}, u32[]{:S(2)}) collective-permute-start(f32[2,32,64]{2,1,0:T(8,128)S(1)} %pad_maximum_fusion.14), channel_id=1, source_target_pairs={{0,128},{1,129},{2,130},{3,131},{4,132},{5,133},{6,134},{7,135},{8... | collective-permute-start | bytes 49160 | tf_op jit(solution)/shard_map/ppermute | solution.py:11
  116.5 27.1 %copy-start.7 = (f32[4,32,64]{2,1,0:T(8,128)S(1)}, f32[4,32,64]{2,1,0:T(8,128)}, u32[]{:S(2)}) copy-start(f32[4,32,64]{2,1,0:T(8,128)} %fusion.257) | copy-start | bytes 98308
  117.6 11.2 %collective-permute-start.14 = (bf16[32,256]{1,0:T(8,128)(2,1)S(1)}, bf16[32,256]{1,0:T(8,128)(2,1)S(1)}, u32[]{:S(2)}, u32[]{:S(2)}) collective-permute-start(bf16[32,256]{1,0:T(8,128)(2,1)S(1)} %get-tuple-element.31), channel_id=1, source_target_pairs={{0,128},{1,129},{2,130},{3,131},{4,132},{5,133},{6,134},{7,135},{8... | collective-permute-start | bytes 49160 | tf_op jit(solution)/shard_map/ppermute | solution.py:11
  120.0 19.4 %collective-permute-start.17 = (f32[2,32,64]{2,1,0:T(8,128)S(1)}, f32[2,32,64]{2,1,0:T(8,128)S(1)}, u32[]{:S(2)}, u32[]{:S(2)}) collective-permute-start(f32[2,32,64]{2,1,0:T(8,128)S(1)} %pad_maximum_fusion.16), channel_id=1, source_target_pairs={{0,256},{1,257},{2,258},{3,259},{4,260},{5,261},{6,262},{7,263},{8... | collective-permute-start | bytes 49160 | tf_op jit(solution)/shard_map/ppermute | solution.py:11
  129.6 9.5 %collective-permute-start.16 = (bf16[32,256]{1,0:T(8,128)(2,1)S(1)}, bf16[32,256]{1,0:T(8,128)(2,1)S(1)}, u32[]{:S(2)}, u32[]{:S(2)}) collective-permute-start(bf16[32,256]{1,0:T(8,128)(2,1)S(1)} %get-tuple-element.33), channel_id=1, source_target_pairs={{0,256},{1,257},{2,258},{3,259},{4,260},{5,261},{6,262},{7,263},{8... | collective-permute-start | bytes 49160 | tf_op jit(solution)/shard_map/ppermute | solution.py:11
  139.4 4.6 %copy-start.2 = (f32[8,256,64]{1,2,0:T(8,128)S(1)}, f32[8,256,64]{1,2,0:T(8,128)}, u32[]{:S(2)}) copy-start(f32[8,256,64]{1,2,0:T(8,128)} %fusion.1) | copy-start | bytes 1572868
  139.4 4.6 %copy-start.4 = (bf16[2048,32]{0,1:T(8,128)(2,1)S(1)}, bf16[2048,32]{0,1:T(8,128)(2,1)}, u32[]{:S(2)}) copy-start(bf16[2048,32]{0,1:T(8,128)(2,1)} %param.14) | copy-start | bytes 393220
where the time goes:
time: 153 us; the launch traced here: 152 us
  starting transfers between devices  72.3 us (47%)
  local copies, waits for them, and re-layouts  39.9 us (26%)
  other arithmetic  17.6 us (12%)
  matrix products  15.1 us (10%)
  waiting for transfers between devices  5.53 us (4%)
    ppermute x18, starting transfers between devices, swapped(): lax.ppermute(array, axis, [(i, i ^ 1 << stride) for i in range(lax.axis_s...  72.3 us
    gather x1, local copies, waits for them, and re-layouts, local(): feats = embeddings[item_order].reshape(leaf_count, leaf_size, -1)  7.5 us
    scatter x2, local copies, waits for them, and re-layouts, local(): return jnp.zeros_like(result).at[item_order].set(result)  6.89 us
    unnamed x57, local copies, waits for them, and re-layouts  6.35 us
    gather x1, local copies, waits for them, and re-layouts, local(): weights = rhs[item_order].reshape(leaf_count, leaf_size, -1)  6.18 us
    gather x8, local copies, waits for them, and re-layouts, local(): current_points = jnp.take(joined, upper_pick[heap_index >> 1], axis=0)  6 us
    ppermute x18, waiting for transfers between devices, swapped(): lax.ppermute(array, axis, [(i, i ^ 1 << stride) for i in range(lax.axis_s...  5.53 us
    gather x8, other arithmetic  4.16 us
  transfers between devices with their start and end apart: 18, of which 2 were waited for; matrix products, arithmetic and copies ran while one was open for 33% of the time, Pallas kernels for 0%

commit v1 on v0

v1 whole, which is shorter than its diff:
```python
import functools

import jax
import jax.numpy as jnp
from jax import lax
from jax.experimental import pallas as pl
from jax.experimental.pallas import tpu as pltpu
from jax.sharding import PartitionSpec as P

RIDGE = 1.0
RADICES = {512: (8, 8, 8)}
F32 = jnp.float32
BF16 = jnp.bfloat16
VMEM_LIMIT = 48 * 1024 * 1024


def dot(a, b):
    return jnp.dot(a, b, preferred_element_type=F32)


def dot_first(a, b):
    return lax.dot_general(a, b, (((0,), (0,)), ((), ())), preferred_element_type=F32)


def dot_last(a, b):
    return lax.dot_general(a, b, (((1,), (1,)), ((), ())), preferred_element_type=F32)


def split(x):
    high = x.astype(BF16)
    return high, (x - high.astype(F32)).astype(BF16)


def dot_wide(a, b):
    a_high, a_low = split(a)
    b_high, b_low = split(b)
    return dot(a_high, b_high) + dot(a_low, b_high) + dot(a_high, b_low)


def dot_right(a, b):
    high, low = split(b)
    return dot(a, high) + dot(a, low)


def dot_first_right(a, b):
    high, low = split(b)
    return dot_first(a, high) + dot_first(a, low)


def iota(shape, axis):
    return lax.broadcasted_iota(jnp.int32, shape, axis)


def one_hot(mask):
    return jnp.where(mask, 1.0, 0.0).astype(BF16)


def kernel_of(distance, width):
    return lax.rsqrt(1.0 + jnp.maximum(distance, 0.0) * (1.0 / width))


def self_kernel(points):
    count, width = points.shape
    gram = dot_last(points, points)
    eye = iota(gram.shape, 0) == iota(gram.shape, 1)
    diagonal = jnp.where(eye, gram, 0.0)
    across = jnp.sum(diagonal, axis=1, keepdims=True)
    down = jnp.sum(diagonal, axis=0, keepdims=True)
    return kernel_of(across + down - 2.0 * gram, width), eye


def columns_of(table):
    return table.astype(F32).T.astype(jnp.int32)


def order_column(order_t, leaf):
    return jnp.concatenate([order_t[:, 2 * leaf : 2 * leaf + 1], order_t[:, 2 * leaf + 1 : 2 * leaf + 2]], axis=0)


def padded_columns(tables, rows):
    stacked = jnp.concatenate(tables, axis=0)
    short = rows - stacked.shape[0]
    if short:
        stacked = jnp.concatenate([stacked, jnp.zeros((short, stacked.shape[1]), jnp.int32)], axis=0)
    wide = jnp.concatenate([stacked, jnp.zeros((rows, 128 - stacked.shape[1]), jnp.int32)], axis=1)
    return columns_of(wide)


def pre_body(leaves, order, rhs, basis, skel, pick, transfer, emb, payload, rhs_tree, points, weights):
    items = rhs.shape[0]
    leaf = items // leaves
    cols = rhs.shape[1]
    rank = skel.shape[1]
    order_t = columns_of(order[...])
    table = padded_columns([skel[...], pick[...]], 16)
    blocks = items // leaf
    joined = jnp.concatenate([rhs[b * leaf : (b + 1) * leaf, :].astype(F32) for b in range(blocks)], axis=1).astype(BF16)
    lane_block = iota((leaf, blocks * cols), 1) // cols
    ids = []
    level = []
    for l in range(leaves):
        column = order_column(order_t, l)
        low, high = column & (leaf - 1), column // leaf
        found = dot(one_hot(low == iota((leaf, leaf), 1)), joined)
        found = jnp.where(high == lane_block, found, 0.0)
        total = found[:, :128]
        for b in range(1, blocks * cols // 128):
            total = total + found[:, b * 128 : (b + 1) * 128]
        picked = total[:, :cols] + total[:, cols:]
        picked = picked.astype(BF16)
        rhs_tree[l * leaf : (l + 1) * leaf, :] = picked
        level.append(dot_first(basis[l * leaf : (l + 1) * leaf, :], picked))
        spot = one_hot(table[:rank, l : l + 1] == iota((rank, leaf), 1))
        digits = jnp.concatenate(
            [jnp.broadcast_to(high, (leaf, 128)), jnp.broadcast_to(low, (leaf, 128))], axis=1
        )
        ids.append(dot(spot, digits.astype(F32).astype(BF16)))
    ids = jnp.concatenate(ids, axis=0).astype(jnp.int32)
    high, low = ids[:, :128], ids[:, 128:]
    lane = iota(high.shape, 1)
    per = leaf // 128
    spots = [one_hot((high == b // per) & (low == lane + 128 * (b % per))) for b in range(items // 128)]
    nodes = dot(jnp.concatenate(spots, axis=1), emb[...]).astype(BF16)
    count = leaves
    at = 0
    while count > 1:
        points[at : at + count * rank, :] = nodes
        weights[at : at + count * rank, :] = jnp.concatenate(level, axis=0)
        at += count * rank
        parents = count // 2
        rows = jnp.concatenate(
            [table[:rank, leaves + q - 1 : leaves + q] + 2 * rank * (q - parents) for q in range(parents, 2 * parents)], axis=0
        )
        nodes = dot(one_hot(rows == iota((parents * rank, count * rank), 1)), nodes).astype(BF16)
        upper = []
        for q in range(parents, 2 * parents):
            pair = jnp.concatenate(level[2 * (q - parents) : 2 * (q - parents) + 2], axis=0)
            moved = transfer[2 * q - 1 : 2 * q + 1].reshape(2 * rank, rank)
            upper.append(dot_first_right(moved, pair))
        level = upper
        count = parents
    own = level[0]
    share = dot_first_right(transfer[0], own)
    tail = jnp.concatenate([own, share], axis=1)
    sent = jnp.concatenate([nodes, tail.astype(BF16)], axis=1)
    for r in range(payload.shape[0]):
        payload[r] = sent


def prep_body(devices, radices, me_ref, pick, own_transfer, *refs):
    rank = own_transfer.shape[1]
    blocks = iter(refs[: sum(n.bit_length() - 1 for n in radices) - 1])
    outs = refs[sum(n.bit_length() - 1 for n in radices) - 1 :]
    selects, lifts, chains = outs[:3]
    select_all, lift_all = outs[3:]
    me = me_ref[0]
    base = 0
    chain = None
    for stage, radix in enumerate(radices):
        depth = radix.bit_length() - 1
        place = (me // (1 << base)) % radix
        wide = radix * rank
        top = (devices + me) // (1 << (base + depth))
        rows = [pick[pl.ds(top * (radix >> h), radix >> h), :] for h in range(1, depth + 1)]
        table = padded_columns(rows, 16)
        moves = [None if stage == 0 and h == 0 else next(blocks) for h in range(depth)]
        eye = iota((wide, wide), 0) == iota((wide, wide), 1)
        select_all[0:wide, :wide] = jnp.where(eye, 1.0, 0.0)
        lift_all[0:wide, :wide] = jnp.where(eye, 1.0, 0.0)
        at, below, column = wide, 0, 0
        starts = [0]
        for h in range(1, depth + 1):
            starts.append(at)
            for p in range(radix >> h):
                pair = slice(below + 2 * rank * p, below + 2 * rank * (p + 1))
                here = slice(at + rank * p, at + rank * (p + 1))
                picked = one_hot(table[:rank, column : column + 1] == iota((rank, 2 * rank), 1))
                select_all[here, :wide] = dot(picked, select_all[pair, :wide].astype(BF16))
                if moves[h - 1] is None:
                    both = iota((2 * rank, rank), 0) % rank == iota((2 * rank, rank), 1)
                    moved = one_hot(both)
                else:
                    moved = moves[h - 1][2 * p : 2 * p + 2].reshape(2 * rank, rank)
                lift_all[here, :wide] = dot_first_right(moved, lift_all[pair, :wide])
                column += 1
            below, at = at, at + rank * (radix >> h)
        spots = [starts[h] + rank * (place // (1 << h)) for h in range(depth)]
        others = [starts[h] + rank * (place // (1 << h) + 1 - 2 * (place // (1 << h) % 2)) for h in range(depth)]
        spots = [pl.multiple_of(s, rank) for s in spots]
        others = [pl.multiple_of(s, rank) for s in others]
        for i, spot in enumerate(spots + others + [starts[depth]]):
            selects[stage, i * rank : (i + 1) * rank, :wide] = select_all[pl.ds(spot, rank), :wide].astype(BF16)
        for i, spot in enumerate(others + [starts[depth]]):
            high, low = split(lift_all[pl.ds(spot, rank), :wide])
            lifts[stage, 0, i * rank : (i + 1) * rank, :wide] = high
            lifts[stage, 1, i * rank : (i + 1) * rank, :wide] = low
        for h in range(depth):
            if chain is None:
                chain = jnp.where(iota((rank, rank), 0) == iota((rank, rank), 1), 1.0, 0.0)
            chains[stage, h * rank : (h + 1) * rank, :] = chain
            if moves[h] is None:
                step = own_transfer[0]
            else:
                step = moves[h][place // (1 << h)]
            high, low = split(chain)
            chain = dot(high, step) + dot(low, step)
        base += depth


def gathered_nodes(stage, depth, rank, cols, gathered, select, lift):
    whole = gathered[...].reshape(gathered.shape[0] * rank, gathered.shape[2])
    width = whole.shape[1] - 2 * cols
    wide = whole.shape[0]
    points = dot(select[:, :wide], whole[:, :width]).astype(BF16)
    tails = whole[:, width:]
    lifted = dot(lift[0, :, :wide], tails) + dot(lift[1, :, :wide], tails)
    if stage == 0:
        first = iota((lifted.shape[0], cols), 0) < rank
        lifted = jnp.where(first, lifted[:, :cols], lifted[:, cols:])
    else:
        lifted = lifted[:, :cols] + lifted[:, cols:]
    return points, lifted


def terms_of(own, other, weights, rank):
    count, width = own.shape
    gram = dot_last(own, other)
    own_wide, other_wide = own.astype(F32), other.astype(F32)
    across = jnp.sum(own_wide * own_wide, axis=1, keepdims=True)
    down = jnp.sum(other_wide * other_wide, axis=1, keepdims=True)
    down = jnp.broadcast_to(down, (count, 128)).T[0:1, :]
    kernel = kernel_of(across + down - 2.0 * gram, width)
    same = iota(gram.shape, 0) // rank == iota(gram.shape, 1) // rank
    return dot_wide(jnp.where(same, kernel, 0.0), weights)


def chained(chain, terms, rank):
    total = None
    for h in range(terms.shape[0] // rank):
        part = dot_wide(chain[h * rank : (h + 1) * rank, :], terms[h * rank : (h + 1) * rank, :])
        total = part if total is None else total + part
    return total


def hop_body(stage, depth, rank, cols, gathered, selects, lifts, payload, pairs, siblings):
    rows = depth * rank
    points, lifted = gathered_nodes(
        stage, depth, rank, cols, gathered, selects[stage, : (2 * depth + 1) * rank, :], lifts[stage, :, : rows + rank, :]
    )
    pairs[...] = points[: 2 * rows, :]
    siblings[...] = lifted[:rows, :]
    high = lifted[rows:, :].astype(BF16).astype(F32)
    tail = jnp.concatenate([high, lifted[rows:, :] - high], axis=1)
    sent = jnp.concatenate([points[2 * rows :, :], tail.astype(BF16)], axis=1)
    for r in range(payload.shape[0]):
        payload[r] = sent


def terms_body(stage, depth, rank, pairs, siblings, chains, before, after):
    rows = depth * rank
    terms = terms_of(pairs[:rows, :], pairs[rows:, :], siblings[...], rank)
    total = chained(chains[stage], terms, rank)
    after[...] = total + before[...] if before is not None else total


def final_body(stage, depth, rank, cols, gathered, selects, lifts, chains, before, spread, product):
    rows = depth * rank
    points, lifted = gathered_nodes(
        stage, depth, rank, cols, gathered, selects[stage, : 2 * rows, :], lifts[stage, :, :rows, :]
    )
    terms = terms_of(points[:rows, :], points[rows:, :], lifted, rank)
    field = chained(chains[stage], terms, rank)
    if before is not None:
        field = field + before[...]
    high = field.astype(BF16).astype(F32)
    low = field - high
    eye = jnp.where(iota((cols, cols), 0) == iota((cols, cols), 1), 1.0, 0.0)
    right = jnp.concatenate([eye, eye, high, high, low, jnp.zeros_like(low)], axis=0).astype(BF16)
    product[...] = dot(spread[...], right).astype(BF16)


def far_body(leaves, rank, cols, points, weights, transfer, result):
    at = 0
    count = leaves
    terms = []
    while count > 1:
        rows = slice(at, at + count * rank)
        kernel, _ = self_kernel(points[rows, :])
        here = iota(kernel.shape, 0) // rank
        there = iota(kernel.shape, 1) // rank
        partner = here + 1 - 2 * (here % 2)
        terms.append(dot_wide(jnp.where(there == partner, kernel, 0.0), weights[rows, :]))
        at += count * rank
        count //= 2
    below = None
    for height in reversed(range(len(terms))):
        count = leaves >> height
        nodes = []
        for n in range(count):
            moved = transfer[count + n - 1]
            term = terms[height][n * rank : (n + 1) * rank, :]
            if below is None:
                node = jnp.concatenate([term, moved.astype(F32), jnp.zeros((rank, 128 - cols - rank), F32)], axis=1)
            else:
                pad = jnp.zeros((rank, 128 - cols), F32)
                node = dot_right(moved, below[n // 2]) + jnp.concatenate([term, pad], axis=1)
            nodes.append(node)
        below = nodes
    result[...] = jnp.concatenate(below, axis=0)


def leaf_body(first, count, rank, order, emb, rhs_tree, basis, far, result):
    items = emb.shape[0]
    leaf = result.shape[0] // count
    cols = rhs_tree.shape[1]
    order_t = columns_of(order[...])
    for i in range(count):
        l = first + i
        rows = slice(l * leaf, (l + 1) * leaf)
        column = order_column(order_t, l)
        feats = dot(one_hot(column == iota((leaf, items), 1)), emb[...]).astype(BF16)
        kernel, eye = self_kernel(feats)
        kernel = jnp.where(eye, kernel + RIDGE, kernel).astype(BF16)
        near = dot(kernel, rhs_tree[rows, :])
        both = dot_right(basis[rows, :], far[l * rank : (l + 1) * rank, :])
        total = near + both[:, :cols]
        total_high = total.astype(BF16).astype(F32)
        moved = both[:, cols : cols + rank]
        moved_high = moved.astype(BF16).astype(F32)
        result[i * leaf : (i + 1) * leaf, :] = jnp.concatenate(
            [total_high, total - total_high, moved_high, moved - moved_high, moved_high, jnp.zeros_like(moved)], axis=1
        ).astype(BF16)


def spread_body(step, order, lower, upper, result):
    chunks = order.shape[0]
    row = jnp.concatenate([order[c : c + 1, :] for c in range(chunks)], axis=1)
    half = lower.shape[0]
    for b in range(result.shape[0] // step):
        mask = row == iota((step, row.shape[1]), 0) + b * step
        hot = one_hot(mask)
        result[b * step : (b + 1) * step, :] = (
            dot(hot[:, :half], lower[...]) + dot(hot[:, half:], upper[...])
        ).astype(BF16)


def call(body, outs, scratch=(), flops=1e8, name=None):
    return pl.pallas_call(
        body,
        out_shape=outs,
        scratch_shapes=list(scratch),
        cost_estimate=pl.CostEstimate(flops=int(flops), bytes_accessed=1 << 20, transcendentals=0),
        compiler_params=pltpu.CompilerParams(vmem_limit_bytes=VMEM_LIMIT),
        name=name,
    )


def shape(dims, dtype):
    return jax.ShapeDtypeStruct(dims, dtype)


def local(
    embeddings,
    rhs,
    item_order,
    leaf_basis,
    leaf_skel,
    local_transfer,
    local_pick,
    upper_transfer,
    upper_pick,
):
    leaves, rank = leaf_skel.shape
    items, cols = rhs.shape
    width = embeddings.shape[1]
    devices = lax.axis_size("leaf")
    radices = RADICES[devices]
    me = lax.axis_index("leaf")
    me = me.astype(jnp.int32).reshape(1)
    order = item_order.reshape(items // 128, 128)
    inner = (2 * leaves - 2) * rank

    payload, rhs_tree, points, weights = call(
        functools.partial(pre_body, leaves),
        (
            shape((radices[0], rank, width + 2 * cols), BF16),
            shape((items, cols), BF16),
            shape((inner, width), BF16),
            shape((inner, cols), F32),
        ),
        name="pre",
    )(order, rhs, leaf_basis, leaf_skel, local_pick, local_transfer, embeddings)

    stages = len(radices)
    most = max(radices)
    depths = [n.bit_length() - 1 for n in radices]
    deepest = max(depths)
    whole = pl.BlockSpec(memory_space=pltpu.VMEM)
    specs = [whole, pl.BlockSpec((1, rank, rank), lambda i, m: (0, 0, 0))]
    base = 0
    for stage, (n, depth) in enumerate(zip(radices, depths)):
        shift = base + depth
        for h in range(depth):
            if stage or h:
                specs.append(
                    pl.BlockSpec((n >> h, rank, rank), functools.partial(lambda s, i, m: ((devices + m[0]) // (1 << s), 0, 0), shift))
                )
        base += depth
    selects, lifts, chains = pl.pallas_call(
        functools.partial(prep_body, devices, radices),
        out_shape=(
            shape((stages, (2 * deepest + 1) * rank, most * rank), BF16),
            shape((stages, 2, (deepest + 1) * rank, most * rank), BF16),
            shape((stages, deepest * rank, rank), F32),
        ),
        grid_spec=pltpu.PrefetchScalarGridSpec(
            num_scalar_prefetch=1,
            grid=(1,),
            in_specs=specs,
            out_specs=(whole, whole, whole),
            scratch_shapes=[pltpu.VMEM((2 * most * rank, most * rank), F32)] * 2,
        ),
        cost_estimate=pl.CostEstimate(flops=int(1e9), bytes_accessed=1 << 20, transcendentals=0),
        compiler_params=pltpu.CompilerParams(vmem_limit_bytes=VMEM_LIMIT),
        name="prep",
    )(me, upper_pick, local_transfer, *([upper_transfer] * (len(specs) - 2)))

    far = call(
        functools.partial(far_body, leaves, rank, cols), shape((leaves * rank, 128), F32), flops=1e9, name="far"
    )(points, weights, local_transfer)
    halves = [
        call(
            functools.partial(leaf_body, first, leaves // 2, rank), shape((items // 2, 256), BF16), flops=2e9, name="leaf"
        )(order, embeddings, rhs_tree, leaf_basis, far)
        for first in (0, leaves // 2)
    ]
    spread = call(
        functools.partial(spread_body, 256), shape((items, 256), BF16), flops=2e9, name="spread"
    )(order, *halves)

    field = None
    base = 0
    for stage, (n, depth) in enumerate(zip(radices, depths)):
        stride = 1 << base
        groups = [
            [high * stride * n + low + stride * j for j in range(n)]
            for high in range(devices // (stride * n))
            for low in range(stride)
        ]
        gathered = lax.all_to_all(payload, "leaf", 0, 0, axis_index_groups=groups)
        base += depth
        if stage + 1 < stages:
            payload, pairs, siblings = call(
                functools.partial(hop_body, stage, depth, rank, cols),
                (
                    shape((radices[stage + 1], rank, width + 2 * cols), BF16),
                    shape((2 * depth * rank, width), BF16),
                    shape((depth * rank, cols), F32),
                ),
                name="hop",
            )(gathered, selects, lifts)
            if field is None:
                body = lambda a, b, c, o, stage=stage, depth=depth: terms_body(stage, depth, rank, a, b, c, None, o)
                field = call(body, shape((rank, cols), F32), name="terms")(pairs, siblings, chains)
            else:
                field = call(functools.partial(terms_body, stage, depth, rank), shape((rank, cols), F32), name="terms")(
                    pairs, siblings, chains, field
                )
    return call(
        functools.partial(final_body, stages - 1, depths[-1], rank, cols), shape((items, cols), BF16), name="final"
    )(gathered, selects, lifts, chains, field, spread)


def solution(mesh):
    return jax.shard_map(
        local,
        mesh=mesh,
        in_specs=(
            P("leaf", None),
            P("leaf", None),
            P("leaf"),
            P("leaf", None),
            P("leaf", None),
            P("leaf", None, None),
            P("leaf", None),
            P(),
            P(),
        ),
        out_specs=P("leaf", None),
        check_vma=False,
    )
```

time: 153 us -> 77.4 us (0.51)
  the two profiles are of different devices: /device:TPU:8 before, /device:TPU:16 now
where the time goes in v1:
time: 77.4 us; the launch traced here: 76.6 us
  starting transfers between devices  23.5 us (30%)
  local copies, waits for them, and re-layouts  23.1 us (30%)
  Pallas kernels  23 us (30%)
  waiting for transfers between devices  6.84 us (9%)
    all_to_all x3, starting transfers between devices, local(): gathered = lax.all_to_all(payload, 'leaf', 0, 0, axis_index_groups=groups)  23.5 us
    unnamed x42, local copies, waits for them, and re-layouts  22.2 us
    pallas_call x2, Pallas kernels, local(): call(functools.partial(leaf_body, first, leaves // 2, rank), shape((items...  8.49 us
    all_to_all x3, waiting for transfers between devices, local(): gathered = lax.all_to_all(payload, 'leaf', 0, 0, axis_index_groups=groups)  6.84 us
    pallas_call x1, Pallas kernels, local(): call(functools.partial(pre_body, leaves), (shape((radices[0], rank, width...  4.95 us
    pallas_call x1, Pallas kernels, local(): call(functools.partial(spread_body, 256), shape((items, 256), BF16), flop...  2.32 us
    pallas_call x2, Pallas kernels, local(): call(functools.partial(hop_body, stage, depth, rank, cols), (shape((radic...  2.05 us
    pallas_call x1, Pallas kernels, local(): pl.pallas_call(functools.partial(prep_body, devices, radices), out_shape=...  1.77 us
  transfers between devices with their start and end apart: 3, of which 2 were waited for; matrix products, arithmetic and copies ran while one was open for 11% of the time, Pallas kernels for 19%

profile of v1, /device:TPU:16, one launch (start us, length us, event | category | flops | bytes accessed | tf_op | source)
XLA Modules:
  0.0 76.6 jit_solution(6107827513701599752)
XLA Ops:
  0.0 1.2 %copy.11.basis = bf16[2048,32]{1,0:T(8,128)(2,1)S(1)} copy(bf16[2048,32]{0,1:T(8,128)(2,1)} %param.12) | data formatting | bytes 262144 | tf_op args[3]
  1.2 1.2 %copy.10.rhs = bf16[2048,64]{1,0:T(8,128)(2,1)S(1)} copy(bf16[2048,64]{0,1:T(8,128)(2,1)} %param.10) | data formatting | bytes 524288 | tf_op args[1]
  2.4 0.0 copy-start.1
  2.4 1.2 %copy-done.1 = bf16[2048,256]{1,0:T(8,128)(2,1)S(1)} copy-done((bf16[2048,256]{1,0:T(8,128)(2,1)S(1)}, bf16[2048,256]{1,0:T(8,128)(2,1)}, u32[]{:S(2)}) %copy-start.1) | copy-done | bytes 1048600
  3.6 0.0 copy-start.3
  3.6 0.9 %copy-done.3 = bf16[15,32,32]{2,1,0:T(8,128)(2,1)S(1)} copy-done((bf16[15,32,32]{2,1,0:T(8,128)(2,1)S(1)}, bf16[15,32,32]{2,1,0:T(8,128)(2,1)}, u32[]{:S(2)}) %copy-start.3) | copy-done | bytes 30744
  4.5 0.0 copy-start.5
  4.5 0.7 copy-done.5
  5.2 0.0 copy-start.7
  5.2 0.7 copy-done.7
  5.9 0.0 copy-start.8
  5.9 0.7 copy-done.8
  6.6 0.0 copy-start.4
  6.6 4.9 %pre.1 = (bf16[8,32,384]{2,1,0:T(8,128)(2,1)}, bf16[2048,64]{1,0:T(8,128)(2,1)S(1)}, bf16[448,256]{1,0:T(8,128)(2,1)S(1)}, f32[448,64]{1,0:T(8,128)S(1)}) custom-call(s32[16,128]{1,0:T(8,128)S(1)} %bitcast.2, bf16[2048,64]{1,0:T(8,128)(2,1)S(1)} %copy.10.rhs, bf16[2048,32]{1,0:T(8,128)(2,1)S(1)} %copy.11.basis, s32[8,32]{1,0:T(8,128)S(1)} %copy-done.7, ...), custom_call_target="tpu_custom_call" | custom-call | flops 100000000 | bytes 1048576 | tf_op jit(solution)/shard_map/pre/pallas_call | solution.py:383
  11.6 0.0 copy-start.9
  11.6 0.7 copy-done.9
  12.3 9.0 %all-to-all-start = ((bf16[8,32,384]{2,1,0:T(8,128)(2,1)}), bf16[8,32,384]{2,1,0:T(8,128)(2,1)S(1)}, u32[]{:S(2)}, u32[]{:S(2)}) async-start(bf16[8,32,384]{2,1,0:T(8,128)(2,1)} %get-tuple-element.18), calls=%async_computation | async-start | bytes 393216 | tf_op jit(solution)/shard_map/all_to_all | solution.py:450
  21.3 1.0 %copy.12.pick = s32[512,32]{1,0:T(8,128)S(1)} copy(s32[512,32]{0,1:T(8,128)} %param.17) | data formatting | bytes 131072 | tf_op args[8]
  22.3 7.2 %copy.13.refs_0_.refs_1_.refs_2_.refs_3_.refs_4_.refs_5_.refs_6_.refs_7_ = bf16[512,32,32]{2,1,0:T(8,128)(2,1)} copy(bf16[512,32,32]{0,2,1:T(8,128)(2,1)} %param.16) | data formatting | bytes 2097152 | tf_op args[7]
  29.4 0.0 copy-done.4
  29.4 0.0 copy-start
  29.4 2.2 %copy-done = bf16[512,32,32]{2,1,0:T(8,128)(2,1)S(1)} copy-done((bf16[512,32,32]{2,1,0:T(8,128)(2,1)S(1)}, bf16[512,32,32]{2,1,0:T(8,128)(2,1)}, u32[]{:S(2)}) %copy-start) | copy-done | bytes 1048600
  31.6 1.8 %prep.1 = (bf16[3,224,256]{2,1,0:T(8,128)(2,1)S(1)}, bf16[3,2,128,256]{3,2,1,0:T(8,128)(2,1)S(1)}, f32[3,96,32]{2,1,0:T(8,128)S(1)}) custom-call(s32[1]{0:T(128)} %bitcast.1.me_ref, s32[512,32]{1,0:T(8,128)S(1)} %copy.12.pick, bf16[15,32,32]{2,1,0:T(8,128)(2,1)S(1)} %copy-done.4, bf16[512,32,32]{2,1,0:T(8,128)(2,1)S(1)} %copy-done, ...), custom_call_target="tpu_custom_call" | custom-call | flops 1000000000 | bytes 1048576 | tf_op jit(solution)/shard_map/prep/pallas_call | solution.py:409
  33.4 0.0 copy-start.2
  33.4 0.0 copy-start.6
  33.4 0.0 all-to-all-done.gathered
  33.4 1.0 %hop.2 = (bf16[8,32,384]{2,1,0:T(8,128)(2,1)}, bf16[192,256]{1,0:T(8,128)(2,1)S(1)}, f32[96,64]{1,0:T(8,128)S(1)}) custom-call(bf16[8,32,384]{2,1,0:T(8,128)(2,1)S(1)} %all-to-all-done.gathered, bf16[3,224,256]{2,1,0:T(8,128)(2,1)S(1)} %get-tuple-element.19.selects, bf16[3,2,128,256]{3,2,1,0:T(8,128)(2,1)S(1)} %get-tuple-element.20.lifts), custom_call_target="tpu_custom_call" | custom-call | flops 100000000 | bytes 1048576 | tf_op jit(solution)/shard_map/hop/pallas_call | solution.py:453
  34.5 0.0 copy-start.11
  34.5 0.6 copy-done.11
  35.1 0.0 copy-start.13
  35.1 0.6 copy-done.13
  35.7 4.2 %all-to-all-start.1 = ((bf16[8,32,384]{2,1,0:T(8,128)(2,1)}), bf16[8,32,384]{2,1,0:T(8,128)(2,1)S(1)}, u32[]{:S(2)}, u32[]{:S(2)}) async-start(bf16[8,32,384]{2,1,0:T(8,128)(2,1)} %get-tuple-element.21), calls=%async_computation.1 | async-start | bytes 393216 | tf_op jit(solution)/shard_map/all_to_all | solution.py:450
  39.9 0.0 copy-start.10
  39.9 0.9 %copy-done.10 = f32[448,64]{1,0:T(8,128)S(1)} copy-done((f32[448,64]{1,0:T(8,128)S(1)}, f32[448,64]{1,0:T(8,128)}, u32[]{:S(2)}) %copy-start.10) | copy-done | bytes 114712
  40.8 1.4 %far.1 = f32[256,128]{1,0:T(8,128)S(1)} custom-call(bf16[448,256]{1,0:T(8,128)(2,1)S(1)} %get-tuple-element.29.points, f32[448,64]{1,0:T(8,128)S(1)} %copy-done.10, bf16[15,32,32]{2,1,0:T(8,128)(2,1)S(1)} %copy-done.4), custom_call_target="tpu_custom_call" | custom-call | flops 1000000000 | bytes 1048576 | tf_op jit(solution)/shard_map/far/pallas_call | solution.py:428
  42.2 0.0 copy-done.2
  42.2 0.0 copy-done.6
  42.2 4.2 %leaf.3.upper = bf16[1024,256]{1,0:T(8,128)(2,1)S(1)} custom-call(s32[16,128]{1,0:T(8,128)S(1)} %bitcast.3, bf16[2048,256]{1,0:T(8,128)(2,1)S(1)} %copy-done.2, bf16[2048,64]{1,0:T(8,128)(2,1)S(1)} %get-tuple-element.28.rhs_tree, bf16[2048,32]{1,0:T(8,128)(2,1)S(1)} %copy.11.basis, f32[256,128]{1,0:T(8,128)S(1)} %far.1), custom_call_target="tpu_custom_call" | custom-call | flops 2000000000 | bytes 1048576 | tf_op jit(solution)/shard_map/leaf/pallas_call | solution.py:432
  46.5 0.0 copy-start.15
  46.5 0.8 %copy-done.15 = bf16[1024,256]{1,0:T(8,128)(2,1)} copy-done((bf16[1024,256]{1,0:T(8,128)(2,1)}, bf16[1024,256]{1,0:T(8,128)(2,1)S(1)}, u32[]{:S(2)}) %copy-start.15) | copy-done | bytes 524312
  47.3 0.0 copy-start.17
  47.3 0.7 copy-done.17
  48.0 4.7 %all-to-all-done.1.gathered = bf16[8,32,384]{2,1,0:T(8,128)(2,1)S(1)} async-done(((bf16[8,32,384]{2,1,0:T(8,128)(2,1)}), bf16[8,32,384]{2,1,0:T(8,128)(2,1)S(1)}, u32[]{:S(2)}, u32[]{:S(2)}) %all-to-all-start.1) | async-done | bytes 196640 | tf_op jit(solution)/shard_map/all_to_all | solution.py:450
  52.6 1.0 %hop.3 = (bf16[8,32,384]{2,1,0:T(8,128)(2,1)}, bf16[192,256]{1,0:T(8,128)(2,1)S(1)}, f32[96,64]{1,0:T(8,128)S(1)}) custom-call(bf16[8,32,384]{2,1,0:T(8,128)(2,1)S(1)} %all-to-all-done.1.gathered, bf16[3,224,256]{2,1,0:T(8,128)(2,1)S(1)} %get-tuple-element.19.selects, bf16[3,2,128,256]{3,2,1,0:T(8,128)(2,1)S(1)} %get-tuple-element.20.lifts), custom_call_target="tpu_custom_call" | custom-call | flops 100000000 | bytes 1048576 | tf_op jit(solution)/shard_map/hop/pallas_call | solution.py:453
  53.6 10.3 %all-to-all-start.2 = ((bf16[8,32,384]{2,1,0:T(8,128)(2,1)}), bf16[8,32,384]{2,1,0:T(8,128)(2,1)S(1)}, u32[]{:S(2)}, u32[]{:S(2)}) async-start(bf16[8,32,384]{2,1,0:T(8,128)(2,1)} %get-tuple-element.22), calls=%async_computation.2 | async-start | bytes 393216 | tf_op jit(solution)/shard_map/all_to_all | solution.py:450
  64.0 0.0 copy-start.18
  64.0 0.9 %copy-done.18 = f32[256,128]{1,0:T(8,128)S(1)} copy-done((f32[256,128]{1,0:T(8,128)S(1)}, f32[256,128]{1,0:T(8,128)}, u32[]{:S(2)}) %copy-start.18) | copy-done | bytes 131096
  64.9 0.0 copy-start.16
  64.9 4.2 %leaf.2.lower = bf16[1024,256]{1,0:T(8,128)(2,1)S(1)} custom-call(s32[16,128]{1,0:T(8,128)S(1)} %bitcast.4, bf16[2048,256]{1,0:T(8,128)(2,1)S(1)} %copy-done.2, bf16[2048,64]{1,0:T(8,128)(2,1)S(1)} %get-tuple-element.28.rhs_tree, bf16[2048,32]{1,0:T(8,128)(2,1)S(1)} %copy.11.basis, f32[256,128]{1,0:T(8,128)S(1)} %copy-done.18), custom_call_target="tpu_custom_call" | custom-call | flops 2000000000 | bytes 1048576 | tf_op jit(solution)/shard_map/leaf/pallas_call | solution.py:432
  69.1 0.0 copy-done.16
  69.1 0.0 copy-start.12
  69.1 0.0 copy-start.14
  69.1 2.3 %spread.1 = bf16[2048,256]{1,0:T(8,128)(2,1)S(1)} custom-call(s32[16,128]{1,0:T(8,128)S(1)} %bitcast.5, bf16[1024,256]{1,0:T(8,128)(2,1)S(1)} %leaf.2.lower, bf16[1024,256]{1,0:T(8,128)(2,1)S(1)} %copy-done.16), custom_call_target="tpu_custom_call" | custom-call | flops 2000000000 | bytes 1048576 | tf_op jit(solution)/shard_map/spread/pallas_call | solution.py:437
  71.5 0.0 copy-done.12
  71.5 0.0 copy-done.14
  71.5 0.5 terms.2.before
  72.0 0.5 terms.3.before
  72.4 2.2 %all-to-all-done.2.gathered = bf16[8,32,384]{2,1,0:T(8,128)(2,1)S(1)} async-done(((bf16[8,32,384]{2,1,0:T(8,128)(2,1)}), bf16[8,32,384]{2,1,0:T(8,128)(2,1)S(1)}, u32[]{:S(2)}, u32[]{:S(2)}) %all-to-all-start.2) | async-done | bytes 196640 | tf_op jit(solution)/shard_map/all_to_all | solution.py:450
  74.6 1.1 %final.1 = bf16[2048,64]{1,0:T(8,128)(2,1)S(1)} custom-call(bf16[8,32,384]{2,1,0:T(8,128)(2,1)S(1)} %all-to-all-done.2.gathered, bf16[3,224,256]{2,1,0:T(8,128)(2,1)S(1)} %get-tuple-element.19.selects, bf16[3,2,128,256]{3,2,1,0:T(8,128)(2,1)S(1)} %get-tuple-element.20.lifts, f32[3,96,32]{2,1,0:T(8,128)S(1)} %get-tuple-element.23.c.chains, ...), custom_call_target="tpu_custom_call" | custom-call | flops 100000000 | bytes 1048576 | tf_op jit(solution)/shard_map/final/pallas_call | solution.py:469
  75.7 0.9 %copy.23 = bf16[2048,64]{0,1:T(8,128)(2,1)} copy(bf16[2048,64]{1,0:T(8,128)(2,1)S(1)} %final.1) | data formatting | bytes 524288 | tf_op jit(solution)/shard_map/final/pallas_call | solution.py:469
Async XLA Ops:
  2.4 1.2 %copy-start.1 = (bf16[2048,256]{1,0:T(8,128)(2,1)S(1)}, bf16[2048,256]{1,0:T(8,128)(2,1)}, u32[]{:S(2)}) copy-start(bf16[2048,256]{1,0:T(8,128)(2,1)} %emb.5) | copy-start | bytes 3145732
  3.6 0.9 %copy-start.3 = (bf16[15,32,32]{2,1,0:T(8,128)(2,1)S(1)}, bf16[15,32,32]{2,1,0:T(8,128)(2,1)}, u32[]{:S(2)}) copy-start(bf16[15,32,32]{2,1,0:T(8,128)(2,1)} %transfer.3) | copy-start | bytes 92164
  4.5 0.7 copy-start.5
  5.2 0.7 copy-start.7
  5.9 0.7 copy-start.8
  6.6 22.8 %copy-start.4 = (bf16[15,32,32]{2,1,0:T(8,128)(2,1)S(1)}, bf16[15,32,32]{2,1,0:T(8,128)(2,1)}, u32[]{:S(2)}) copy-start(bf16[15,32,32]{2,1,0:T(8,128)(2,1)} %transfer.3) | copy-start | bytes 92164
  11.6 0.7 copy-start.9
  12.3 21.2 %all-to-all-start = ((bf16[8,32,384]{2,1,0:T(8,128)(2,1)}), bf16[8,32,384]{2,1,0:T(8,128)(2,1)S(1)}, u32[]{:S(2)}, u32[]{:S(2)}) async-start(bf16[8,32,384]{2,1,0:T(8,128)(2,1)} %get-tuple-element.18), calls=%async_computation | async-start | bytes 393216 | tf_op jit(solution)/shard_map/all_to_all | solution.py:450
  29.4 2.2 %copy-start = (bf16[512,32,32]{2,1,0:T(8,128)(2,1)S(1)}, bf16[512,32,32]{2,1,0:T(8,128)(2,1)}, u32[]{:S(2)}) copy-start(bf16[512,32,32]{2,1,0:T(8,128)(2,1)} %copy.13.refs_0_.refs_1_.refs_2_.refs_3_.refs_4_.refs_5_.refs_6_.refs_7_) | copy-start | bytes 3145732
  33.4 8.8 %copy-start.2 = (bf16[2048,256]{1,0:T(8,128)(2,1)S(1)}, bf16[2048,256]{1,0:T(8,128)(2,1)}, u32[]{:S(2)}) copy-start(bf16[2048,256]{1,0:T(8,128)(2,1)} %emb.5) | copy-start | bytes 3145732
  33.4 8.8 %copy-start.6 = (s32[2048]{0:T(1024)S(1)}, s32[2048]{0:T(1024)}, u32[]{:S(2)}) copy-start(s32[2048]{0:T(1024)} %param.11) | copy-start | bytes 24580
  34.5 0.6 copy-start.11
  35.1 0.6 copy-start.13
  35.7 16.9 %all-to-all-start.1 = ((bf16[8,32,384]{2,1,0:T(8,128)(2,1)}), bf16[8,32,384]{2,1,0:T(8,128)(2,1)S(1)}, u32[]{:S(2)}, u32[]{:S(2)}) async-start(bf16[8,32,384]{2,1,0:T(8,128)(2,1)} %get-tuple-element.21), calls=%async_computation.1 | async-start | bytes 393216 | tf_op jit(solution)/shard_map/all_to_all | solution.py:450
  39.9 0.9 %copy-start.10 = (f32[448,64]{1,0:T(8,128)S(1)}, f32[448,64]{1,0:T(8,128)}, u32[]{:S(2)}) copy-start(f32[448,64]{1,0:T(8,128)} %copy-done.9) | copy-start | bytes 344068
  46.5 0.8 %copy-start.15 = (bf16[1024,256]{1,0:T(8,128)(2,1)}, bf16[1024,256]{1,0:T(8,128)(2,1)S(1)}, u32[]{:S(2)}) copy-start(bf16[1024,256]{1,0:T(8,128)(2,1)S(1)} %leaf.3.upper) | copy-start | bytes 1572868
  47.3 0.7 copy-start.17
  53.6 21.0 %all-to-all-start.2 = ((bf16[8,32,384]{2,1,0:T(8,128)(2,1)}), bf16[8,32,384]{2,1,0:T(8,128)(2,1)S(1)}, u32[]{:S(2)}, u32[]{:S(2)}) async-start(bf16[8,32,384]{2,1,0:T(8,128)(2,1)} %get-tuple-element.22), calls=%async_computation.2 | async-start | bytes 393216 | tf_op jit(solution)/shard_map/all_to_all | solution.py:450
  64.0 0.9 %copy-start.18 = (f32[256,128]{1,0:T(8,128)S(1)}, f32[256,128]{1,0:T(8,128)}, u32[]{:S(2)}) copy-start(f32[256,128]{1,0:T(8,128)} %copy-done.17) | copy-start | bytes 393220
  64.9 4.2 %copy-start.16 = (bf16[1024,256]{1,0:T(8,128)(2,1)S(1)}, bf16[1024,256]{1,0:T(8,128)(2,1)}, u32[]{:S(2)}) copy-start(bf16[1024,256]{1,0:T(8,128)(2,1)} %copy-done.15) | copy-start | bytes 1572868
  69.1 2.4 %copy-start.12 = (bf16[192,256]{1,0:T(8,128)(2,1)S(1)}, bf16[192,256]{1,0:T(8,128)(2,1)}, u32[]{:S(2)}) copy-start(bf16[192,256]{1,0:T(8,128)(2,1)} %copy-done.11) | copy-start | bytes 294916
  69.1 2.4 %copy-start.14 = (f32[96,64]{1,0:T(8,128)S(1)}, f32[96,64]{1,0:T(8,128)}, u32[]{:S(2)}) copy-start(f32[96,64]{1,0:T(8,128)} %copy-done.13) | copy-start | bytes 73732

commit v2 on v1

v2 whole, which is shorter than its diff:
```python
import functools

import jax
import jax.numpy as jnp
from jax import lax
from jax.experimental import pallas as pl
from jax.experimental.pallas import tpu as pltpu
from jax.sharding import PartitionSpec as P

RIDGE = 1.0
RADICES = {512: (8, 4, 8)}
F32 = jnp.float32
BF16 = jnp.bfloat16
ALL_VMEM = 63 * 1024 * 1024
VMEM_LIMIT = 8 * 1024 * 1024


def dot(a, b):
    return jnp.dot(a, b, preferred_element_type=F32)


def dot_first(a, b):
    return lax.dot_general(a, b, (((0,), (0,)), ((), ())), preferred_element_type=F32)


def dot_last(a, b):
    return lax.dot_general(a, b, (((1,), (1,)), ((), ())), preferred_element_type=F32)


def split(x):
    high = x.astype(BF16)
    return high, (x - high.astype(F32)).astype(BF16)


def dot_wide(a, b):
    a_high, a_low = split(a)
    b_high, b_low = split(b)
    return dot(a_high, b_high) + dot(a_low, b_high) + dot(a_high, b_low)


def dot_right(a, b):
    high, low = split(b)
    return dot(a, high) + dot(a, low)


def dot_first_right(a, b):
    high, low = split(b)
    return dot_first(a, high) + dot_first(a, low)


def dot_first_wide(a, b):
    a_high, a_low = split(a)
    b_high, b_low = split(b)
    return dot_first(a_high, b_high) + dot_first(a_low, b_high) + dot_first(a_high, b_low)


def iota(shape, axis):
    return lax.broadcasted_iota(jnp.int32, shape, axis)


def one_hot(mask):
    return jnp.where(mask, 1.0, 0.0).astype(BF16)


def kernel_of(distance, width):
    return lax.rsqrt(1.0 + jnp.maximum(distance, 0.0) * (1.0 / width))


def self_kernel(points):
    count, width = points.shape
    gram = dot_last(points, points)
    eye = iota(gram.shape, 0) == iota(gram.shape, 1)
    diagonal = jnp.where(eye, gram, 0.0)
    across = jnp.sum(diagonal, axis=1, keepdims=True)
    down = jnp.sum(diagonal, axis=0, keepdims=True)
    return kernel_of(across + down - 2.0 * gram, width), eye


def columns_of(table):
    return table.astype(F32).T.astype(jnp.int32)


def order_column(order_t, leaf):
    return jnp.concatenate([order_t[:, 2 * leaf : 2 * leaf + 1], order_t[:, 2 * leaf + 1 : 2 * leaf + 2]], axis=0)


def order_row(order, leaf):
    return jnp.concatenate([order[2 * leaf : 2 * leaf + 1, :], order[2 * leaf + 1 : 2 * leaf + 2, :]], axis=1)


def padded_columns(tables, rows):
    stacked = jnp.concatenate(tables, axis=0)
    short = rows - stacked.shape[0]
    if short:
        stacked = jnp.concatenate([stacked, jnp.zeros((short, stacked.shape[1]), jnp.int32)], axis=0)
    wide = jnp.concatenate([stacked, jnp.zeros((rows, 128 - stacked.shape[1]), jnp.int32)], axis=1)
    return columns_of(wide)


def fetch(sources, targets, sems):
    copies = [pltpu.make_async_copy(s, t, sems.at[i]) for i, (s, t) in enumerate(zip(sources, targets))]
    for copy in copies:
        copy.start()
    return copies


def digits_of(places, leaf):
    return (places // leaf).astype(F32).astype(BF16), (places & (leaf - 1)).astype(F32).astype(BF16)


def skeleton_ids(leaves, leaf, order, table, rank):
    rows = jnp.concatenate([order[pl.ds(0, leaves, stride=2), :], order[pl.ds(1, leaves, stride=2), :]], axis=1)
    high, low = digits_of(rows, leaf)
    digits = jnp.concatenate([high.astype(F32), low.astype(F32)], axis=0).astype(BF16)
    spots = jnp.concatenate([table[:rank, l : l + 1] for l in range(leaves)], axis=0)
    found = dot_last(one_hot(spots == iota((spots.shape[0], leaf), 1)), digits)
    lane = iota(found.shape, 1)
    own = iota(found.shape, 0) // rank
    block = jnp.sum(jnp.where(lane == own, found, 0.0), axis=1, keepdims=True)
    offset = jnp.sum(jnp.where(lane == own + leaves, found, 0.0), axis=1, keepdims=True)
    lane = iota((spots.shape[0], 128), 1)
    return jnp.where(lane == 0, block, jnp.where(lane == 1, offset, 0.0)).astype(BF16)


def items_of(ids, leaf, emb):
    ids = ids.astype(F32).astype(jnp.int32)
    spots = ids[:, :1] * leaf + ids[:, 1:2]
    return dot(one_hot(spots == iota((ids.shape[0], emb.shape[0]), 1)), emb[...]).astype(BF16)


def picked_of(nodes, parents, table, leaves, rank):
    rows = jnp.concatenate(
        [table[:rank, leaves + q - 1 : leaves + q] + 2 * rank * (q - parents) for q in range(parents, 2 * parents)], axis=0
    )
    return dot(one_hot(rows == iota((parents * rank, nodes.shape[0]), 1)), nodes).astype(BF16)


def pre_body(leaves, *refs):
    sources, (payload, rhs_tree, weights), targets, sems = refs[:7], refs[7:10], refs[10:17], refs[17]
    copies = fetch(sources, targets, sems)
    order, skel, pick, rhs, basis, transfer, emb = targets
    cols, items = rhs.shape
    leaf = items // leaves
    rank = skel.shape[1]
    blocks = items // leaf
    for copy in copies[:3]:
        copy.wait()
    table = padded_columns([skel[...], pick[...]], 16)
    nodes = skeleton_ids(leaves, leaf, order, table, rank)
    parents = leaves // 2
    while parents:
        nodes = picked_of(nodes, parents, table, leaves, rank)
        parents //= 2
    for copy in copies[3:6]:
        copy.wait()
    joined = jnp.concatenate([rhs[:, b * leaf : (b + 1) * leaf] for b in range(blocks)], axis=0)
    level = []
    for l in range(leaves):
        row = order_row(order, l)
        low, high = row & (leaf - 1), row // leaf
        found = dot(joined, one_hot(low == iota((leaf, leaf), 0)))
        total = None
        for b in range(blocks):
            part = jnp.where(high == b, found[b * cols : (b + 1) * cols, :], 0.0)
            total = part if total is None else total + part
        picked = total.astype(BF16)
        rhs_tree[:, l * leaf : (l + 1) * leaf] = picked
        level.append(dot_last(basis[:, l * leaf : (l + 1) * leaf], picked))
    chain = [transfer[1].astype(F32), transfer[2].astype(F32)]
    count = 4
    while count <= leaves:
        chain = [dot_right(transfer[count + n - 1], chain[n // 2]) for n in range(count)]
        count *= 2
    chain = jnp.concatenate(chain, axis=0)
    high, low = split(chain)
    chain = jnp.concatenate([chain, dot(high, transfer[0]) + dot(low, transfer[0])], axis=1)
    level = jnp.concatenate(level, axis=0)
    weights[...] = level
    top = dot_first_wide(chain, level)
    copies[6].wait()
    nodes = items_of(nodes, leaf, emb)
    payload[...] = jnp.concatenate([nodes, top[:rank, :].astype(BF16), top[rank:, :].astype(BF16)], axis=1)


def packed(weights, width):
    rank, cols = weights.shape
    rows = rank * cols // width
    return jnp.concatenate([weights[r : r + rows, :] for r in range(0, rank, rows)], axis=1)


def send(payload, points, weights):
    rank, width = points.shape
    points = points.astype(BF16)
    tail = packed(weights, width).astype(BF16)
    for r in range(payload.shape[0]):
        payload[r, :rank, :] = points
        payload[r, rank:, :] = tail


def side_body(rank, me_ref, mine, pick, hot, kept):
    me = me_ref[0]
    devices = pick.shape[1]
    parent = one_hot(iota((8, devices), 1) == (devices + me) // 2)
    spots = dot_last(pick[...].astype(F32).astype(BF16), parent)[:, :1].astype(jnp.int32)
    shift = jnp.where(me % 2 == 0, 0, rank)
    spots = jnp.where(spots >= shift, spots - shift, spots + rank)
    hot[...] = one_hot(spots == iota((rank, 2 * rank), 1))
    kept[...] = mine[...]


def pair_body(rank, cols, hot, mine, other, payload, pairs, siblings):
    width = mine.shape[1] - 2 * cols
    both = jnp.concatenate([mine[:, :width], other[:, :width]], axis=0)
    pairs[...] = both
    siblings[...] = other[:, width : width + cols].astype(F32)
    total = mine[:, width + cols :].astype(F32) + other[:, width + cols :].astype(F32)
    send(payload, dot(hot[...], both), total)


def slots_of(radix):
    starts, at = [], 0
    for h in range(radix.bit_length()):
        starts.append(at)
        at += radix >> h
    return starts


def prep_body(devices, radices, me_ref, pick_hbm, upper_hbm, local_hbm, *refs):
    selects, lifts, chains, select_all, lift_all, pick, upper, own_transfer, rows_of, sems = refs
    copies = fetch((pick_hbm, upper_hbm, local_hbm.at[pl.ds(0, 1)]), (pick, upper, own_transfer), sems)
    rank = own_transfer.shape[1]
    me = me_ref[0]
    most = max(radices)
    slots = 2 * most
    nodes = slots * len(radices)
    here = iota((nodes, devices), 0)
    wanted = jnp.full((nodes, devices), -1, jnp.int32)
    base = 1
    for stage, radix in enumerate(radices):
        depth = radix.bit_length() - 1
        top = (devices + me) // (1 << (base + depth))
        for h, start in enumerate(slots_of(radix)):
            first = stage * slots + start
            inside = (here >= first) & (here < first + (radix >> h))
            wanted = jnp.where(inside, here - first + top * (radix >> h), wanted)
        base += depth
    hot = one_hot(wanted == iota((nodes, devices), 1))
    for copy in copies:
        copy.wait()
    table = dot_last(pick[...].astype(F32).astype(BF16), hot).astype(jnp.int32)
    flat = dot_last(hot, upper[...].reshape(rank * rank, devices))
    for a in range(rank):
        rows_of[a * nodes : (a + 1) * nodes, :] = flat[:, a * rank : (a + 1) * rank]

    def moved_of(slot):
        return rows_of[pl.ds(slot, rank, stride=nodes), :]

    base = 1
    chain = own_transfer[0].astype(F32)
    for stage, radix in enumerate(radices):
        depth = radix.bit_length() - 1
        place = (me // (1 << base)) % radix
        wide = radix * rank
        starts = [rank * s for s in slots_of(radix)]
        eye = iota((wide, wide), 0) == iota((wide, wide), 1)
        select_all[0:wide, :wide] = jnp.where(eye, 1.0, 0.0)
        lift_all[0:wide, :wide] = jnp.where(eye, 1.0, 0.0)
        for h in range(1, depth + 1):
            below, at = starts[h - 1], starts[h]
            for p in range(radix >> h):
                pair = slice(below + 2 * rank * p, below + 2 * rank * (p + 1))
                spot = slice(at + rank * p, at + rank * (p + 1))
                slot = stage * slots + at // rank + p
                picked = one_hot(table[:, slot : slot + 1] == iota((rank, 2 * rank), 1))
                select_all[spot, :wide] = dot(picked, select_all[pair, :wide].astype(BF16))
                child = stage * slots + below // rank + 2 * p
                moved = jnp.concatenate([moved_of(child), moved_of(child + 1)], axis=0).astype(BF16)
                lift_all[spot, :wide] = dot_first_right(moved, lift_all[pair, :wide])
        steps = [place // (1 << h) for h in range(depth)]
        mine = [pl.multiple_of(starts[h] + rank * s, rank) for h, s in enumerate(steps)]
        others = [pl.multiple_of(starts[h] + rank * (s + 1 - 2 * (s % 2)), rank) for h, s in enumerate(steps)]
        for i, spot in enumerate(mine + others + [starts[depth]]):
            selects[stage, i * rank : (i + 1) * rank, :wide] = select_all[pl.ds(spot, rank), :wide].astype(BF16)
        for i, spot in enumerate(others + [starts[depth]]):
            high, low = split(lift_all[pl.ds(spot, rank), :wide])
            lifts[stage, 0, i * rank : (i + 1) * rank, :wide] = high
            lifts[stage, 1, i * rank : (i + 1) * rank, :wide] = low
        for h in range(depth):
            step = moved_of(stage * slots + starts[h] // rank + steps[h]).astype(BF16)
            chains[stage, h * rank : (h + 1) * rank, :] = chain
            high, low = split(chain)
            chain = dot(high, step) + dot(low, step)
        base += depth


def gathered_nodes(rank, cols, gathered, select, lift):
    count, rows, width = gathered.shape
    wide = count * rank
    points = dot(select[:, :wide], gathered[:, :rank, :].reshape(wide, width)).astype(BF16)
    tails = gathered[:, rank:, :].astype(F32)
    parts = [tails[j, :, c : c + cols] for j in range(count) for c in range(0, width, cols)]
    weights = jnp.concatenate(parts, axis=0).astype(BF16)
    return points, dot(lift[0, :, :wide], weights) + dot(lift[1, :, :wide], weights)


def terms_of(own, other, weights, rank):
    count, width = own.shape
    gram = dot_last(own, other)
    own_wide, other_wide = own.astype(F32), other.astype(F32)
    across = jnp.sum(own_wide * own_wide, axis=1, keepdims=True)
    down = jnp.sum(other_wide * other_wide, axis=1, keepdims=True)
    down = jnp.broadcast_to(down, (count, 128)).T[0:1, :]
    kernel = kernel_of(across + down - 2.0 * gram, width)
    same = iota(gram.shape, 0) // rank == iota(gram.shape, 1) // rank
    return dot_wide(jnp.where(same, kernel, 0.0), weights)


def chained(chain, terms, rank):
    total = None
    for h in range(terms.shape[0] // rank):
        part = dot_wide(chain[h * rank : (h + 1) * rank, :], terms[h * rank : (h + 1) * rank, :])
        total = part if total is None else total + part
    return total


def hop_body(stage, depth, rank, cols, gathered, selects, lifts, payload, pairs, siblings):
    rows = depth * rank
    points, lifted = gathered_nodes(
        rank, cols, gathered, selects[stage, : (2 * depth + 1) * rank, :], lifts[stage, :, : rows + rank, :]
    )
    pairs[...] = points[: 2 * rows, :]
    siblings[...] = lifted[:rows, :]
    send(payload, points[2 * rows :, :], lifted[rows:, :])


def terms_body(depths, rank, chains, *refs):
    total = terms_of(refs[0][:rank, :], refs[0][rank:, :], refs[1][...], rank)
    for stage, depth in enumerate(depths):
        pairs, siblings = refs[2 * stage + 2], refs[2 * stage + 3]
        rows = depth * rank
        terms = terms_of(pairs[:rows, :], pairs[rows:, :], siblings[...], rank)
        total = total + chained(chains[stage], terms, rank)
    refs[-1][...] = total


def final_body(stage, depth, rank, cols, gathered, selects, lifts, chains, before, spread, product):
    rows = depth * rank
    points, lifted = gathered_nodes(
        rank, cols, gathered, selects[stage, : 2 * rows, :], lifts[stage, :, :rows, :]
    )
    terms = terms_of(points[:rows, :], points[rows:, :], lifted, rank)
    field = chained(chains[stage], terms, rank) + before[...]
    high = field.astype(BF16).astype(F32)
    low = field - high
    eye = jnp.where(iota((cols, cols), 0) == iota((cols, cols), 1), 1.0, 0.0)
    right = jnp.concatenate([eye, eye, high, high, low, jnp.zeros_like(low)], axis=0).astype(BF16)
    product[...] = dot_first(right, spread[...]).astype(BF16)


def far_body(leaves, parts, rank, cols, pick, weights, transfer, *refs):
    count = leaves
    terms = []
    table = padded_columns([pick[...]], 8)
    points = jnp.concatenate([ref[...] for ref in refs[:parts]], axis=0)
    result = refs[parts]
    level = weights[...]
    while count > 1:
        kernel, _ = self_kernel(points)
        here = iota(kernel.shape, 0) // rank
        there = iota(kernel.shape, 1) // rank
        partner = here + 1 - 2 * (here % 2)
        terms.append(dot_wide(jnp.where(there == partner, kernel, 0.0), level))
        half = count // 2
        if half > 1:
            points = picked_of(points, half, table, 0, rank)
            level = jnp.concatenate(
                [
                    dot_first_right(
                        transfer[2 * q - 1 : 2 * q + 1].reshape(2 * rank, rank),
                        level[2 * rank * (q - half) : 2 * rank * (q - half + 1), :],
                    )
                    for q in range(half, 2 * half)
                ],
                axis=0,
            )
        count = half
    below = None
    for height in reversed(range(len(terms))):
        count = leaves >> height
        nodes = []
        for n in range(count):
            moved = transfer[count + n - 1]
            term = terms[height][n * rank : (n + 1) * rank, :]
            if below is None:
                node = jnp.concatenate([term, moved.astype(F32), jnp.zeros((rank, 128 - cols - rank), F32)], axis=1)
            else:
                pad = jnp.zeros((rank, 128 - cols), F32)
                node = dot_right(moved, below[n // 2]) + jnp.concatenate([term, pad], axis=1)
            nodes.append(node)
        below = nodes
    result[...] = jnp.concatenate(below, axis=0)


def leaf_body(first, count, rank, order, emb, rhs_tree, skel, near, points):
    items = emb.shape[0]
    leaf = near.shape[1] // count
    order_t = columns_of(order[...])
    table = padded_columns([skel[...]], 8)
    for i in range(0, count, 2):
        column = jnp.concatenate([order_column(order_t, first + i), order_column(order_t, first + i + 1)], axis=0)
        high, low = digits_of(column, leaf)
        offset = one_hot(iota((2 * leaf, leaf), 1) == (column & (leaf - 1)))
        block = jnp.broadcast_to(high, (2 * leaf, leaf))
        hot = jnp.concatenate([jnp.where(block == b, offset, jnp.zeros_like(offset)) for b in range(items // leaf)], axis=1)
        both = dot(hot, emb[...]).astype(BF16)
        for j in range(i, i + 2):
            l = first + j
            feats = both[(j - i) * leaf : (j - i + 1) * leaf, :]
            kernel, eye = self_kernel(feats)
            kernel = jnp.where(eye, kernel + RIDGE, kernel).astype(BF16)
            near[:, j * leaf : (j + 1) * leaf] = dot(rhs_tree[:, l * leaf : (l + 1) * leaf], kernel)
            spots = one_hot(table[:rank, l : l + 1] == iota((rank, leaf), 1))
            points[j * rank : (j + 1) * rank, :] = dot(spots, feats).astype(BF16)


def spread_body(parts, leaf, rank, order, basis, far, *refs):
    near, result, tree, offset, block = refs[:parts], refs[parts], refs[parts + 1], refs[parts + 2], refs[parts + 3]
    items = basis.shape[1]
    cols = near[0].shape[0]
    order_t = columns_of(order[...])
    for c in range(order.shape[0]):
        column = order_t[:, c : c + 1]
        rows = slice(c * 128, (c + 1) * 128)
        offset[rows, :] = one_hot(iota((128, leaf), 1) == (column & (leaf - 1)))
        block[rows, :] = jnp.broadcast_to(digits_of(column, leaf)[0], (128, leaf))
    l = 0
    for part in near:
        for i in range(part.shape[1] // leaf):
            lanes = slice(l * leaf, (l + 1) * leaf)
            high, low = split(far[l * rank : (l + 1) * rank, :])
            both = dot_first(high, basis[:, lanes]) + dot_first(low, basis[:, lanes])
            total = part[:, i * leaf : (i + 1) * leaf] + both[:cols, :]
            total_high = total.astype(BF16).astype(F32)
            moved = both[cols : cols + rank, :]
            moved_high = moved.astype(BF16).astype(F32)
            tree[:, lanes] = jnp.concatenate(
                [total_high, total - total_high, moved_high, moved - moved_high, moved_high, jnp.zeros_like(moved)], axis=0
            ).astype(BF16)
            l += 1
    for b in range(items // leaf):
        hot = jnp.where(block[...] == b, offset[...], jnp.zeros_like(offset))
        result[:, b * leaf : (b + 1) * leaf] = dot(tree[...], hot).astype(BF16)


def call(body, outs, scratch=(), flops=1e8, name=None, specs=None, limit=VMEM_LIMIT):
    extra = {} if specs is None else {"in_specs": specs}
    return pl.pallas_call(
        body,
        out_shape=outs,
        scratch_shapes=list(scratch),
        cost_estimate=pl.CostEstimate(flops=int(flops), bytes_accessed=1 << 20, transcendentals=0),
        compiler_params=pltpu.CompilerParams(vmem_limit_bytes=limit),
        name=name,
        **extra,
    )


def after(values, earlier):
    return lax.optimization_barrier((*values, earlier))[:-1]


def shape(dims, dtype):
    return jax.ShapeDtypeStruct(dims, dtype)


def local(
    embeddings,
    rhs,
    item_order,
    leaf_basis,
    leaf_skel,
    local_transfer,
    local_pick,
    upper_transfer,
    upper_pick,
):
    leaves, rank = leaf_skel.shape
    items, cols = rhs.shape
    width = embeddings.shape[1]
    devices = lax.axis_size("leaf")
    radices = RADICES[devices]
    me = lax.axis_index("leaf")
    me = me.astype(jnp.int32).reshape(1)
    order = item_order.reshape(items // 128, 128)
    basis_t = leaf_basis.T
    far_away = pl.BlockSpec(memory_space=pltpu.HBM)

    given = (order, leaf_skel, local_pick, rhs.T, basis_t, local_transfer, embeddings)
    payload, rhs_tree, weights = call(
        functools.partial(pre_body, leaves),
        (
            shape((rank, width + 2 * cols), BF16),
            shape((cols, items), BF16),
            shape((leaves * rank, cols), F32),
        ),
        scratch=[pltpu.VMEM(x.shape, x.dtype) for x in given] + [pltpu.SemaphoreType.DMA((len(given),))],
        specs=[far_away] * len(given),
        limit=ALL_VMEM,
        name="pre",
    )(*given)
    other = lax.ppermute(payload, "leaf", [(i, i ^ 1) for i in range(devices)])
    memory = pl.BlockSpec(memory_space=pltpu.SMEM)
    whole = pl.BlockSpec(memory_space=pltpu.VMEM)
    hot, kept = call(
        functools.partial(side_body, rank),
        (shape((rank, 2 * rank), BF16), shape(payload.shape, BF16)),
        specs=[memory] + [whole] * 2,
        name="side",
    )(me, payload, upper_pick.T)
    sent = rank + rank * cols // width
    payload, pairs, siblings = call(
        functools.partial(pair_body, rank, cols),
        (
            shape((radices[0], sent, width), BF16),
            shape((2 * rank, width), BF16),
            shape((rank, cols), F32),
        ),
        name="pair",
    )(hot, kept, other)
    held = [pairs, siblings]

    stages = len(radices)
    most = max(radices)
    depths = [n.bit_length() - 1 for n in radices]
    deepest = max(depths)
    nodes = 2 * most * stages
    (me,) = after((me,), payload)
    selects, lifts, chains = call(
        functools.partial(prep_body, devices, radices),
        (
            shape((stages, (2 * deepest + 1) * rank, most * rank), BF16),
            shape((stages, 2, (deepest + 1) * rank, most * rank), BF16),
            shape((stages, deepest * rank, rank), F32),
        ),
        scratch=[
            pltpu.VMEM((2 * most * rank, most * rank), F32),
            pltpu.VMEM((2 * most * rank, most * rank), F32),
            pltpu.VMEM((rank, devices), jnp.int32),
            pltpu.VMEM((rank, rank, devices), BF16),
            pltpu.VMEM((1, rank, rank), BF16),
            pltpu.VMEM((rank * nodes, rank), F32),
            pltpu.SemaphoreType.DMA((3,)),
        ],
        specs=[memory] + [far_away] * 3,
        flops=2e9,
        name="prep",
    )(me, upper_pick.T, upper_transfer.transpose(1, 2, 0), local_transfer)

    def leaf_part(first, count, earlier):
        return call(
            functools.partial(leaf_body, first, count, rank),
            (shape((cols, items // leaves * count), F32), shape((count * rank, width), BF16)),
            flops=2e9,
            name="leaf",
        )(after((order,), earlier)[0], embeddings, rhs_tree, leaf_skel)

    lead = leaves * 3 // 4
    parts = [leaf_part(0, lead, payload)]
    base = 1
    for stage, (n, depth) in enumerate(zip(radices, depths)):
        stride = 1 << base
        groups = [
            [high * stride * n + low + stride * j for j in range(n)]
            for high in range(devices // (stride * n))
            for low in range(stride)
        ]
        gathered = lax.all_to_all(payload, "leaf", 0, 0, axis_index_groups=groups)
        base += depth
        if stage == 1:
            parts.append(leaf_part(lead, leaves - lead, payload))
            far = call(
                functools.partial(far_body, leaves, len(parts), rank, cols),
                shape((leaves * rank, 128), F32),
                flops=1e9,
                name="far",
            )(local_pick, weights, local_transfer, *[part[1] for part in parts])
            if stage + 1 < stages:
                gathered, far = lax.optimization_barrier((gathered, far))
        elif stage + 1 < stages:
            gathered, parts[-1] = lax.optimization_barrier((gathered, parts[-1]))
        if stage + 1 < stages:
            payload, pairs, siblings = call(
                functools.partial(hop_body, stage, depth, rank, cols),
                (
                    shape((radices[stage + 1], sent, width), BF16),
                    shape((2 * depth * rank, width), BF16),
                    shape((depth * rank, cols), F32),
                ),
                name="hop",
            )(gathered, selects, lifts)
            held += [pairs, siblings]
    chains_last, far = after((chains, far), payload)
    spread = call(
        functools.partial(spread_body, len(parts), items // leaves, rank),
        shape((256, items), BF16),
        scratch=[
            pltpu.VMEM((256, items), BF16),
            pltpu.VMEM((items, items // leaves), BF16),
            pltpu.VMEM((items, items // leaves), BF16),
        ],
        flops=2e9,
        name="spread",
    )(order, basis_t, far, *[part[0] for part in parts])
    field = call(functools.partial(terms_body, depths[:-1], rank), shape((rank, cols), F32), name="terms")(chains_last, *held)
    product = call(
        functools.partial(final_body, stages - 1, depths[-1], rank, cols), shape((cols, items), BF16), name="final"
    )(gathered, selects, lifts, chains, field, spread)
    return product.T


def solution(mesh):
    return jax.shard_map(
        local,
        mesh=mesh,
        in_specs=(
            P("leaf", None),
            P("leaf", None),
            P("leaf"),
            P("leaf", None),
            P("leaf", None),
            P("leaf", None, None),
            P("leaf", None),
            P(),
            P(),
        ),
        out_specs=P("leaf", None),
        check_vma=False,
    )
```

time: 77.4 us -> 60.6 us (0.78)
  the two profiles are of different devices: /device:TPU:16 before, /device:TPU:8 now
where the time goes in v2:
time: 60.6 us; the launch traced here: 60 us
  Pallas kernels  25.3 us (42%)
  starting transfers between devices  24.3 us (40%)
  waiting for transfers between devices  8.21 us (14%)
  local copies, waits for them, and re-layouts  2.02 us (3%)
    all_to_all x3, starting transfers between devices, local(): gathered = lax.all_to_all(payload, 'leaf', 0, 0, axis_index_groups=groups)  22.3 us
    all_to_all x3, waiting for transfers between devices, local(): gathered = lax.all_to_all(payload, 'leaf', 0, 0, axis_index_groups=groups)  7.79 us
    pallas_call x2, Pallas kernels, leaf_part(): call(functools.partial(leaf_body, first, count, rank), (shape((cols, item...  7.77 us
    pallas_call x1, Pallas kernels, local(): call(functools.partial(pre_body, leaves), (shape((rank, width + 2 * cols)...  5.75 us
    pallas_call x1, Pallas kernels, local(): call(functools.partial(spread_body, len(parts), items // leaves, rank), s...  2.75 us
    pallas_call x1, Pallas kernels, local(): call(functools.partial(prep_body, devices, radices), (shape((stages, (2 *...  2.15 us
    ppermute x1, starting transfers between devices, local(): other = lax.ppermute(payload, 'leaf', [(i, i ^ 1) for i in range(devices)])  2.05 us
    unnamed x24, local copies, waits for them, and re-layouts  2.02 us
  transfers between devices with their start and end apart: 4, of which 3 were waited for; matrix products, arithmetic and copies ran while one was open for 0% of the time, Pallas kernels for 25%

profile of v2, /device:TPU:8, one launch (start us, length us, event | category | flops | bytes accessed | tf_op | source)
XLA Modules:
  0.0 60.0 jit_solution(13089404504302431765)
XLA Ops:
  0.0 0.0 copy-start.10
  0.0 5.8 %pre.1 = (bf16[32,384]{1,0:T(8,128)(2,1)}, bf16[64,2048]{1,0:T(8,128)(2,1)}, f32[256,64]{1,0:T(8,128)}) custom-call(s32[16,128]{1,0:T(8,128)} %bitcast.9, s32[8,32]{1,0:T(8,128)} %skel.3, s32[7,32]{1,0:T(8,128)} %pick.1, bf16[64,2048]{1,0:T(8,128)(2,1)} %bitcast.16, bf16[32,2048]{1,0:T(8,128)(2,1)} %bitcast.7, bf16[15,32,32]{2,1,0:T(8,128)(2,1)} %transfer.1, ...), custom_call_target="tpu_custom_call" | custom-call | flops 100000000 | bytes 1048576 | tf_op jit(solution)/shard_map/pre/pallas_call | solution.py:499
  5.8 0.0 copy-start
  5.8 2.1 %collective-permute-start = (bf16[32,384]{1,0:T(8,128)(2,1)}, bf16[32,384]{1,0:T(8,128)(2,1)S(1)}, u32[]{:S(2)}, u32[]{:S(2)}) collective-permute-start(bf16[32,384]{1,0:T(8,128)(2,1)} %get-tuple-element.36.mine), channel_id=1, source_target_pairs={{0,1},{1,0},{2,3},{3,2},{4,5},{5,4},{6,7},{7,6},{8,9},{9,8},{10,11... | collective-permute-start | bytes 73736 | tf_op jit(solution)/shard_map/ppermute | solution.py:511
  7.8 0.0 copy-done.10
  7.9 0.0 copy-start.11
  7.9 0.7 %copy-done.11 = bf16[32,384]{1,0:T(8,128)(2,1)S(1)} copy-done((bf16[32,384]{1,0:T(8,128)(2,1)S(1)}, bf16[32,384]{1,0:T(8,128)(2,1)}, u32[]{:S(2)}) %copy-start.11) | copy-done | bytes 24600
  8.6 0.2 side.1
  8.8 0.4 collective-permute-done.other
  9.2 0.8 %pair.1 = (bf16[8,40,256]{2,1,0:T(8,128)(2,1)}, bf16[64,256]{1,0:T(8,128)(2,1)S(1)}, f32[32,64]{1,0:T(8,128)S(1)}) custom-call(bf16[32,64]{1,0:T(8,128)(2,1)S(1)} %get-tuple-element.37.hot, bf16[32,384]{1,0:T(8,128)(2,1)S(1)} %get-tuple-element.38.mine, bf16[32,384]{1,0:T(8,128)(2,1)S(1)} %collective-permute-done.other), custom_call_target="tpu_custom_call" | custom-call | flops 100000000 | bytes 1048576 | tf_op jit(solution)/shard_map/pair/pallas_call | solution.py:521
  10.0 0.0 copy-start.3
  10.0 0.0 copy-start.4
  10.0 9.2 %all-to-all-start = ((bf16[8,40,256]{2,1,0:T(8,128)(2,1)}), bf16[8,40,256]{2,1,0:T(8,128)(2,1)S(1)}, u32[]{:S(2)}, u32[]{:S(2)}) async-start(bf16[8,40,256]{2,1,0:T(8,128)(2,1)} %get-tuple-element.39), calls=%async_computation | async-start | bytes 327680 | tf_op jit(solution)/shard_map/all_to_all | solution.py:577
  19.3 0.0 copy-done
  19.3 0.0 copy-done.3
  19.3 0.0 copy-done.4
  19.3 0.0 copy-start.7
  19.3 0.9 %copy-done.7 = bf16[64,2048]{1,0:T(8,128)(2,1)S(1)} copy-done((bf16[64,2048]{1,0:T(8,128)(2,1)S(1)}, bf16[64,2048]{1,0:T(8,128)(2,1)}, u32[]{:S(2)}) %copy-start.7) | copy-done | bytes 262168
  20.2 0.0 copy-start.2
  20.2 0.0 copy-start.6
  20.2 5.8 %leaf.2 = (f32[64,1536]{1,0:T(8,128)S(1)}, bf16[192,256]{1,0:T(8,128)(2,1)S(1)}) custom-call(s32[16,128]{1,0:T(8,128)S(1)} %bitcast.10, bf16[2048,256]{1,0:T(8,128)(2,1)S(1)} %copy-done, bf16[64,2048]{1,0:T(8,128)(2,1)S(1)} %copy-done.7, s32[8,32]{1,0:T(8,128)S(1)} %copy-done.4), custom_call_target="tpu_custom_call" | custom-call | flops 2000000000 | bytes 1048576 | tf_op jit(solution)/shard_map/leaf/pallas_call | solution.py:560
  26.0 0.0 copy-done.2
  26.0 0.0 copy-done.6
  26.0 2.2 %prep.1 = (bf16[3,224,256]{2,1,0:T(8,128)(2,1)S(1)}, bf16[3,2,128,256]{3,2,1,0:T(8,128)(2,1)S(1)}, f32[3,96,32]{2,1,0:T(8,128)S(1)}) custom-call(s32[1]{0:T(128)} %bitcast.me_ref, s32[32,512]{1,0:T(8,128)S(1)} %bitcast.15, bf16[32,32,512]{2,1,0:T(8,128)(2,1)S(1)} %bitcast.13, bf16[15,32,32]{2,1,0:T(8,128)(2,1)S(1)} %copy-done.2), custom_call_target="tpu_custom_call" | custom-call | flops 2000000000 | bytes 1048576 | tf_op jit(solution)/shard_map/prep/pallas_call | solution.py:538
  28.2 0.0 all-to-all-done.gathered
  28.2 0.0 copy-start.8
  28.2 1.0 %hop.2 = (bf16[4,40,256]{2,1,0:T(8,128)(2,1)}, bf16[192,256]{1,0:T(8,128)(2,1)S(1)}, f32[96,64]{1,0:T(8,128)S(1)}) custom-call(bf16[8,40,256]{2,1,0:T(8,128)(2,1)S(1)} %all-to-all-done.gathered, bf16[3,224,256]{2,1,0:T(8,128)(2,1)S(1)} %get-tuple-element.46.selects, bf16[3,2,128,256]{3,2,1,0:T(8,128)(2,1)S(1)} %get-tuple-element.47.lifts), custom_call_target="tpu_custom_call" | custom-call | flops 100000000 | bytes 1048576 | tf_op jit(solution)/shard_map/hop/pallas_call | solution.py:592
  29.2 3.3 %all-to-all-start.1 = ((bf16[4,40,256]{2,1,0:T(8,128)(2,1)}), bf16[4,40,256]{2,1,0:T(8,128)(2,1)S(1)}, u32[]{:S(2)}, u32[]{:S(2)}) async-start(bf16[4,40,256]{2,1,0:T(8,128)(2,1)} %get-tuple-element.48), calls=%async_computation.1 | async-start | bytes 163840 | tf_op jit(solution)/shard_map/all_to_all | solution.py:577
  32.5 0.0 copy-done.8
  32.5 0.0 copy-start.5
  32.5 0.0 copy-start.9
  32.5 2.0 %leaf.3 = (f32[64,512]{1,0:T(8,128)S(1)}, bf16[64,256]{1,0:T(8,128)(2,1)S(1)}) custom-call(s32[16,128]{1,0:T(8,128)S(1)} %bitcast.11, bf16[2048,256]{1,0:T(8,128)(2,1)S(1)} %copy-done, bf16[64,2048]{1,0:T(8,128)(2,1)S(1)} %copy-done.8, s32[8,32]{1,0:T(8,128)S(1)} %copy-done.4), custom_call_target="tpu_custom_call" | custom-call | flops 2000000000 | bytes 1048576 | tf_op jit(solution)/shard_map/leaf/pallas_call | solution.py:560
  34.5 0.0 copy-done.5
  34.6 0.0 copy-done.9
  34.6 1.6 %far.1 = f32[256,128]{1,0:T(8,128)S(1)} custom-call(s32[7,32]{1,0:T(8,128)S(1)} %copy-done.5, f32[256,64]{1,0:T(8,128)S(1)} %copy-done.9, bf16[15,32,32]{2,1,0:T(8,128)(2,1)S(1)} %copy-done.2, bf16[192,256]{1,0:T(8,128)(2,1)S(1)} %get-tuple-element.50.refs_0_, bf16[64,256]{1,0:T(8,128)(2,1)S(1)} %get-tuple-element.52.refs_1_), custom_call_target="tpu_custom_call" | custom-call | flops 1000000000 | bytes 1048576 | tf_op jit(solution)/shard_map/far/pallas_call | solution.py:581
  36.2 2.0 %all-to-all-done.1.gathered = bf16[4,40,256]{2,1,0:T(8,128)(2,1)S(1)} async-done(((bf16[4,40,256]{2,1,0:T(8,128)(2,1)}), bf16[4,40,256]{2,1,0:T(8,128)(2,1)S(1)}, u32[]{:S(2)}, u32[]{:S(2)}) %all-to-all-start.1) | async-done | bytes 81952 | tf_op jit(solution)/shard_map/all_to_all | solution.py:577
  38.2 1.0 %hop.3 = (bf16[8,40,256]{2,1,0:T(8,128)(2,1)}, bf16[128,256]{1,0:T(8,128)(2,1)S(1)}, f32[64,64]{1,0:T(8,128)S(1)}) custom-call(bf16[4,40,256]{2,1,0:T(8,128)(2,1)S(1)} %all-to-all-done.1.gathered, bf16[3,224,256]{2,1,0:T(8,128)(2,1)S(1)} %get-tuple-element.46.selects, bf16[3,2,128,256]{3,2,1,0:T(8,128)(2,1)S(1)} %get-tuple-element.47.lifts), custom_call_target="tpu_custom_call" | custom-call | flops 100000000 | bytes 1048576 | tf_op jit(solution)/shard_map/hop/pallas_call | solution.py:592
  39.1 9.8 %all-to-all-start.2 = ((bf16[8,40,256]{2,1,0:T(8,128)(2,1)}), bf16[8,40,256]{2,1,0:T(8,128)(2,1)S(1)}, u32[]{:S(2)}, u32[]{:S(2)}) async-start(bf16[8,40,256]{2,1,0:T(8,128)(2,1)} %get-tuple-element.54), calls=%async_computation.2 | async-start | bytes 327680 | tf_op jit(solution)/shard_map/all_to_all | solution.py:577
  48.9 0.0 copy-start.1
  48.9 0.6 %terms.1.before = f32[32,64]{1,0:T(8,128)S(1)} custom-call(f32[3,96,32]{2,1,0:T(8,128)S(1)} %get-tuple-element.57.chains, bf16[64,256]{1,0:T(8,128)(2,1)S(1)} %get-tuple-element.58.refs_0_, f32[32,64]{1,0:T(8,128)S(1)} %get-tuple-element.59.refs_1_, bf16[192,256]{1,0:T(8,128)(2,1)S(1)} %get-tuple-element.60.refs_2_, f32[96,64]{1,0:T(8,128)S(1)} %get-tuple-element.61.refs_3_, ...), custom_call_target="tpu_custom_call" | custom-call | flops 100000000 | bytes 1048576 | tf_op jit(solution)/shard_map/terms/pallas_call | solution.py:614
  49.5 0.3 copy-done.1
  49.8 2.8 %spread.1 = bf16[256,2048]{1,0:T(8,128)(2,1)S(1)} custom-call(s32[16,128]{1,0:T(8,128)S(1)} %bitcast.12, bf16[32,2048]{1,0:T(8,128)(2,1)S(1)} %bitcast.8, f32[256,128]{1,0:T(8,128)S(1)} %far.1, f32[64,1536]{1,0:T(8,128)S(1)} %get-tuple-element.65.refs_0_, f32[64,512]{1,0:T(8,128)S(1)} %get-tuple-element.66.refs_1_), custom_call_target="tpu_custom_call" | custom-call | flops 2000000000 | bytes 1048576 | tf_op jit(solution)/shard_map/spread/pallas_call | solution.py:603
  52.6 5.8 %all-to-all-done.2.gathered = bf16[8,40,256]{2,1,0:T(8,128)(2,1)S(1)} async-done(((bf16[8,40,256]{2,1,0:T(8,128)(2,1)}), bf16[8,40,256]{2,1,0:T(8,128)(2,1)S(1)}, u32[]{:S(2)}, u32[]{:S(2)}) %all-to-all-start.2) | async-done | bytes 163872 | tf_op jit(solution)/shard_map/all_to_all | solution.py:577
  58.3 1.7 %final.1 = bf16[64,2048]{1,0:T(8,128)(2,1)} custom-call(bf16[8,40,256]{2,1,0:T(8,128)(2,1)S(1)} %all-to-all-done.2.gathered, bf16[3,224,256]{2,1,0:T(8,128)(2,1)S(1)} %get-tuple-element.46.selects, bf16[3,2,128,256]{3,2,1,0:T(8,128)(2,1)S(1)} %get-tuple-element.47.lifts, f32[3,96,32]{2,1,0:T(8,128)S(1)} %get-tuple-element.57.chains, ...), custom_call_target="tpu_custom_call" | custom-call | flops 100000000 | bytes 1048576 | tf_op jit(solution)/shard_map/final/pallas_call | solution.py:615
Async XLA Ops:
  0.0 7.8 %copy-start.10 = (s32[512,32]{0,1:T(8,128)S(1)}, s32[512,32]{0,1:T(8,128)}, u32[]{:S(2)}) copy-start(s32[512,32]{0,1:T(8,128)} %param.17) | copy-start | bytes 196612
  5.8 13.5 %copy-start = (bf16[2048,256]{1,0:T(8,128)(2,1)S(1)}, bf16[2048,256]{1,0:T(8,128)(2,1)}, u32[]{:S(2)}) copy-start(bf16[2048,256]{1,0:T(8,128)(2,1)} %emb.3) | copy-start | bytes 3145732
  5.8 3.4 %collective-permute-start = (bf16[32,384]{1,0:T(8,128)(2,1)}, bf16[32,384]{1,0:T(8,128)(2,1)S(1)}, u32[]{:S(2)}, u32[]{:S(2)}) collective-permute-start(bf16[32,384]{1,0:T(8,128)(2,1)} %get-tuple-element.36.mine), channel_id=1, source_target_pairs={{0,1},{1,0},{2,3},{3,2},{4,5},{5,4},{6,7},{7,6},{8,9},{9,8},{10,11... | collective-permute-start | bytes 73736 | tf_op jit(solution)/shard_map/ppermute | solution.py:511
  7.9 0.7 %copy-start.11 = (bf16[32,384]{1,0:T(8,128)(2,1)S(1)}, bf16[32,384]{1,0:T(8,128)(2,1)}, u32[]{:S(2)}) copy-start(bf16[32,384]{1,0:T(8,128)(2,1)} %get-tuple-element.36.mine) | copy-start | bytes 73732
  10.0 9.2 %copy-start.3 = (s32[2048]{0:T(1024)S(1)}, s32[2048]{0:T(1024)}, u32[]{:S(2)}) copy-start(s32[2048]{0:T(1024)} %param.11) | copy-start | bytes 24580
  10.0 9.2 %copy-start.4 = (s32[8,32]{1,0:T(8,128)S(1)}, s32[8,32]{1,0:T(8,128)}, u32[]{:S(2)}) copy-start(s32[8,32]{1,0:T(8,128)} %skel.3) | copy-start | bytes 3076
  10.0 18.2 %all-to-all-start = ((bf16[8,40,256]{2,1,0:T(8,128)(2,1)}), bf16[8,40,256]{2,1,0:T(8,128)(2,1)S(1)}, u32[]{:S(2)}, u32[]{:S(2)}) async-start(bf16[8,40,256]{2,1,0:T(8,128)(2,1)} %get-tuple-element.39), calls=%async_computation | async-start | bytes 327680 | tf_op jit(solution)/shard_map/all_to_all | solution.py:577
  19.3 1.0 %copy-start.7 = (bf16[64,2048]{1,0:T(8,128)(2,1)S(1)}, bf16[64,2048]{1,0:T(8,128)(2,1)}, u32[]{:S(2)}) copy-start(bf16[64,2048]{1,0:T(8,128)(2,1)} %get-tuple-element.41.rhs_tree) | copy-start | bytes 786436
  20.2 5.8 %copy-start.2 = (bf16[15,32,32]{2,1,0:T(8,128)(2,1)S(1)}, bf16[15,32,32]{2,1,0:T(8,128)(2,1)}, u32[]{:S(2)}) copy-start(bf16[15,32,32]{2,1,0:T(8,128)(2,1)} %transfer.1) | copy-start | bytes 92164
  20.2 5.8 %copy-start.6 = (bf16[512,32,32]{0,2,1:T(8,128)(2,1)S(1)}, bf16[512,32,32]{0,2,1:T(8,128)(2,1)}, u32[]{:S(2)}) copy-start(bf16[512,32,32]{0,2,1:T(8,128)(2,1)} %param.16) | copy-start | bytes 3145732
  28.2 4.3 %copy-start.8 = (bf16[64,2048]{1,0:T(8,128)(2,1)S(1)}, bf16[64,2048]{1,0:T(8,128)(2,1)}, u32[]{:S(2)}) copy-start(bf16[64,2048]{1,0:T(8,128)(2,1)} %get-tuple-element.41.rhs_tree) | copy-start | bytes 786436
  29.2 9.0 %all-to-all-start.1 = ((bf16[4,40,256]{2,1,0:T(8,128)(2,1)}), bf16[4,40,256]{2,1,0:T(8,128)(2,1)S(1)}, u32[]{:S(2)}, u32[]{:S(2)}) async-start(bf16[4,40,256]{2,1,0:T(8,128)(2,1)} %get-tuple-element.48), calls=%async_computation.1 | async-start | bytes 163840 | tf_op jit(solution)/shard_map/all_to_all | solution.py:577
  32.5 2.0 %copy-start.5 = (s32[7,32]{1,0:T(8,128)S(1)}, s32[7,32]{1,0:T(8,128)}, u32[]{:S(2)}) copy-start(s32[7,32]{1,0:T(8,128)} %pick.1) | copy-start | bytes 2692
  32.5 2.0 %copy-start.9 = (f32[256,64]{1,0:T(8,128)S(1)}, f32[256,64]{1,0:T(8,128)}, u32[]{:S(2)}) copy-start(f32[256,64]{1,0:T(8,128)} %get-tuple-element.49.weights) | copy-start | bytes 196612
  39.1 19.2 %all-to-all-start.2 = ((bf16[8,40,256]{2,1,0:T(8,128)(2,1)}), bf16[8,40,256]{2,1,0:T(8,128)(2,1)S(1)}, u32[]{:S(2)}, u32[]{:S(2)}) async-start(bf16[8,40,256]{2,1,0:T(8,128)(2,1)} %get-tuple-element.54), calls=%async_computation.2 | async-start | bytes 327680 | tf_op jit(solution)/shard_map/all_to_all | solution.py:577
  48.9 0.9 %copy-start.1 = (bf16[2048,32]{0,1:T(8,128)(2,1)S(1)}, bf16[2048,32]{0,1:T(8,128)(2,1)}, u32[]{:S(2)}) copy-start(bf16[2048,32]{0,1:T(8,128)(2,1)} %param.12) | copy-start | bytes 393220

commit v3 on v2

--- a/solution.py
+++ b/solution.py
@@ -143,19 +143,12 @@
     leaf = items // leaves
     rank = skel.shape[1]
     blocks = items // leaf
-    for copy in copies[:3]:
+    for copy in copies[:6]:
         copy.wait()
     table = padded_columns([skel[...], pick[...]], 16)
-    nodes = skeleton_ids(leaves, leaf, order, table, rank)
-    parents = leaves // 2
-    while parents:
-        nodes = picked_of(nodes, parents, table, leaves, rank)
-        parents //= 2
-    for copy in copies[3:6]:
-        copy.wait()
     joined = jnp.concatenate([rhs[:, b * leaf : (b + 1) * leaf] for b in range(blocks)], axis=0)
-    level = []
-    for l in range(leaves):
+
+    def gather(l):
         row = order_row(order, l)
         low, high = row & (leaf - 1), row // leaf
         found = dot(joined, one_hot(low == iota((leaf, leaf), 0)))
@@ -165,21 +158,38 @@
             total = part if total is None else total + part
         picked = total.astype(BF16)
         rhs_tree[:, l * leaf : (l + 1) * leaf] = picked
-        level.append(dot_last(basis[:, l * leaf : (l + 1) * leaf], picked))
-    chain = [transfer[1].astype(F32), transfer[2].astype(F32)]
-    count = 4
-    while count <= leaves:
-        chain = [dot_right(transfer[count + n - 1], chain[n // 2]) for n in range(count)]
-        count *= 2
-    chain = jnp.concatenate(chain, axis=0)
-    high, low = split(chain)
-    chain = jnp.concatenate([chain, dot(high, transfer[0]) + dot(low, transfer[0])], axis=1)
-    level = jnp.concatenate(level, axis=0)
-    weights[...] = level
-    top = dot_first_wide(chain, level)
-    copies[6].wait()
-    nodes = items_of(nodes, leaf, emb)
-    payload[...] = jnp.concatenate([nodes, top[:rank, :].astype(BF16), top[rank:, :].astype(BF16)], axis=1)
+        lifted = dot_last(basis[:, l * leaf : (l + 1) * leaf], picked)
+        weights[l * rank : (l + 1) * rank, :] = lifted
+        return lifted
+
+    def lift(q, left, right):
+        pair = jnp.concatenate([left, right], axis=0)
+        return dot_first_right(transfer[2 * q - 1 : 2 * q + 1].reshape(2 * rank, rank), pair)
+
+    nodes, parents, pending = None, leaves, {}
+    for l in range(leaves):
+        node, q = gather(l), leaves + l
+        if l == 1:
+            copies[6].wait()
+        if l == leaves - 1:
+            nodes = items_of(nodes, leaf, emb)
+        while q % 2:
+            node = lift(q // 2, pending.pop(q - 1), node)
+            q //= 2
+            if q == 1:
+                break
+        pending[q] = node
+        if nodes is None:
+            nodes = skeleton_ids(leaves, leaf, order, table, rank)
+        elif parents > 1:
+            parents //= 2
+            nodes = picked_of(nodes, parents, table, leaves, rank)
+    while parents > 1:
+        parents //= 2
+        nodes = picked_of(nodes, parents, table, leaves, rank)
+    own = pending[1]
+    share = dot_first_right(transfer[0], own)
+    payload[...] = jnp.concatenate([nodes, own.astype(BF16), share.astype(BF16)], axis=1)
 
 
 def packed(weights, width):
@@ -564,8 +574,8 @@
             name="leaf",
         )(after((order,), earlier)[0], embeddings, rhs_tree, leaf_skel)
 
-    lead = leaves * 3 // 4
-    parts = [leaf_part(0, lead, payload)]
+    lead = leaves // 2
+    parts = [leaf_part(0, lead, chains)]
     base = 1
     for stage, (n, depth) in enumerate(zip(radices, depths)):
         stride = 1 << base
@@ -578,16 +588,9 @@
         base += depth
         if stage == 1:
             parts.append(leaf_part(lead, leaves - lead, payload))
-            far = call(
-                functools.partial(far_body, leaves, len(parts), rank, cols),
-                shape((leaves * rank, 128), F32),
-                flops=1e9,
-                name="far",
-            )(local_pick, weights, local_transfer, *[part[1] for part in parts])
-            if stage + 1 < stages:
-                gathered, far = lax.optimization_barrier((gathered, far))
-        elif stage + 1 < stages:
-            gathered, parts[-1] = lax.optimization_barrier((gathered, parts[-1]))
+        if stage + 1 < stages:
+            gathered, *held_points = lax.optimization_barrier((gathered, *parts[-1]))
+            parts[-1] = held_points
         if stage + 1 < stages:
             payload, pairs, siblings = call(
                 functools.partial(hop_body, stage, depth, rank, cols),
@@ -599,7 +602,13 @@
                 name="hop",
             )(gathered, selects, lifts)
             held += [pairs, siblings]
-    chains_last, far = after((chains, far), payload)
+    chains_last, far_weights = after((chains, weights), payload)
+    far = call(
+        functools.partial(far_body, leaves, len(parts), rank, cols),
+        shape((leaves * rank, 128), F32),
+        flops=1e9,
+        name="far",
+    )(local_pick, far_weights, local_transfer, *[part[1] for part in parts])
     spread = call(
         functools.partial(spread_body, len(parts), items // leaves, rank),
         shape((256, items), BF16),

time: 60.6 us -> 59.3 us (0.979)
  the two profiles are of different devices: /device:TPU:8 before, /device:TPU:2 now
where the time goes in v3:
time: 59.3 us; the launch traced here: 58.7 us
  Pallas kernels  24.8 us (42%)
  starting transfers between devices  24.3 us (41%)
  waiting for transfers between devices  7.21 us (12%)
  local copies, waits for them, and re-layouts  2.27 us (4%)
    all_to_all x3, starting transfers between devices, local(): gathered = lax.all_to_all(payload, 'leaf', 0, 0, axis_index_groups=groups)  22.4 us
    pallas_call x2, Pallas kernels, leaf_part(): call(functools.partial(leaf_body, first, count, rank), (shape((cols, item...  8.24 us
    all_to_all x3, waiting for transfers between devices, local(): gathered = lax.all_to_all(payload, 'leaf', 0, 0, axis_index_groups=groups)  6.8 us
    pallas_call x1, Pallas kernels, local(): call(functools.partial(pre_body, leaves), (shape((rank, width + 2 * cols)...  4.81 us
    pallas_call x1, Pallas kernels, local(): call(functools.partial(spread_body, len(parts), items // leaves, rank), s...  2.74 us
    unnamed x22, local copies, waits for them, and re-layouts  2.27 us
    pallas_call x1, Pallas kernels, local(): call(functools.partial(prep_body, devices, radices), (shape((stages, (2 *...  2.15 us
    pallas_call x2, Pallas kernels, local(): call(functools.partial(hop_body, stage, depth, rank, cols), (shape((radic...  1.96 us
  transfers between devices with their start and end apart: 4, of which 4 were waited for; matrix products, arithmetic and copies ran while one was open for 0% of the time, Pallas kernels for 27%

profile of v3, /device:TPU:2, one launch (start us, length us, event | category | flops | bytes accessed | tf_op | source)
XLA Modules:
  0.0 58.7 jit_solution(7827277236593322973)
XLA Ops:
  0.0 0.0 copy-start.9
  0.0 4.8 %pre.1 = (bf16[32,384]{1,0:T(8,128)(2,1)}, bf16[64,2048]{1,0:T(8,128)(2,1)}, f32[256,64]{1,0:T(8,128)}) custom-call(s32[16,128]{1,0:T(8,128)} %bitcast.9, s32[8,32]{1,0:T(8,128)} %skel.3, s32[7,32]{1,0:T(8,128)} %pick.1, bf16[64,2048]{1,0:T(8,128)(2,1)} %bitcast.16, bf16[32,2048]{1,0:T(8,128)(2,1)} %bitcast.7, bf16[15,32,32]{2,1,0:T(8,128)(2,1)} %transfer.1, ...), custom_call_target="tpu_custom_call" | custom-call | flops 100000000 | bytes 1048576 | tf_op jit(solution)/shard_map/pre/pallas_call | solution.py:509
  4.8 1.9 %collective-permute-start = (bf16[32,384]{1,0:T(8,128)(2,1)}, bf16[32,384]{1,0:T(8,128)(2,1)S(1)}, u32[]{:S(2)}, u32[]{:S(2)}) collective-permute-start(bf16[32,384]{1,0:T(8,128)(2,1)} %get-tuple-element.37.mine), channel_id=1, source_target_pairs={{0,1},{1,0},{2,3},{3,2},{4,5},{5,4},{6,7},{7,6},{8,9},{9,8},{10,11... | collective-permute-start | bytes 73736 | tf_op jit(solution)/shard_map/ppermute | solution.py:521
  6.7 0.0 copy-done.9
  6.8 0.0 copy-start.10
  6.8 0.7 %copy-done.10 = bf16[32,384]{1,0:T(8,128)(2,1)S(1)} copy-done((bf16[32,384]{1,0:T(8,128)(2,1)S(1)}, bf16[32,384]{1,0:T(8,128)(2,1)}, u32[]{:S(2)}) %copy-start.10) | copy-done | bytes 24600
  7.5 0.2 side.1
  7.7 0.4 collective-permute-done.other
  8.1 0.8 %pair.1 = (bf16[8,40,256]{2,1,0:T(8,128)(2,1)}, bf16[64,256]{1,0:T(8,128)(2,1)S(1)}, f32[32,64]{1,0:T(8,128)S(1)}) custom-call(bf16[32,64]{1,0:T(8,128)(2,1)S(1)} %get-tuple-element.38.hot, bf16[32,384]{1,0:T(8,128)(2,1)S(1)} %get-tuple-element.39.mine, bf16[32,384]{1,0:T(8,128)(2,1)S(1)} %collective-permute-done.other), custom_call_target="tpu_custom_call" | custom-call | flops 100000000 | bytes 1048576 | tf_op jit(solution)/shard_map/pair/pallas_call | solution.py:531
  8.9 0.0 copy-start.2
  8.9 7.2 %all-to-all-start = ((bf16[8,40,256]{2,1,0:T(8,128)(2,1)}), bf16[8,40,256]{2,1,0:T(8,128)(2,1)S(1)}, u32[]{:S(2)}, u32[]{:S(2)}) async-start(bf16[8,40,256]{2,1,0:T(8,128)(2,1)} %get-tuple-element.40), calls=%async_computation | async-start | bytes 327680 | tf_op jit(solution)/shard_map/all_to_all | solution.py:587
  16.1 0.0 copy-done.2
  16.1 0.0 copy-start.6
  16.2 1.2 %copy-done.6 = bf16[512,32,32]{0,2,1:T(8,128)(2,1)S(1)} copy-done((bf16[512,32,32]{0,2,1:T(8,128)(2,1)S(1)}, bf16[512,32,32]{0,2,1:T(8,128)(2,1)}, u32[]{:S(2)}) %copy-start.6) | copy-done | bytes 1048600
  17.4 0.0 copy-start
  17.4 0.0 copy-start.3
  17.4 0.0 copy-start.4
  17.4 0.0 copy-start.7
  17.4 2.1 %prep.1 = (bf16[3,224,256]{2,1,0:T(8,128)(2,1)S(1)}, bf16[3,2,128,256]{3,2,1,0:T(8,128)(2,1)S(1)}, f32[3,96,32]{2,1,0:T(8,128)S(1)}) custom-call(s32[1]{0:T(128)} %bitcast.me_ref, s32[32,512]{1,0:T(8,128)S(1)} %bitcast.15, bf16[32,32,512]{2,1,0:T(8,128)(2,1)S(1)} %bitcast.13, bf16[15,32,32]{2,1,0:T(8,128)(2,1)S(1)} %copy-done.2), custom_call_target="tpu_custom_call" | custom-call | flops 2000000000 | bytes 1048576 | tf_op jit(solution)/shard_map/prep/pallas_call | solution.py:548
  19.5 0.0 copy-done
  19.6 0.0 copy-done.3
  19.6 0.0 copy-done.4
  19.6 0.0 copy-done.7
  19.6 4.1 %leaf.2 = (f32[64,1024]{1,0:T(8,128)S(1)}, bf16[128,256]{1,0:T(8,128)(2,1)S(1)}) custom-call(s32[16,128]{1,0:T(8,128)S(1)} %bitcast.10, bf16[2048,256]{1,0:T(8,128)(2,1)S(1)} %copy-done, bf16[64,2048]{1,0:T(8,128)(2,1)S(1)} %copy-done.7, s32[8,32]{1,0:T(8,128)S(1)} %copy-done.4), custom_call_target="tpu_custom_call" | custom-call | flops 2000000000 | bytes 1048576 | tf_op jit(solution)/shard_map/leaf/pallas_call | solution.py:570
  23.7 2.5 %all-to-all-done.gathered = bf16[8,40,256]{2,1,0:T(8,128)(2,1)S(1)} async-done(((bf16[8,40,256]{2,1,0:T(8,128)(2,1)}), bf16[8,40,256]{2,1,0:T(8,128)(2,1)S(1)}, u32[]{:S(2)}, u32[]{:S(2)}) %all-to-all-start) | async-done | bytes 163872 | tf_op jit(solution)/shard_map/all_to_all | solution.py:587
  26.2 1.0 %hop.2 = (bf16[4,40,256]{2,1,0:T(8,128)(2,1)}, bf16[192,256]{1,0:T(8,128)(2,1)S(1)}, f32[96,64]{1,0:T(8,128)S(1)}) custom-call(bf16[8,40,256]{2,1,0:T(8,128)(2,1)S(1)} %all-to-all-done.gathered, bf16[3,224,256]{2,1,0:T(8,128)(2,1)S(1)} %get-tuple-element.48.selects, bf16[3,2,128,256]{3,2,1,0:T(8,128)(2,1)S(1)} %get-tuple-element.49.lifts), custom_call_target="tpu_custom_call" | custom-call | flops 100000000 | bytes 1048576 | tf_op jit(solution)/shard_map/hop/pallas_call | solution.py:595
  27.2 5.6 %all-to-all-start.1 = ((bf16[4,40,256]{2,1,0:T(8,128)(2,1)}), bf16[4,40,256]{2,1,0:T(8,128)(2,1)S(1)}, u32[]{:S(2)}, u32[]{:S(2)}) async-start(bf16[4,40,256]{2,1,0:T(8,128)(2,1)} %get-tuple-element.50), calls=%async_computation.1 | async-start | bytes 163840 | tf_op jit(solution)/shard_map/all_to_all | solution.py:587
  32.9 4.1 %leaf.3 = (f32[64,1024]{1,0:T(8,128)S(1)}, bf16[128,256]{1,0:T(8,128)(2,1)S(1)}) custom-call(s32[16,128]{1,0:T(8,128)S(1)} %bitcast.11, bf16[2048,256]{1,0:T(8,128)(2,1)S(1)} %copy-done, bf16[64,2048]{1,0:T(8,128)(2,1)S(1)} %copy-done.7, s32[8,32]{1,0:T(8,128)S(1)} %copy-done.4), custom_call_target="tpu_custom_call" | custom-call | flops 2000000000 | bytes 1048576 | tf_op jit(solution)/shard_map/leaf/pallas_call | solution.py:570
  37.0 0.1 all-to-all-done.1.gathered
  37.1 1.0 %hop.3 = (bf16[8,40,256]{2,1,0:T(8,128)(2,1)}, bf16[128,256]{1,0:T(8,128)(2,1)S(1)}, f32[64,64]{1,0:T(8,128)S(1)}) custom-call(bf16[4,40,256]{2,1,0:T(8,128)(2,1)S(1)} %all-to-all-done.1.gathered, bf16[3,224,256]{2,1,0:T(8,128)(2,1)S(1)} %get-tuple-element.48.selects, bf16[3,2,128,256]{3,2,1,0:T(8,128)(2,1)S(1)} %get-tuple-element.49.lifts), custom_call_target="tpu_custom_call" | custom-call | flops 100000000 | bytes 1048576 | tf_op jit(solution)/shard_map/hop/pallas_call | solution.py:595
  38.1 9.5 %all-to-all-start.2 = ((bf16[8,40,256]{2,1,0:T(8,128)(2,1)}), bf16[8,40,256]{2,1,0:T(8,128)(2,1)S(1)}, u32[]{:S(2)}, u32[]{:S(2)}) async-start(bf16[8,40,256]{2,1,0:T(8,128)(2,1)} %get-tuple-element.55), calls=%async_computation.2 | async-start | bytes 327680 | tf_op jit(solution)/shard_map/all_to_all | solution.py:587
  47.6 0.0 copy-start.5
  47.6 0.0 copy-start.8
  47.6 0.6 %terms.1.before = f32[32,64]{1,0:T(8,128)S(1)} custom-call(f32[3,96,32]{2,1,0:T(8,128)S(1)} %get-tuple-element.57.chains, bf16[64,256]{1,0:T(8,128)(2,1)S(1)} %get-tuple-element.58.refs_0_, f32[32,64]{1,0:T(8,128)S(1)} %get-tuple-element.59.refs_1_, bf16[192,256]{1,0:T(8,128)(2,1)S(1)} %get-tuple-element.60.refs_2_, f32[96,64]{1,0:T(8,128)S(1)} %get-tuple-element.61.refs_3_, ...), custom_call_target="tpu_custom_call" | custom-call | flops 100000000 | bytes 1048576 | tf_op jit(solution)/shard_map/terms/pallas_call | solution.py:623
  48.2 0.1 copy-done.5
  48.3 0.2 copy-done.8
  48.5 0.0 copy-start.1
  48.5 1.6 %far.1 = f32[256,128]{1,0:T(8,128)S(1)} custom-call(s32[7,32]{1,0:T(8,128)S(1)} %copy-done.5, f32[256,64]{1,0:T(8,128)S(1)} %copy-done.8, bf16[15,32,32]{2,1,0:T(8,128)(2,1)S(1)} %copy-done.2, bf16[128,256]{1,0:T(8,128)(2,1)S(1)} %get-tuple-element.65.refs_0_, bf16[128,256]{1,0:T(8,128)(2,1)S(1)} %get-tuple-element.66.refs_1_), custom_call_target="tpu_custom_call" | custom-call | flops 1000000000 | bytes 1048576 | tf_op jit(solution)/shard_map/far/pallas_call | solution.py:606
  50.1 0.0 copy-done.1
  50.2 2.7 %spread.1 = bf16[256,2048]{1,0:T(8,128)(2,1)S(1)} custom-call(s32[16,128]{1,0:T(8,128)S(1)} %bitcast.12, bf16[32,2048]{1,0:T(8,128)(2,1)S(1)} %bitcast.8, f32[256,128]{1,0:T(8,128)S(1)} %far.1, f32[64,1024]{1,0:T(8,128)S(1)} %get-tuple-element.67.refs_0_, f32[64,1024]{1,0:T(8,128)S(1)} %get-tuple-element.68.refs_1_), custom_call_target="tpu_custom_call" | custom-call | flops 2000000000 | bytes 1048576 | tf_op jit(solution)/shard_map/spread/pallas_call | solution.py:612
  52.9 4.1 %all-to-all-done.2.gathered = bf16[8,40,256]{2,1,0:T(8,128)(2,1)S(1)} async-done(((bf16[8,40,256]{2,1,0:T(8,128)(2,1)}), bf16[8,40,256]{2,1,0:T(8,128)(2,1)S(1)}, u32[]{:S(2)}, u32[]{:S(2)}) %all-to-all-start.2) | async-done | bytes 163872 | tf_op jit(solution)/shard_map/all_to_all | solution.py:587
  57.0 1.7 %final.1 = bf16[64,2048]{1,0:T(8,128)(2,1)} custom-call(bf16[8,40,256]{2,1,0:T(8,128)(2,1)S(1)} %all-to-all-done.2.gathered, bf16[3,224,256]{2,1,0:T(8,128)(2,1)S(1)} %get-tuple-element.48.selects, bf16[3,2,128,256]{3,2,1,0:T(8,128)(2,1)S(1)} %get-tuple-element.49.lifts, f32[3,96,32]{2,1,0:T(8,128)S(1)} %get-tuple-element.57.chains, ...), custom_call_target="tpu_custom_call" | custom-call | flops 100000000 | bytes 1048576 | tf_op jit(solution)/shard_map/final/pallas_call | solution.py:624
Async XLA Ops:
  0.0 6.8 %copy-start.9 = (s32[512,32]{0,1:T(8,128)S(1)}, s32[512,32]{0,1:T(8,128)}, u32[]{:S(2)}) copy-start(s32[512,32]{0,1:T(8,128)} %param.17) | copy-start | bytes 196612
  4.8 3.3 %collective-permute-start = (bf16[32,384]{1,0:T(8,128)(2,1)}, bf16[32,384]{1,0:T(8,128)(2,1)S(1)}, u32[]{:S(2)}, u32[]{:S(2)}) collective-permute-start(bf16[32,384]{1,0:T(8,128)(2,1)} %get-tuple-element.37.mine), channel_id=1, source_target_pairs={{0,1},{1,0},{2,3},{3,2},{4,5},{5,4},{6,7},{7,6},{8,9},{9,8},{10,11... | collective-permute-start | bytes 73736 | tf_op jit(solution)/shard_map/ppermute | solution.py:521
  6.8 0.7 %copy-start.10 = (bf16[32,384]{1,0:T(8,128)(2,1)S(1)}, bf16[32,384]{1,0:T(8,128)(2,1)}, u32[]{:S(2)}) copy-start(bf16[32,384]{1,0:T(8,128)(2,1)} %get-tuple-element.37.mine) | copy-start | bytes 73732
  8.9 7.2 %copy-start.2 = (bf16[15,32,32]{2,1,0:T(8,128)(2,1)S(1)}, bf16[15,32,32]{2,1,0:T(8,128)(2,1)}, u32[]{:S(2)}) copy-start(bf16[15,32,32]{2,1,0:T(8,128)(2,1)} %transfer.1) | copy-start | bytes 92164
  8.9 17.3 %all-to-all-start = ((bf16[8,40,256]{2,1,0:T(8,128)(2,1)}), bf16[8,40,256]{2,1,0:T(8,128)(2,1)S(1)}, u32[]{:S(2)}, u32[]{:S(2)}) async-start(bf16[8,40,256]{2,1,0:T(8,128)(2,1)} %get-tuple-element.40), calls=%async_computation | async-start | bytes 327680 | tf_op jit(solution)/shard_map/all_to_all | solution.py:587
  16.1 1.2 %copy-start.6 = (bf16[512,32,32]{0,2,1:T(8,128)(2,1)S(1)}, bf16[512,32,32]{0,2,1:T(8,128)(2,1)}, u32[]{:S(2)}) copy-start(bf16[512,32,32]{0,2,1:T(8,128)(2,1)} %param.16) | copy-start | bytes 3145732
  17.4 2.2 %copy-start = (bf16[2048,256]{1,0:T(8,128)(2,1)S(1)}, bf16[2048,256]{1,0:T(8,128)(2,1)}, u32[]{:S(2)}) copy-start(bf16[2048,256]{1,0:T(8,128)(2,1)} %emb.3) | copy-start | bytes 3145732
  17.4 2.2 %copy-start.3 = (s32[2048]{0:T(1024)S(1)}, s32[2048]{0:T(1024)}, u32[]{:S(2)}) copy-start(s32[2048]{0:T(1024)} %param.11) | copy-start | bytes 24580
  17.4 2.2 %copy-start.4 = (s32[8,32]{1,0:T(8,128)S(1)}, s32[8,32]{1,0:T(8,128)}, u32[]{:S(2)}) copy-start(s32[8,32]{1,0:T(8,128)} %skel.3) | copy-start | bytes 3076
  17.4 2.2 %copy-start.7 = (bf16[64,2048]{1,0:T(8,128)(2,1)S(1)}, bf16[64,2048]{1,0:T(8,128)(2,1)}, u32[]{:S(2)}) copy-start(bf16[64,2048]{1,0:T(8,128)(2,1)} %get-tuple-element.44.rhs_tree) | copy-start | bytes 786436
  27.2 9.9 %all-to-all-start.1 = ((bf16[4,40,256]{2,1,0:T(8,128)(2,1)}), bf16[4,40,256]{2,1,0:T(8,128)(2,1)S(1)}, u32[]{:S(2)}, u32[]{:S(2)}) async-start(bf16[4,40,256]{2,1,0:T(8,128)(2,1)} %get-tuple-element.50), calls=%async_computation.1 | async-start | bytes 163840 | tf_op jit(solution)/shard_map/all_to_all | solution.py:587
  38.1 18.9 %all-to-all-start.2 = ((bf16[8,40,256]{2,1,0:T(8,128)(2,1)}), bf16[8,40,256]{2,1,0:T(8,128)(2,1)S(1)}, u32[]{:S(2)}, u32[]{:S(2)}) async-start(bf16[8,40,256]{2,1,0:T(8,128)(2,1)} %get-tuple-element.55), calls=%async_computation.2 | async-start | bytes 327680 | tf_op jit(solution)/shard_map/all_to_all | solution.py:587
  47.6 0.7 %copy-start.5 = (s32[7,32]{1,0:T(8,128)S(1)}, s32[7,32]{1,0:T(8,128)}, u32[]{:S(2)}) copy-start(s32[7,32]{1,0:T(8,128)} %pick.1) | copy-start | bytes 2692
  47.6 0.9 %copy-start.8 = (f32[256,64]{1,0:T(8,128)S(1)}, f32[256,64]{1,0:T(8,128)}, u32[]{:S(2)}) copy-start(f32[256,64]{1,0:T(8,128)} %get-tuple-element.64.weights) | copy-start | bytes 196612
  48.5 1.6 %copy-start.1 = (bf16[2048,32]{0,1:T(8,128)(2,1)S(1)}, bf16[2048,32]{0,1:T(8,128)(2,1)}, u32[]{:S(2)}) copy-start(bf16[2048,32]{0,1:T(8,128)(2,1)} %param.12) | copy-start | bytes 393220

commit v4 on v3

--- a/solution.py
+++ b/solution.py
@@ -149,18 +149,21 @@
     joined = jnp.concatenate([rhs[:, b * leaf : (b + 1) * leaf] for b in range(blocks)], axis=0)
 
     def gather(l):
-        row = order_row(order, l)
+        row = jnp.concatenate([order_row(order, l + j) for j in range(4)], axis=1)
         low, high = row & (leaf - 1), row // leaf
-        found = dot(joined, one_hot(low == iota((leaf, leaf), 0)))
+        found = dot(joined, one_hot(low == iota((leaf, 4 * leaf), 0)))
         total = None
         for b in range(blocks):
             part = jnp.where(high == b, found[b * cols : (b + 1) * cols, :], 0.0)
             total = part if total is None else total + part
         picked = total.astype(BF16)
-        rhs_tree[:, l * leaf : (l + 1) * leaf] = picked
-        lifted = dot_last(basis[:, l * leaf : (l + 1) * leaf], picked)
-        weights[l * rank : (l + 1) * rank, :] = lifted
-        return lifted
+        rhs_tree[:, l * leaf : (l + 4) * leaf] = picked
+        found = []
+        for j in range(4):
+            lanes = slice((l + j) * leaf, (l + j + 1) * leaf)
+            found.append(dot_last(basis[:, lanes], picked[:, j * leaf : (j + 1) * leaf]))
+            weights[(l + j) * rank : (l + j + 1) * rank, :] = found[-1]
+        return found
 
     def lift(q, left, right):
         pair = jnp.concatenate([left, right], axis=0)
@@ -168,7 +171,9 @@
 
     nodes, parents, pending = None, leaves, {}
     for l in range(leaves):
-        node, q = gather(l), leaves + l
+        if l % 4 == 0:
+            group = gather(l)
+        node, q = group[l % 4], leaves + l
         if l == 1:
             copies[6].wait()
         if l == leaves - 1:
@@ -414,18 +419,17 @@
 def leaf_body(first, count, rank, order, emb, rhs_tree, skel, near, points):
     items = emb.shape[0]
     leaf = near.shape[1] // count
-    order_t = columns_of(order[...])
     table = padded_columns([skel[...]], 8)
-    for i in range(0, count, 2):
-        column = jnp.concatenate([order_column(order_t, first + i), order_column(order_t, first + i + 1)], axis=0)
-        high, low = digits_of(column, leaf)
-        offset = one_hot(iota((2 * leaf, leaf), 1) == (column & (leaf - 1)))
-        block = jnp.broadcast_to(high, (2 * leaf, leaf))
-        hot = jnp.concatenate([jnp.where(block == b, offset, jnp.zeros_like(offset)) for b in range(items // leaf)], axis=1)
-        both = dot(hot, emb[...]).astype(BF16)
-        for j in range(i, i + 2):
+    turned = emb[...].T
+    for i in range(0, count, 4):
+        row = jnp.concatenate([order_row(order, first + j) for j in range(i, i + 4)], axis=1)
+        offset = one_hot(iota((leaf, 4 * leaf), 0) == (row & (leaf - 1)))
+        block = jnp.broadcast_to(digits_of(row, leaf)[0], (leaf, 4 * leaf))
+        hot = jnp.concatenate([jnp.where(block == b, offset, jnp.zeros_like(offset)) for b in range(items // leaf)], axis=0)
+        both = dot(turned, hot).astype(BF16)
+        for j in range(i, i + 4):
             l = first + j
-            feats = both[(j - i) * leaf : (j - i + 1) * leaf, :]
+            feats = both[:, (j - i) * leaf : (j - i + 1) * leaf].astype(F32).T.astype(BF16)
             kernel, eye = self_kernel(feats)
             kernel = jnp.where(eye, kernel + RIDGE, kernel).astype(BF16)
             near[:, j * leaf : (j + 1) * leaf] = dot(rhs_tree[:, l * leaf : (l + 1) * leaf], kernel)

time: 59.3 us -> 58.5 us (0.987)
  Pallas kernels: 24.8 us -> 19.9 us
  waiting for transfers between devices: 7.21 us -> 11.3 us
    pallas_call x2, Pallas kernels: 8.24 us -> 4.1 us  [leaf_part(): call(functools.partial(leaf_body, first, count, rank), (shape((cols, item...]
    all_to_all x3, waiting for transfers between devices: 6.8 us -> 10.9 us  [local(): gathered = lax.all_to_all(payload, 'leaf', 0, 0, axis_index_groups=groups)]
    pallas_call x1, Pallas kernels: 4.81 us -> 4.03 us  [local(): call(functools.partial(pre_body, leaves), (shape((rank, width + 2 * cols)...]
  transfers between devices with their start and end apart: 4 -> 4, of which waited for: 4 -> 4; matrix products, arithmetic and copies ran while one was open for 0% -> 0% of each run, Pallas kernels for 27% -> 20%
where the time goes in v4:
time: 58.5 us; the launch traced here: 58 us
  starting transfers between devices  24.3 us (42%)
  Pallas kernels  19.9 us (34%)
  waiting for transfers between devices  11.3 us (19%)
  local copies, waits for them, and re-layouts  2.28 us (4%)
    all_to_all x3, starting transfers between devices, local(): gathered = lax.all_to_all(payload, 'leaf', 0, 0, axis_index_groups=groups)  22.4 us
    all_to_all x3, waiting for transfers between devices, local(): gathered = lax.all_to_all(payload, 'leaf', 0, 0, axis_index_groups=groups)  10.9 us
    pallas_call x2, Pallas kernels, leaf_part(): call(functools.partial(leaf_body, first, count, rank), (shape((cols, item...  4.1 us
    pallas_call x1, Pallas kernels, local(): call(functools.partial(pre_body, leaves), (shape((rank, width + 2 * cols)...  4.03 us
    pallas_call x1, Pallas kernels, local(): call(functools.partial(spread_body, len(parts), items // leaves, rank), s...  2.75 us
    unnamed x22, local copies, waits for them, and re-layouts  2.28 us
    pallas_call x1, Pallas kernels, local(): call(functools.partial(prep_body, devices, radices), (shape((stages, (2 *...  2.15 us
    pallas_call x2, Pallas kernels, local(): call(functools.partial(hop_body, stage, depth, rank, cols), (shape((radic...  1.96 us
  transfers between devices with their start and end apart: 4, of which 4 were waited for; matrix products, arithmetic and copies ran while one was open for 0% of the time, Pallas kernels for 20%

profile of v4, /device:TPU:2, one launch (start us, length us, event | category | flops | bytes accessed | tf_op | source)
XLA Modules:
  0.0 58.0 jit_solution(6013777098271156411)
XLA Ops:
  0.0 0.0 copy-start.9
  0.0 4.0 %pre.1 = (bf16[32,384]{1,0:T(8,128)(2,1)}, bf16[64,2048]{1,0:T(8,128)(2,1)}, f32[256,64]{1,0:T(8,128)}) custom-call(s32[16,128]{1,0:T(8,128)} %bitcast.9, s32[8,32]{1,0:T(8,128)} %skel.3, s32[7,32]{1,0:T(8,128)} %pick.1, bf16[64,2048]{1,0:T(8,128)(2,1)} %bitcast.16, bf16[32,2048]{1,0:T(8,128)(2,1)} %bitcast.7, bf16[15,32,32]{2,1,0:T(8,128)(2,1)} %transfer.1, ...), custom_call_target="tpu_custom_call" | custom-call | flops 100000000 | bytes 1048576 | tf_op jit(solution)/shard_map/pre/pallas_call | solution.py:513
  4.0 1.9 %collective-permute-start = (bf16[32,384]{1,0:T(8,128)(2,1)}, bf16[32,384]{1,0:T(8,128)(2,1)S(1)}, u32[]{:S(2)}, u32[]{:S(2)}) collective-permute-start(bf16[32,384]{1,0:T(8,128)(2,1)} %get-tuple-element.37.mine), channel_id=1, source_target_pairs={{0,1},{1,0},{2,3},{3,2},{4,5},{5,4},{6,7},{7,6},{8,9},{9,8},{10,11... | collective-permute-start | bytes 73736 | tf_op jit(solution)/shard_map/ppermute | solution.py:525
  6.0 0.0 copy-done.9
  6.0 0.0 copy-start.10
  6.0 0.7 %copy-done.10 = bf16[32,384]{1,0:T(8,128)(2,1)S(1)} copy-done((bf16[32,384]{1,0:T(8,128)(2,1)S(1)}, bf16[32,384]{1,0:T(8,128)(2,1)}, u32[]{:S(2)}) %copy-start.10) | copy-done | bytes 24600
  6.7 0.2 side.1
  6.9 0.4 collective-permute-done.other
  7.3 0.8 %pair.1 = (bf16[8,40,256]{2,1,0:T(8,128)(2,1)}, bf16[64,256]{1,0:T(8,128)(2,1)S(1)}, f32[32,64]{1,0:T(8,128)S(1)}) custom-call(bf16[32,64]{1,0:T(8,128)(2,1)S(1)} %get-tuple-element.38.hot, bf16[32,384]{1,0:T(8,128)(2,1)S(1)} %get-tuple-element.39.mine, bf16[32,384]{1,0:T(8,128)(2,1)S(1)} %collective-permute-done.other), custom_call_target="tpu_custom_call" | custom-call | flops 100000000 | bytes 1048576 | tf_op jit(solution)/shard_map/pair/pallas_call | solution.py:535
  8.1 0.0 copy-start.2
  8.1 7.2 %all-to-all-start = ((bf16[8,40,256]{2,1,0:T(8,128)(2,1)}), bf16[8,40,256]{2,1,0:T(8,128)(2,1)S(1)}, u32[]{:S(2)}, u32[]{:S(2)}) async-start(bf16[8,40,256]{2,1,0:T(8,128)(2,1)} %get-tuple-element.40), calls=%async_computation | async-start | bytes 327680 | tf_op jit(solution)/shard_map/all_to_all | solution.py:591
  15.4 0.0 copy-done.2
  15.4 0.0 copy-start.6
  15.4 1.2 %copy-done.6 = bf16[512,32,32]{0,2,1:T(8,128)(2,1)S(1)} copy-done((bf16[512,32,32]{0,2,1:T(8,128)(2,1)S(1)}, bf16[512,32,32]{0,2,1:T(8,128)(2,1)}, u32[]{:S(2)}) %copy-start.6) | copy-done | bytes 1048600
  16.6 0.0 copy-start
  16.6 0.0 copy-start.3
  16.6 0.0 copy-start.4
  16.6 0.0 copy-start.7
  16.6 2.2 %prep.1 = (bf16[3,224,256]{2,1,0:T(8,128)(2,1)S(1)}, bf16[3,2,128,256]{3,2,1,0:T(8,128)(2,1)S(1)}, f32[3,96,32]{2,1,0:T(8,128)S(1)}) custom-call(s32[1]{0:T(128)} %bitcast.me_ref, s32[32,512]{1,0:T(8,128)S(1)} %bitcast.15, bf16[32,32,512]{2,1,0:T(8,128)(2,1)S(1)} %bitcast.13, bf16[15,32,32]{2,1,0:T(8,128)(2,1)S(1)} %copy-done.2), custom_call_target="tpu_custom_call" | custom-call | flops 2000000000 | bytes 1048576 | tf_op jit(solution)/shard_map/prep/pallas_call | solution.py:552
  18.8 0.0 copy-done
  18.8 0.0 copy-done.3
  18.8 0.0 copy-done.4
  18.8 0.0 copy-done.7
  18.8 2.1 %leaf.2 = (f32[64,1024]{1,0:T(8,128)S(1)}, bf16[128,256]{1,0:T(8,128)(2,1)S(1)}) custom-call(s32[16,128]{1,0:T(8,128)S(1)} %bitcast.10, bf16[2048,256]{1,0:T(8,128)(2,1)S(1)} %copy-done, bf16[64,2048]{1,0:T(8,128)(2,1)S(1)} %copy-done.7, s32[8,32]{1,0:T(8,128)S(1)} %copy-done.4), custom_call_target="tpu_custom_call" | custom-call | flops 2000000000 | bytes 1048576 | tf_op jit(solution)/shard_map/leaf/pallas_call | solution.py:574
  20.9 4.6 %all-to-all-done.gathered = bf16[8,40,256]{2,1,0:T(8,128)(2,1)S(1)} async-done(((bf16[8,40,256]{2,1,0:T(8,128)(2,1)}), bf16[8,40,256]{2,1,0:T(8,128)(2,1)S(1)}, u32[]{:S(2)}, u32[]{:S(2)}) %all-to-all-start) | async-done | bytes 163872 | tf_op jit(solution)/shard_map/all_to_all | solution.py:591
  25.5 1.0 %hop.2 = (bf16[4,40,256]{2,1,0:T(8,128)(2,1)}, bf16[192,256]{1,0:T(8,128)(2,1)S(1)}, f32[96,64]{1,0:T(8,128)S(1)}) custom-call(bf16[8,40,256]{2,1,0:T(8,128)(2,1)S(1)} %all-to-all-done.gathered, bf16[3,224,256]{2,1,0:T(8,128)(2,1)S(1)} %get-tuple-element.48.selects, bf16[3,2,128,256]{3,2,1,0:T(8,128)(2,1)S(1)} %get-tuple-element.49.lifts), custom_call_target="tpu_custom_call" | custom-call | flops 100000000 | bytes 1048576 | tf_op jit(solution)/shard_map/hop/pallas_call | solution.py:599
  26.5 5.6 %all-to-all-start.1 = ((bf16[4,40,256]{2,1,0:T(8,128)(2,1)}), bf16[4,40,256]{2,1,0:T(8,128)(2,1)S(1)}, u32[]{:S(2)}, u32[]{:S(2)}) async-start(bf16[4,40,256]{2,1,0:T(8,128)(2,1)} %get-tuple-element.50), calls=%async_computation.1 | async-start | bytes 163840 | tf_op jit(solution)/shard_map/all_to_all | solution.py:591
  32.1 2.0 %leaf.3 = (f32[64,1024]{1,0:T(8,128)S(1)}, bf16[128,256]{1,0:T(8,128)(2,1)S(1)}) custom-call(s32[16,128]{1,0:T(8,128)S(1)} %bitcast.11, bf16[2048,256]{1,0:T(8,128)(2,1)S(1)} %copy-done, bf16[64,2048]{1,0:T(8,128)(2,1)S(1)} %copy-done.7, s32[8,32]{1,0:T(8,128)S(1)} %copy-done.4), custom_call_target="tpu_custom_call" | custom-call | flops 2000000000 | bytes 1048576 | tf_op jit(solution)/shard_map/leaf/pallas_call | solution.py:574
  34.2 2.2 %all-to-all-done.1.gathered = bf16[4,40,256]{2,1,0:T(8,128)(2,1)S(1)} async-done(((bf16[4,40,256]{2,1,0:T(8,128)(2,1)}), bf16[4,40,256]{2,1,0:T(8,128)(2,1)S(1)}, u32[]{:S(2)}, u32[]{:S(2)}) %all-to-all-start.1) | async-done | bytes 81952 | tf_op jit(solution)/shard_map/all_to_all | solution.py:591
  36.4 1.0 %hop.3 = (bf16[8,40,256]{2,1,0:T(8,128)(2,1)}, bf16[128,256]{1,0:T(8,128)(2,1)S(1)}, f32[64,64]{1,0:T(8,128)S(1)}) custom-call(bf16[4,40,256]{2,1,0:T(8,128)(2,1)S(1)} %all-to-all-done.1.gathered, bf16[3,224,256]{2,1,0:T(8,128)(2,1)S(1)} %get-tuple-element.48.selects, bf16[3,2,128,256]{3,2,1,0:T(8,128)(2,1)S(1)} %get-tuple-element.49.lifts), custom_call_target="tpu_custom_call" | custom-call | flops 100000000 | bytes 1048576 | tf_op jit(solution)/shard_map/hop/pallas_call | solution.py:599
  37.3 9.5 %all-to-all-start.2 = ((bf16[8,40,256]{2,1,0:T(8,128)(2,1)}), bf16[8,40,256]{2,1,0:T(8,128)(2,1)S(1)}, u32[]{:S(2)}, u32[]{:S(2)}) async-start(bf16[8,40,256]{2,1,0:T(8,128)(2,1)} %get-tuple-element.55), calls=%async_computation.2 | async-start | bytes 327680 | tf_op jit(solution)/shard_map/all_to_all | solution.py:591
  46.8 0.0 copy-start.5
  46.8 0.0 copy-start.8
  46.8 0.6 %terms.1.before = f32[32,64]{1,0:T(8,128)S(1)} custom-call(f32[3,96,32]{2,1,0:T(8,128)S(1)} %get-tuple-element.57.chains, bf16[64,256]{1,0:T(8,128)(2,1)S(1)} %get-tuple-element.58.refs_0_, f32[32,64]{1,0:T(8,128)S(1)} %get-tuple-element.59.refs_1_, bf16[192,256]{1,0:T(8,128)(2,1)S(1)} %get-tuple-element.60.refs_2_, f32[96,64]{1,0:T(8,128)S(1)} %get-tuple-element.61.refs_3_, ...), custom_call_target="tpu_custom_call" | custom-call | flops 100000000 | bytes 1048576 | tf_op jit(solution)/shard_map/terms/pallas_call | solution.py:627
  47.4 0.1 copy-done.5
  47.5 0.2 copy-done.8
  47.7 0.0 copy-start.1
  47.7 1.6 %far.1 = f32[256,128]{1,0:T(8,128)S(1)} custom-call(s32[7,32]{1,0:T(8,128)S(1)} %copy-done.5, f32[256,64]{1,0:T(8,128)S(1)} %copy-done.8, bf16[15,32,32]{2,1,0:T(8,128)(2,1)S(1)} %copy-done.2, bf16[128,256]{1,0:T(8,128)(2,1)S(1)} %get-tuple-element.65.refs_0_, bf16[128,256]{1,0:T(8,128)(2,1)S(1)} %get-tuple-element.66.refs_1_), custom_call_target="tpu_custom_call" | custom-call | flops 1000000000 | bytes 1048576 | tf_op jit(solution)/shard_map/far/pallas_call | solution.py:610
  49.4 0.0 copy-done.1
  49.4 2.7 %spread.1 = bf16[256,2048]{1,0:T(8,128)(2,1)S(1)} custom-call(s32[16,128]{1,0:T(8,128)S(1)} %bitcast.12, bf16[32,2048]{1,0:T(8,128)(2,1)S(1)} %bitcast.8, f32[256,128]{1,0:T(8,128)S(1)} %far.1, f32[64,1024]{1,0:T(8,128)S(1)} %get-tuple-element.67.refs_0_, f32[64,1024]{1,0:T(8,128)S(1)} %get-tuple-element.68.refs_1_), custom_call_target="tpu_custom_call" | custom-call | flops 2000000000 | bytes 1048576 | tf_op jit(solution)/shard_map/spread/pallas_call | solution.py:616
  52.1 4.1 %all-to-all-done.2.gathered = bf16[8,40,256]{2,1,0:T(8,128)(2,1)S(1)} async-done(((bf16[8,40,256]{2,1,0:T(8,128)(2,1)}), bf16[8,40,256]{2,1,0:T(8,128)(2,1)S(1)}, u32[]{:S(2)}, u32[]{:S(2)}) %all-to-all-start.2) | async-done | bytes 163872 | tf_op jit(solution)/shard_map/all_to_all | solution.py:591
  56.3 1.7 %final.1 = bf16[64,2048]{1,0:T(8,128)(2,1)} custom-call(bf16[8,40,256]{2,1,0:T(8,128)(2,1)S(1)} %all-to-all-done.2.gathered, bf16[3,224,256]{2,1,0:T(8,128)(2,1)S(1)} %get-tuple-element.48.selects, bf16[3,2,128,256]{3,2,1,0:T(8,128)(2,1)S(1)} %get-tuple-element.49.lifts, f32[3,96,32]{2,1,0:T(8,128)S(1)} %get-tuple-element.57.chains, ...), custom_call_target="tpu_custom_call" | custom-call | flops 100000000 | bytes 1048576 | tf_op jit(solution)/shard_map/final/pallas_call | solution.py:628
Async XLA Ops:
  0.0 6.0 %copy-start.9 = (s32[512,32]{0,1:T(8,128)S(1)}, s32[512,32]{0,1:T(8,128)}, u32[]{:S(2)}) copy-start(s32[512,32]{0,1:T(8,128)} %param.17) | copy-start | bytes 196612
  4.0 3.3 %collective-permute-start = (bf16[32,384]{1,0:T(8,128)(2,1)}, bf16[32,384]{1,0:T(8,128)(2,1)S(1)}, u32[]{:S(2)}, u32[]{:S(2)}) collective-permute-start(bf16[32,384]{1,0:T(8,128)(2,1)} %get-tuple-element.37.mine), channel_id=1, source_target_pairs={{0,1},{1,0},{2,3},{3,2},{4,5},{5,4},{6,7},{7,6},{8,9},{9,8},{10,11... | collective-permute-start | bytes 73736 | tf_op jit(solution)/shard_map/ppermute | solution.py:525
  6.0 0.7 %copy-start.10 = (bf16[32,384]{1,0:T(8,128)(2,1)S(1)}, bf16[32,384]{1,0:T(8,128)(2,1)}, u32[]{:S(2)}) copy-start(bf16[32,384]{1,0:T(8,128)(2,1)} %get-tuple-element.37.mine) | copy-start | bytes 73732
  8.1 7.2 %copy-start.2 = (bf16[15,32,32]{2,1,0:T(8,128)(2,1)S(1)}, bf16[15,32,32]{2,1,0:T(8,128)(2,1)}, u32[]{:S(2)}) copy-start(bf16[15,32,32]{2,1,0:T(8,128)(2,1)} %transfer.1) | copy-start | bytes 92164
  8.1 17.3 %all-to-all-start = ((bf16[8,40,256]{2,1,0:T(8,128)(2,1)}), bf16[8,40,256]{2,1,0:T(8,128)(2,1)S(1)}, u32[]{:S(2)}, u32[]{:S(2)}) async-start(bf16[8,40,256]{2,1,0:T(8,128)(2,1)} %get-tuple-element.40), calls=%async_computation | async-start | bytes 327680 | tf_op jit(solution)/shard_map/all_to_all | solution.py:591
  15.4 1.2 %copy-start.6 = (bf16[512,32,32]{0,2,1:T(8,128)(2,1)S(1)}, bf16[512,32,32]{0,2,1:T(8,128)(2,1)}, u32[]{:S(2)}) copy-start(bf16[512,32,32]{0,2,1:T(8,128)(2,1)} %param.16) | copy-start | bytes 3145732
  16.6 2.2 %copy-start = (bf16[2048,256]{1,0:T(8,128)(2,1)S(1)}, bf16[2048,256]{1,0:T(8,128)(2,1)}, u32[]{:S(2)}) copy-start(bf16[2048,256]{1,0:T(8,128)(2,1)} %emb.3) | copy-start | bytes 3145732
  16.6 2.2 %copy-start.3 = (s32[2048]{0:T(1024)S(1)}, s32[2048]{0:T(1024)}, u32[]{:S(2)}) copy-start(s32[2048]{0:T(1024)} %param.11) | copy-start | bytes 24580
  16.6 2.2 %copy-start.4 = (s32[8,32]{1,0:T(8,128)S(1)}, s32[8,32]{1,0:T(8,128)}, u32[]{:S(2)}) copy-start(s32[8,32]{1,0:T(8,128)} %skel.3) | copy-start | bytes 3076
  16.6 2.2 %copy-start.7 = (bf16[64,2048]{1,0:T(8,128)(2,1)S(1)}, bf16[64,2048]{1,0:T(8,128)(2,1)}, u32[]{:S(2)}) copy-start(bf16[64,2048]{1,0:T(8,128)(2,1)} %get-tuple-element.44.rhs_tree) | copy-start | bytes 786436
  26.5 9.9 %all-to-all-start.1 = ((bf16[4,40,256]{2,1,0:T(8,128)(2,1)}), bf16[4,40,256]{2,1,0:T(8,128)(2,1)S(1)}, u32[]{:S(2)}, u32[]{:S(2)}) async-start(bf16[4,40,256]{2,1,0:T(8,128)(2,1)} %get-tuple-element.50), calls=%async_computation.1 | async-start | bytes 163840 | tf_op jit(solution)/shard_map/all_to_all | solution.py:591
  37.3 18.9 %all-to-all-start.2 = ((bf16[8,40,256]{2,1,0:T(8,128)(2,1)}), bf16[8,40,256]{2,1,0:T(8,128)(2,1)S(1)}, u32[]{:S(2)}, u32[]{:S(2)}) async-start(bf16[8,40,256]{2,1,0:T(8,128)(2,1)} %get-tuple-element.55), calls=%async_computation.2 | async-start | bytes 327680 | tf_op jit(solution)/shard_map/all_to_all | solution.py:591
  46.8 0.7 %copy-start.5 = (s32[7,32]{1,0:T(8,128)S(1)}, s32[7,32]{1,0:T(8,128)}, u32[]{:S(2)}) copy-start(s32[7,32]{1,0:T(8,128)} %pick.1) | copy-start | bytes 2692
  46.8 0.9 %copy-start.8 = (f32[256,64]{1,0:T(8,128)S(1)}, f32[256,64]{1,0:T(8,128)}, u32[]{:S(2)}) copy-start(f32[256,64]{1,0:T(8,128)} %get-tuple-element.64.weights) | copy-start | bytes 196612
  47.7 1.6 %copy-start.1 = (bf16[2048,32]{0,1:T(8,128)(2,1)S(1)}, bf16[2048,32]{0,1:T(8,128)(2,1)}, u32[]{:S(2)}) copy-start(bf16[2048,32]{0,1:T(8,128)(2,1)} %param.12) | copy-start | bytes 393220

commit v5 on v4

--- a/solution.py
+++ b/solution.py
@@ -308,12 +308,13 @@
         base += depth
 
 
-def gathered_nodes(rank, cols, gathered, select, lift):
+def gathered_nodes(rank, cols, gathered, select, lift, turned=False):
     count, rows, width = gathered.shape
     wide = count * rank
-    points = dot(select[:, :wide], gathered[:, :rank, :].reshape(wide, width)).astype(BF16)
+    places = range(count)[::-1] if turned else range(count)
+    points = dot(select[:, :wide], jnp.concatenate([gathered[j, :rank, :] for j in places], axis=0)).astype(BF16)
     tails = gathered[:, rank:, :].astype(F32)
-    parts = [tails[j, :, c : c + cols] for j in range(count) for c in range(0, width, cols)]
+    parts = [tails[j, :, c : c + cols] for j in places for c in range(0, width, cols)]
     weights = jnp.concatenate(parts, axis=0).astype(BF16)
     return points, dot(lift[0, :, :wide], weights) + dot(lift[1, :, :wide], weights)
 
@@ -361,7 +362,7 @@
 def final_body(stage, depth, rank, cols, gathered, selects, lifts, chains, before, spread, product):
     rows = depth * rank
     points, lifted = gathered_nodes(
-        rank, cols, gathered, selects[stage, : 2 * rows, :], lifts[stage, :, :rows, :]
+        rank, cols, gathered, selects[stage, : 2 * rows, :], lifts[stage, :, :rows, :], turned=True
     )
     terms = terms_of(points[:rows, :], points[rows:, :], lifted, rank)
     field = chained(chains[stage], terms, rank) + before[...]
@@ -584,7 +585,7 @@
     for stage, (n, depth) in enumerate(zip(radices, depths)):
         stride = 1 << base
         groups = [
-            [high * stride * n + low + stride * j for j in range(n)]
+            [high * stride * n + low + stride * j for j in (range(n) if stage + 1 < stages else range(n)[::-1])]
             for high in range(devices // (stride * n))
             for low in range(stride)
         ]

time: 58.5 us -> 57 us (0.974)
  waiting for transfers between devices: 11.3 us -> 7.78 us
  starting transfers between devices: 24.3 us -> 26.3 us
    all_to_all x3, waiting for transfers between devices: 10.9 us -> 7.36 us  [local(): gathered = lax.all_to_all(payload, 'leaf', 0, 0, axis_index_groups=groups)]
    all_to_all x3, starting transfers between devices: 22.4 us -> 24.4 us  [local(): gathered = lax.all_to_all(payload, 'leaf', 0, 0, axis_index_groups=groups)]
where the time goes in v5:
time: 57 us; the launch traced here: 56.4 us
  starting transfers between devices  26.3 us (46%)
  Pallas kernels  19.9 us (35%)
  waiting for transfers between devices  7.78 us (14%)
  local copies, waits for them, and re-layouts  2.29 us (4%)
    all_to_all x3, starting transfers between devices, local(): gathered = lax.all_to_all(payload, 'leaf', 0, 0, axis_index_groups=groups)  24.4 us
    all_to_all x3, waiting for transfers between devices, local(): gathered = lax.all_to_all(payload, 'leaf', 0, 0, axis_index_groups=groups)  7.36 us
    pallas_call x2, Pallas kernels, leaf_part(): call(functools.partial(leaf_body, first, count, rank), (shape((cols, item...  4.1 us
    pallas_call x1, Pallas kernels, local(): call(functools.partial(pre_body, leaves), (shape((rank, width + 2 * cols)...  4.03 us
    pallas_call x1, Pallas kernels, local(): call(functools.partial(spread_body, len(parts), items // leaves, rank), s...  2.74 us
    unnamed x22, local copies, waits for them, and re-layouts  2.29 us
    pallas_call x1, Pallas kernels, local(): call(functools.partial(prep_body, devices, radices), (shape((stages, (2 *...  2.15 us
    pallas_call x2, Pallas kernels, local(): call(functools.partial(hop_body, stage, depth, rank, cols), (shape((radic...  1.96 us
  transfers between devices with their start and end apart: 4, of which 4 were waited for; matrix products, arithmetic and copies ran while one was open for 0% of the time, Pallas kernels for 20%

profile of v5, /device:TPU:2, one launch (start us, length us, event | category | flops | bytes accessed | tf_op | source)
XLA Modules:
  0.0 56.4 jit_solution(2117220492893562764)
XLA Ops:
  0.0 0.0 copy-start.9
  0.0 4.0 %pre.1 = (bf16[32,384]{1,0:T(8,128)(2,1)}, bf16[64,2048]{1,0:T(8,128)(2,1)}, f32[256,64]{1,0:T(8,128)}) custom-call(s32[16,128]{1,0:T(8,128)} %bitcast.9, s32[8,32]{1,0:T(8,128)} %skel.3, s32[7,32]{1,0:T(8,128)} %pick.1, bf16[64,2048]{1,0:T(8,128)(2,1)} %bitcast.16, bf16[32,2048]{1,0:T(8,128)(2,1)} %bitcast.7, bf16[15,32,32]{2,1,0:T(8,128)(2,1)} %transfer.1, ...), custom_call_target="tpu_custom_call" | custom-call | flops 100000000 | bytes 1048576 | tf_op jit(solution)/shard_map/pre/pallas_call | solution.py:514
  4.0 1.9 %collective-permute-start = (bf16[32,384]{1,0:T(8,128)(2,1)}, bf16[32,384]{1,0:T(8,128)(2,1)S(1)}, u32[]{:S(2)}, u32[]{:S(2)}) collective-permute-start(bf16[32,384]{1,0:T(8,128)(2,1)} %get-tuple-element.37.mine), channel_id=1, source_target_pairs={{0,1},{1,0},{2,3},{3,2},{4,5},{5,4},{6,7},{7,6},{8,9},{9,8},{10,11... | collective-permute-start | bytes 73736 | tf_op jit(solution)/shard_map/ppermute | solution.py:526
  6.0 0.0 copy-done.9
  6.0 0.0 copy-start.10
  6.0 0.7 %copy-done.10 = bf16[32,384]{1,0:T(8,128)(2,1)S(1)} copy-done((bf16[32,384]{1,0:T(8,128)(2,1)S(1)}, bf16[32,384]{1,0:T(8,128)(2,1)}, u32[]{:S(2)}) %copy-start.10) | copy-done | bytes 24600
  6.7 0.2 side.1
  6.9 0.4 collective-permute-done.other
  7.3 0.8 %pair.1 = (bf16[8,40,256]{2,1,0:T(8,128)(2,1)}, bf16[64,256]{1,0:T(8,128)(2,1)S(1)}, f32[32,64]{1,0:T(8,128)S(1)}) custom-call(bf16[32,64]{1,0:T(8,128)(2,1)S(1)} %get-tuple-element.38.hot, bf16[32,384]{1,0:T(8,128)(2,1)S(1)} %get-tuple-element.39.mine, bf16[32,384]{1,0:T(8,128)(2,1)S(1)} %collective-permute-done.other), custom_call_target="tpu_custom_call" | custom-call | flops 100000000 | bytes 1048576 | tf_op jit(solution)/shard_map/pair/pallas_call | solution.py:536
  8.1 0.0 copy-start.2
  8.1 7.2 %all-to-all-start = ((bf16[8,40,256]{2,1,0:T(8,128)(2,1)}), bf16[8,40,256]{2,1,0:T(8,128)(2,1)S(1)}, u32[]{:S(2)}, u32[]{:S(2)}) async-start(bf16[8,40,256]{2,1,0:T(8,128)(2,1)} %get-tuple-element.40), calls=%async_computation | async-start | bytes 327680 | tf_op jit(solution)/shard_map/all_to_all | solution.py:592
  15.4 0.0 copy-done.2
  15.4 0.0 copy-start.6
  15.4 1.2 %copy-done.6 = bf16[512,32,32]{0,2,1:T(8,128)(2,1)S(1)} copy-done((bf16[512,32,32]{0,2,1:T(8,128)(2,1)S(1)}, bf16[512,32,32]{0,2,1:T(8,128)(2,1)}, u32[]{:S(2)}) %copy-start.6) | copy-done | bytes 1048600
  16.6 0.0 copy-start
  16.6 0.0 copy-start.3
  16.6 0.0 copy-start.4
  16.6 0.0 copy-start.7
  16.6 2.2 %prep.1 = (bf16[3,224,256]{2,1,0:T(8,128)(2,1)S(1)}, bf16[3,2,128,256]{3,2,1,0:T(8,128)(2,1)S(1)}, f32[3,96,32]{2,1,0:T(8,128)S(1)}) custom-call(s32[1]{0:T(128)} %bitcast.me_ref, s32[32,512]{1,0:T(8,128)S(1)} %bitcast.15, bf16[32,32,512]{2,1,0:T(8,128)(2,1)S(1)} %bitcast.13, bf16[15,32,32]{2,1,0:T(8,128)(2,1)S(1)} %copy-done.2), custom_call_target="tpu_custom_call" | custom-call | flops 2000000000 | bytes 1048576 | tf_op jit(solution)/shard_map/prep/pallas_call | solution.py:553
  18.8 0.0 copy-done
  18.8 0.0 copy-done.3
  18.8 0.0 copy-done.4
  18.8 0.0 copy-done.7
  18.8 2.1 %leaf.2 = (f32[64,1024]{1,0:T(8,128)S(1)}, bf16[128,256]{1,0:T(8,128)(2,1)S(1)}) custom-call(s32[16,128]{1,0:T(8,128)S(1)} %bitcast.10, bf16[2048,256]{1,0:T(8,128)(2,1)S(1)} %copy-done, bf16[64,2048]{1,0:T(8,128)(2,1)S(1)} %copy-done.7, s32[8,32]{1,0:T(8,128)S(1)} %copy-done.4), custom_call_target="tpu_custom_call" | custom-call | flops 2000000000 | bytes 1048576 | tf_op jit(solution)/shard_map/leaf/pallas_call | solution.py:575
  20.9 4.6 %all-to-all-done.gathered = bf16[8,40,256]{2,1,0:T(8,128)(2,1)S(1)} async-done(((bf16[8,40,256]{2,1,0:T(8,128)(2,1)}), bf16[8,40,256]{2,1,0:T(8,128)(2,1)S(1)}, u32[]{:S(2)}, u32[]{:S(2)}) %all-to-all-start) | async-done | bytes 163872 | tf_op jit(solution)/shard_map/all_to_all | solution.py:592
  25.5 1.0 %hop.2 = (bf16[4,40,256]{2,1,0:T(8,128)(2,1)}, bf16[192,256]{1,0:T(8,128)(2,1)S(1)}, f32[96,64]{1,0:T(8,128)S(1)}) custom-call(bf16[8,40,256]{2,1,0:T(8,128)(2,1)S(1)} %all-to-all-done.gathered, bf16[3,224,256]{2,1,0:T(8,128)(2,1)S(1)} %get-tuple-element.48.selects, bf16[3,2,128,256]{3,2,1,0:T(8,128)(2,1)S(1)} %get-tuple-element.49.lifts), custom_call_target="tpu_custom_call" | custom-call | flops 100000000 | bytes 1048576 | tf_op jit(solution)/shard_map/hop/pallas_call | solution.py:600
  26.5 5.6 %all-to-all-start.1 = ((bf16[4,40,256]{2,1,0:T(8,128)(2,1)}), bf16[4,40,256]{2,1,0:T(8,128)(2,1)S(1)}, u32[]{:S(2)}, u32[]{:S(2)}) async-start(bf16[4,40,256]{2,1,0:T(8,128)(2,1)} %get-tuple-element.50), calls=%async_computation.1 | async-start | bytes 163840 | tf_op jit(solution)/shard_map/all_to_all | solution.py:592
  32.1 2.0 %leaf.3 = (f32[64,1024]{1,0:T(8,128)S(1)}, bf16[128,256]{1,0:T(8,128)(2,1)S(1)}) custom-call(s32[16,128]{1,0:T(8,128)S(1)} %bitcast.11, bf16[2048,256]{1,0:T(8,128)(2,1)S(1)} %copy-done, bf16[64,2048]{1,0:T(8,128)(2,1)S(1)} %copy-done.7, s32[8,32]{1,0:T(8,128)S(1)} %copy-done.4), custom_call_target="tpu_custom_call" | custom-call | flops 2000000000 | bytes 1048576 | tf_op jit(solution)/shard_map/leaf/pallas_call | solution.py:575
  34.2 2.2 %all-to-all-done.1.gathered = bf16[4,40,256]{2,1,0:T(8,128)(2,1)S(1)} async-done(((bf16[4,40,256]{2,1,0:T(8,128)(2,1)}), bf16[4,40,256]{2,1,0:T(8,128)(2,1)S(1)}, u32[]{:S(2)}, u32[]{:S(2)}) %all-to-all-start.1) | async-done | bytes 81952 | tf_op jit(solution)/shard_map/all_to_all | solution.py:592
  36.4 1.0 %hop.3 = (bf16[8,40,256]{2,1,0:T(8,128)(2,1)}, bf16[128,256]{1,0:T(8,128)(2,1)S(1)}, f32[64,64]{1,0:T(8,128)S(1)}) custom-call(bf16[4,40,256]{2,1,0:T(8,128)(2,1)S(1)} %all-to-all-done.1.gathered, bf16[3,224,256]{2,1,0:T(8,128)(2,1)S(1)} %get-tuple-element.48.selects, bf16[3,2,128,256]{3,2,1,0:T(8,128)(2,1)S(1)} %get-tuple-element.49.lifts), custom_call_target="tpu_custom_call" | custom-call | flops 100000000 | bytes 1048576 | tf_op jit(solution)/shard_map/hop/pallas_call | solution.py:600
  37.3 11.5 %all-to-all-start.2 = ((bf16[8,40,256]{2,1,0:T(8,128)(2,1)}), bf16[8,40,256]{2,1,0:T(8,128)(2,1)S(1)}, u32[]{:S(2)}, u32[]{:S(2)}) async-start(bf16[8,40,256]{2,1,0:T(8,128)(2,1)} %get-tuple-element.55), calls=%async_computation.2 | async-start | bytes 327680 | tf_op jit(solution)/shard_map/all_to_all | solution.py:592
  48.9 0.0 copy-start.5
  48.9 0.0 copy-start.8
  48.9 0.6 %terms.1.before = f32[32,64]{1,0:T(8,128)S(1)} custom-call(f32[3,96,32]{2,1,0:T(8,128)S(1)} %get-tuple-element.57.chains, bf16[64,256]{1,0:T(8,128)(2,1)S(1)} %get-tuple-element.58.refs_0_, f32[32,64]{1,0:T(8,128)S(1)} %get-tuple-element.59.refs_1_, bf16[192,256]{1,0:T(8,128)(2,1)S(1)} %get-tuple-element.60.refs_2_, f32[96,64]{1,0:T(8,128)S(1)} %get-tuple-element.61.refs_3_, ...), custom_call_target="tpu_custom_call" | custom-call | flops 100000000 | bytes 1048576 | tf_op jit(solution)/shard_map/terms/pallas_call | solution.py:628
  49.5 0.1 copy-done.5
  49.6 0.2 copy-done.8
  49.8 0.0 copy-start.1
  49.8 1.6 %far.1 = f32[256,128]{1,0:T(8,128)S(1)} custom-call(s32[7,32]{1,0:T(8,128)S(1)} %copy-done.5, f32[256,64]{1,0:T(8,128)S(1)} %copy-done.8, bf16[15,32,32]{2,1,0:T(8,128)(2,1)S(1)} %copy-done.2, bf16[128,256]{1,0:T(8,128)(2,1)S(1)} %get-tuple-element.65.refs_0_, bf16[128,256]{1,0:T(8,128)(2,1)S(1)} %get-tuple-element.66.refs_1_), custom_call_target="tpu_custom_call" | custom-call | flops 1000000000 | bytes 1048576 | tf_op jit(solution)/shard_map/far/pallas_call | solution.py:611
  51.4 0.0 copy-done.1
  51.4 2.7 %spread.1 = bf16[256,2048]{1,0:T(8,128)(2,1)S(1)} custom-call(s32[16,128]{1,0:T(8,128)S(1)} %bitcast.12, bf16[32,2048]{1,0:T(8,128)(2,1)S(1)} %bitcast.8, f32[256,128]{1,0:T(8,128)S(1)} %far.1, f32[64,1024]{1,0:T(8,128)S(1)} %get-tuple-element.67.refs_0_, f32[64,1024]{1,0:T(8,128)S(1)} %get-tuple-element.68.refs_1_), custom_call_target="tpu_custom_call" | custom-call | flops 2000000000 | bytes 1048576 | tf_op jit(solution)/shard_map/spread/pallas_call | solution.py:617
  54.2 0.6 all-to-all-done.2.gathered
  54.7 1.7 %final.1 = bf16[64,2048]{1,0:T(8,128)(2,1)} custom-call(bf16[8,40,256]{2,1,0:T(8,128)(2,1)S(1)} %all-to-all-done.2.gathered, bf16[3,224,256]{2,1,0:T(8,128)(2,1)S(1)} %get-tuple-element.48.selects, bf16[3,2,128,256]{3,2,1,0:T(8,128)(2,1)S(1)} %get-tuple-element.49.lifts, f32[3,96,32]{2,1,0:T(8,128)S(1)} %get-tuple-element.57.chains, ...), custom_call_target="tpu_custom_call" | custom-call | flops 100000000 | bytes 1048576 | tf_op jit(solution)/shard_map/final/pallas_call | solution.py:629
Async XLA Ops:
  0.0 6.0 %copy-start.9 = (s32[512,32]{0,1:T(8,128)S(1)}, s32[512,32]{0,1:T(8,128)}, u32[]{:S(2)}) copy-start(s32[512,32]{0,1:T(8,128)} %param.17) | copy-start | bytes 196612
  4.0 3.3 %collective-permute-start = (bf16[32,384]{1,0:T(8,128)(2,1)}, bf16[32,384]{1,0:T(8,128)(2,1)S(1)}, u32[]{:S(2)}, u32[]{:S(2)}) collective-permute-start(bf16[32,384]{1,0:T(8,128)(2,1)} %get-tuple-element.37.mine), channel_id=1, source_target_pairs={{0,1},{1,0},{2,3},{3,2},{4,5},{5,4},{6,7},{7,6},{8,9},{9,8},{10,11... | collective-permute-start | bytes 73736 | tf_op jit(solution)/shard_map/ppermute | solution.py:526
  6.0 0.7 %copy-start.10 = (bf16[32,384]{1,0:T(8,128)(2,1)S(1)}, bf16[32,384]{1,0:T(8,128)(2,1)}, u32[]{:S(2)}) copy-start(bf16[32,384]{1,0:T(8,128)(2,1)} %get-tuple-element.37.mine) | copy-start | bytes 73732
  8.1 7.2 %copy-start.2 = (bf16[15,32,32]{2,1,0:T(8,128)(2,1)S(1)}, bf16[15,32,32]{2,1,0:T(8,128)(2,1)}, u32[]{:S(2)}) copy-start(bf16[15,32,32]{2,1,0:T(8,128)(2,1)} %transfer.1) | copy-start | bytes 92164
  8.1 17.3 %all-to-all-start = ((bf16[8,40,256]{2,1,0:T(8,128)(2,1)}), bf16[8,40,256]{2,1,0:T(8,128)(2,1)S(1)}, u32[]{:S(2)}, u32[]{:S(2)}) async-start(bf16[8,40,256]{2,1,0:T(8,128)(2,1)} %get-tuple-element.40), calls=%async_computation | async-start | bytes 327680 | tf_op jit(solution)/shard_map/all_to_all | solution.py:592
  15.4 1.2 %copy-start.6 = (bf16[512,32,32]{0,2,1:T(8,128)(2,1)S(1)}, bf16[512,32,32]{0,2,1:T(8,128)(2,1)}, u32[]{:S(2)}) copy-start(bf16[512,32,32]{0,2,1:T(8,128)(2,1)} %param.16) | copy-start | bytes 3145732
  16.6 2.2 %copy-start = (bf16[2048,256]{1,0:T(8,128)(2,1)S(1)}, bf16[2048,256]{1,0:T(8,128)(2,1)}, u32[]{:S(2)}) copy-start(bf16[2048,256]{1,0:T(8,128)(2,1)} %emb.3) | copy-start | bytes 3145732
  16.6 2.2 %copy-start.3 = (s32[2048]{0:T(1024)S(1)}, s32[2048]{0:T(1024)}, u32[]{:S(2)}) copy-start(s32[2048]{0:T(1024)} %param.11) | copy-start | bytes 24580
  16.6 2.2 %copy-start.4 = (s32[8,32]{1,0:T(8,128)S(1)}, s32[8,32]{1,0:T(8,128)}, u32[]{:S(2)}) copy-start(s32[8,32]{1,0:T(8,128)} %skel.3) | copy-start | bytes 3076
  16.6 2.2 %copy-start.7 = (bf16[64,2048]{1,0:T(8,128)(2,1)S(1)}, bf16[64,2048]{1,0:T(8,128)(2,1)}, u32[]{:S(2)}) copy-start(bf16[64,2048]{1,0:T(8,128)(2,1)} %get-tuple-element.44.rhs_tree) | copy-start | bytes 786436
  26.5 9.9 %all-to-all-start.1 = ((bf16[4,40,256]{2,1,0:T(8,128)(2,1)}), bf16[4,40,256]{2,1,0:T(8,128)(2,1)S(1)}, u32[]{:S(2)}, u32[]{:S(2)}) async-start(bf16[4,40,256]{2,1,0:T(8,128)(2,1)} %get-tuple-element.50), calls=%async_computation.1 | async-start | bytes 163840 | tf_op jit(solution)/shard_map/all_to_all | solution.py:592
  37.3 17.4 %all-to-all-start.2 = ((bf16[8,40,256]{2,1,0:T(8,128)(2,1)}), bf16[8,40,256]{2,1,0:T(8,128)(2,1)S(1)}, u32[]{:S(2)}, u32[]{:S(2)}) async-start(bf16[8,40,256]{2,1,0:T(8,128)(2,1)} %get-tuple-element.55), calls=%async_computation.2 | async-start | bytes 327680 | tf_op jit(solution)/shard_map/all_to_all | solution.py:592
  48.9 0.7 %copy-start.5 = (s32[7,32]{1,0:T(8,128)S(1)}, s32[7,32]{1,0:T(8,128)}, u32[]{:S(2)}) copy-start(s32[7,32]{1,0:T(8,128)} %pick.1) | copy-start | bytes 2692
  48.9 0.9 %copy-start.8 = (f32[256,64]{1,0:T(8,128)S(1)}, f32[256,64]{1,0:T(8,128)}, u32[]{:S(2)}) copy-start(f32[256,64]{1,0:T(8,128)} %get-tuple-element.64.weights) | copy-start | bytes 196612
  49.8 1.6 %copy-start.1 = (bf16[2048,32]{0,1:T(8,128)(2,1)S(1)}, bf16[2048,32]{0,1:T(8,128)(2,1)}, u32[]{:S(2)}) copy-start(bf16[2048,32]{0,1:T(8,128)(2,1)} %param.12) | copy-start | bytes 393220

commit v6 on v5

--- a/solution.py
+++ b/solution.py
@@ -149,17 +149,17 @@
     joined = jnp.concatenate([rhs[:, b * leaf : (b + 1) * leaf] for b in range(blocks)], axis=0)
 
     def gather(l):
-        row = jnp.concatenate([order_row(order, l + j) for j in range(4)], axis=1)
+        row = jnp.concatenate([order_row(order, l + j) for j in range(8)], axis=1)
         low, high = row & (leaf - 1), row // leaf
-        found = dot(joined, one_hot(low == iota((leaf, 4 * leaf), 0)))
+        found = dot(joined, one_hot(low == iota((leaf, 8 * leaf), 0)))
         total = None
         for b in range(blocks):
             part = jnp.where(high == b, found[b * cols : (b + 1) * cols, :], 0.0)
             total = part if total is None else total + part
         picked = total.astype(BF16)
-        rhs_tree[:, l * leaf : (l + 4) * leaf] = picked
+        rhs_tree[:, l * leaf : (l + 8) * leaf] = picked
         found = []
-        for j in range(4):
+        for j in range(8):
             lanes = slice((l + j) * leaf, (l + j + 1) * leaf)
             found.append(dot_last(basis[:, lanes], picked[:, j * leaf : (j + 1) * leaf]))
             weights[(l + j) * rank : (l + j + 1) * rank, :] = found[-1]
@@ -171,9 +171,9 @@
 
     nodes, parents, pending = None, leaves, {}
     for l in range(leaves):
-        if l % 4 == 0:
+        if l % 8 == 0:
             group = gather(l)
-        node, q = group[l % 4], leaves + l
+        node, q = group[l % 8], leaves + l
         if l == 1:
             copies[6].wait()
         if l == leaves - 1:

time: 57 us -> 56.7 us (level)
  no operation moved by 1% of the time
where the time goes in v6:
time: 56.7 us; the launch traced here: 56.2 us
  starting transfers between devices  26.3 us (46%)
  Pallas kernels  19.7 us (35%)
  waiting for transfers between devices  7.78 us (14%)
  local copies, waits for them, and re-layouts  2.29 us (4%)
    all_to_all x3, starting transfers between devices, local(): gathered = lax.all_to_all(payload, 'leaf', 0, 0, axis_index_groups=groups)  24.4 us
    all_to_all x3, waiting for transfers between devices, local(): gathered = lax.all_to_all(payload, 'leaf', 0, 0, axis_index_groups=groups)  7.36 us
    pallas_call x2, Pallas kernels, leaf_part(): call(functools.partial(leaf_body, first, count, rank), (shape((cols, item...  4.1 us
    pallas_call x1, Pallas kernels, local(): call(functools.partial(pre_body, leaves), (shape((rank, width + 2 * cols)...  3.8 us
    pallas_call x1, Pallas kernels, local(): call(functools.partial(spread_body, len(parts), items // leaves, rank), s...  2.74 us
    unnamed x22, local copies, waits for them, and re-layouts  2.29 us
    pallas_call x1, Pallas kernels, local(): call(functools.partial(prep_body, devices, radices), (shape((stages, (2 *...  2.15 us
    pallas_call x2, Pallas kernels, local(): call(functools.partial(hop_body, stage, depth, rank, cols), (shape((radic...  1.96 us
  transfers between devices with their start and end apart: 4, of which 4 were waited for; matrix products, arithmetic and copies ran while one was open for 0% of the time, Pallas kernels for 20%

profile of v6, /device:TPU:2, one launch (start us, length us, event | category | flops | bytes accessed | tf_op | source)
XLA Modules:
  0.0 56.2 jit_solution(15893528150853613673)
XLA Ops:
  0.0 0.0 copy-start.9
  0.0 3.8 %pre.1 = (bf16[32,384]{1,0:T(8,128)(2,1)}, bf16[64,2048]{1,0:T(8,128)(2,1)}, f32[256,64]{1,0:T(8,128)}) custom-call(s32[16,128]{1,0:T(8,128)} %bitcast.9, s32[8,32]{1,0:T(8,128)} %skel.3, s32[7,32]{1,0:T(8,128)} %pick.1, bf16[64,2048]{1,0:T(8,128)(2,1)} %bitcast.16, bf16[32,2048]{1,0:T(8,128)(2,1)} %bitcast.7, bf16[15,32,32]{2,1,0:T(8,128)(2,1)} %transfer.1, ...), custom_call_target="tpu_custom_call" | custom-call | flops 100000000 | bytes 1048576 | tf_op jit(solution)/shard_map/pre/pallas_call | solution.py:514
  3.8 1.9 %collective-permute-start = (bf16[32,384]{1,0:T(8,128)(2,1)}, bf16[32,384]{1,0:T(8,128)(2,1)S(1)}, u32[]{:S(2)}, u32[]{:S(2)}) collective-permute-start(bf16[32,384]{1,0:T(8,128)(2,1)} %get-tuple-element.37.mine), channel_id=1, source_target_pairs={{0,1},{1,0},{2,3},{3,2},{4,5},{5,4},{6,7},{7,6},{8,9},{9,8},{10,11... | collective-permute-start | bytes 73736 | tf_op jit(solution)/shard_map/ppermute | solution.py:526
  5.7 0.0 copy-done.9
  5.7 0.0 copy-start.10
  5.8 0.7 %copy-done.10 = bf16[32,384]{1,0:T(8,128)(2,1)S(1)} copy-done((bf16[32,384]{1,0:T(8,128)(2,1)S(1)}, bf16[32,384]{1,0:T(8,128)(2,1)}, u32[]{:S(2)}) %copy-start.10) | copy-done | bytes 24600
  6.5 0.2 side.1
  6.7 0.4 collective-permute-done.other
  7.1 0.8 %pair.1 = (bf16[8,40,256]{2,1,0:T(8,128)(2,1)}, bf16[64,256]{1,0:T(8,128)(2,1)S(1)}, f32[32,64]{1,0:T(8,128)S(1)}) custom-call(bf16[32,64]{1,0:T(8,128)(2,1)S(1)} %get-tuple-element.38.hot, bf16[32,384]{1,0:T(8,128)(2,1)S(1)} %get-tuple-element.39.mine, bf16[32,384]{1,0:T(8,128)(2,1)S(1)} %collective-permute-done.other), custom_call_target="tpu_custom_call" | custom-call | flops 100000000 | bytes 1048576 | tf_op jit(solution)/shard_map/pair/pallas_call | solution.py:536
  7.9 0.0 copy-start.2
  7.9 7.2 %all-to-all-start = ((bf16[8,40,256]{2,1,0:T(8,128)(2,1)}), bf16[8,40,256]{2,1,0:T(8,128)(2,1)S(1)}, u32[]{:S(2)}, u32[]{:S(2)}) async-start(bf16[8,40,256]{2,1,0:T(8,128)(2,1)} %get-tuple-element.40), calls=%async_computation | async-start | bytes 327680 | tf_op jit(solution)/shard_map/all_to_all | solution.py:592
  15.1 0.0 copy-done.2
  15.1 0.0 copy-start.6
  15.2 1.2 %copy-done.6 = bf16[512,32,32]{0,2,1:T(8,128)(2,1)S(1)} copy-done((bf16[512,32,32]{0,2,1:T(8,128)(2,1)S(1)}, bf16[512,32,32]{0,2,1:T(8,128)(2,1)}, u32[]{:S(2)}) %copy-start.6) | copy-done | bytes 1048600
  16.4 0.0 copy-start
  16.4 0.0 copy-start.3
  16.4 0.0 copy-start.4
  16.4 0.0 copy-start.7
  16.4 2.1 %prep.1 = (bf16[3,224,256]{2,1,0:T(8,128)(2,1)S(1)}, bf16[3,2,128,256]{3,2,1,0:T(8,128)(2,1)S(1)}, f32[3,96,32]{2,1,0:T(8,128)S(1)}) custom-call(s32[1]{0:T(128)} %bitcast.me_ref, s32[32,512]{1,0:T(8,128)S(1)} %bitcast.15, bf16[32,32,512]{2,1,0:T(8,128)(2,1)S(1)} %bitcast.13, bf16[15,32,32]{2,1,0:T(8,128)(2,1)S(1)} %copy-done.2), custom_call_target="tpu_custom_call" | custom-call | flops 2000000000 | bytes 1048576 | tf_op jit(solution)/shard_map/prep/pallas_call | solution.py:553
  18.5 0.0 copy-done
  18.5 0.0 copy-done.3
  18.6 0.0 copy-done.4
  18.6 0.0 copy-done.7
  18.6 2.1 %leaf.2 = (f32[64,1024]{1,0:T(8,128)S(1)}, bf16[128,256]{1,0:T(8,128)(2,1)S(1)}) custom-call(s32[16,128]{1,0:T(8,128)S(1)} %bitcast.10, bf16[2048,256]{1,0:T(8,128)(2,1)S(1)} %copy-done, bf16[64,2048]{1,0:T(8,128)(2,1)S(1)} %copy-done.7, s32[8,32]{1,0:T(8,128)S(1)} %copy-done.4), custom_call_target="tpu_custom_call" | custom-call | flops 2000000000 | bytes 1048576 | tf_op jit(solution)/shard_map/leaf/pallas_call | solution.py:575
  20.6 4.6 %all-to-all-done.gathered = bf16[8,40,256]{2,1,0:T(8,128)(2,1)S(1)} async-done(((bf16[8,40,256]{2,1,0:T(8,128)(2,1)}), bf16[8,40,256]{2,1,0:T(8,128)(2,1)S(1)}, u32[]{:S(2)}, u32[]{:S(2)}) %all-to-all-start) | async-done | bytes 163872 | tf_op jit(solution)/shard_map/all_to_all | solution.py:592
  25.2 1.0 %hop.2 = (bf16[4,40,256]{2,1,0:T(8,128)(2,1)}, bf16[192,256]{1,0:T(8,128)(2,1)S(1)}, f32[96,64]{1,0:T(8,128)S(1)}) custom-call(bf16[8,40,256]{2,1,0:T(8,128)(2,1)S(1)} %all-to-all-done.gathered, bf16[3,224,256]{2,1,0:T(8,128)(2,1)S(1)} %get-tuple-element.48.selects, bf16[3,2,128,256]{3,2,1,0:T(8,128)(2,1)S(1)} %get-tuple-element.49.lifts), custom_call_target="tpu_custom_call" | custom-call | flops 100000000 | bytes 1048576 | tf_op jit(solution)/shard_map/hop/pallas_call | solution.py:600
  26.2 5.6 %all-to-all-start.1 = ((bf16[4,40,256]{2,1,0:T(8,128)(2,1)}), bf16[4,40,256]{2,1,0:T(8,128)(2,1)S(1)}, u32[]{:S(2)}, u32[]{:S(2)}) async-start(bf16[4,40,256]{2,1,0:T(8,128)(2,1)} %get-tuple-element.50), calls=%async_computation.1 | async-start | bytes 163840 | tf_op jit(solution)/shard_map/all_to_all | solution.py:592
  31.9 2.0 %leaf.3 = (f32[64,1024]{1,0:T(8,128)S(1)}, bf16[128,256]{1,0:T(8,128)(2,1)S(1)}) custom-call(s32[16,128]{1,0:T(8,128)S(1)} %bitcast.11, bf16[2048,256]{1,0:T(8,128)(2,1)S(1)} %copy-done, bf16[64,2048]{1,0:T(8,128)(2,1)S(1)} %copy-done.7, s32[8,32]{1,0:T(8,128)S(1)} %copy-done.4), custom_call_target="tpu_custom_call" | custom-call | flops 2000000000 | bytes 1048576 | tf_op jit(solution)/shard_map/leaf/pallas_call | solution.py:575
  33.9 2.2 %all-to-all-done.1.gathered = bf16[4,40,256]{2,1,0:T(8,128)(2,1)S(1)} async-done(((bf16[4,40,256]{2,1,0:T(8,128)(2,1)}), bf16[4,40,256]{2,1,0:T(8,128)(2,1)S(1)}, u32[]{:S(2)}, u32[]{:S(2)}) %all-to-all-start.1) | async-done | bytes 81952 | tf_op jit(solution)/shard_map/all_to_all | solution.py:592
  36.1 1.0 %hop.3 = (bf16[8,40,256]{2,1,0:T(8,128)(2,1)}, bf16[128,256]{1,0:T(8,128)(2,1)S(1)}, f32[64,64]{1,0:T(8,128)S(1)}) custom-call(bf16[4,40,256]{2,1,0:T(8,128)(2,1)S(1)} %all-to-all-done.1.gathered, bf16[3,224,256]{2,1,0:T(8,128)(2,1)S(1)} %get-tuple-element.48.selects, bf16[3,2,128,256]{3,2,1,0:T(8,128)(2,1)S(1)} %get-tuple-element.49.lifts), custom_call_target="tpu_custom_call" | custom-call | flops 100000000 | bytes 1048576 | tf_op jit(solution)/shard_map/hop/pallas_call | solution.py:600
  37.1 11.5 %all-to-all-start.2 = ((bf16[8,40,256]{2,1,0:T(8,128)(2,1)}), bf16[8,40,256]{2,1,0:T(8,128)(2,1)S(1)}, u32[]{:S(2)}, u32[]{:S(2)}) async-start(bf16[8,40,256]{2,1,0:T(8,128)(2,1)} %get-tuple-element.55), calls=%async_computation.2 | async-start | bytes 327680 | tf_op jit(solution)/shard_map/all_to_all | solution.py:592
  48.6 0.0 copy-start.5
  48.6 0.0 copy-start.8
  48.6 0.6 %terms.1.before = f32[32,64]{1,0:T(8,128)S(1)} custom-call(f32[3,96,32]{2,1,0:T(8,128)S(1)} %get-tuple-element.57.chains, bf16[64,256]{1,0:T(8,128)(2,1)S(1)} %get-tuple-element.58.refs_0_, f32[32,64]{1,0:T(8,128)S(1)} %get-tuple-element.59.refs_1_, bf16[192,256]{1,0:T(8,128)(2,1)S(1)} %get-tuple-element.60.refs_2_, f32[96,64]{1,0:T(8,128)S(1)} %get-tuple-element.61.refs_3_, ...), custom_call_target="tpu_custom_call" | custom-call | flops 100000000 | bytes 1048576 | tf_op jit(solution)/shard_map/terms/pallas_call | solution.py:628
  49.2 0.1 copy-done.5
  49.3 0.2 copy-done.8
  49.6 0.0 copy-start.1
  49.6 1.6 %far.1 = f32[256,128]{1,0:T(8,128)S(1)} custom-call(s32[7,32]{1,0:T(8,128)S(1)} %copy-done.5, f32[256,64]{1,0:T(8,128)S(1)} %copy-done.8, bf16[15,32,32]{2,1,0:T(8,128)(2,1)S(1)} %copy-done.2, bf16[128,256]{1,0:T(8,128)(2,1)S(1)} %get-tuple-element.65.refs_0_, bf16[128,256]{1,0:T(8,128)(2,1)S(1)} %get-tuple-element.66.refs_1_), custom_call_target="tpu_custom_call" | custom-call | flops 1000000000 | bytes 1048576 | tf_op jit(solution)/shard_map/far/pallas_call | solution.py:611
  51.2 0.0 copy-done.1
  51.2 2.7 %spread.1 = bf16[256,2048]{1,0:T(8,128)(2,1)S(1)} custom-call(s32[16,128]{1,0:T(8,128)S(1)} %bitcast.12, bf16[32,2048]{1,0:T(8,128)(2,1)S(1)} %bitcast.8, f32[256,128]{1,0:T(8,128)S(1)} %far.1, f32[64,1024]{1,0:T(8,128)S(1)} %get-tuple-element.67.refs_0_, f32[64,1024]{1,0:T(8,128)S(1)} %get-tuple-element.68.refs_1_), custom_call_target="tpu_custom_call" | custom-call | flops 2000000000 | bytes 1048576 | tf_op jit(solution)/shard_map/spread/pallas_call | solution.py:617
  53.9 0.6 all-to-all-done.2.gathered
  54.5 1.7 %final.1 = bf16[64,2048]{1,0:T(8,128)(2,1)} custom-call(bf16[8,40,256]{2,1,0:T(8,128)(2,1)S(1)} %all-to-all-done.2.gathered, bf16[3,224,256]{2,1,0:T(8,128)(2,1)S(1)} %get-tuple-element.48.selects, bf16[3,2,128,256]{3,2,1,0:T(8,128)(2,1)S(1)} %get-tuple-element.49.lifts, f32[3,96,32]{2,1,0:T(8,128)S(1)} %get-tuple-element.57.chains, ...), custom_call_target="tpu_custom_call" | custom-call | flops 100000000 | bytes 1048576 | tf_op jit(solution)/shard_map/final/pallas_call | solution.py:629
Async XLA Ops:
  0.0 5.7 %copy-start.9 = (s32[512,32]{0,1:T(8,128)S(1)}, s32[512,32]{0,1:T(8,128)}, u32[]{:S(2)}) copy-start(s32[512,32]{0,1:T(8,128)} %param.17) | copy-start | bytes 196612
  3.8 3.3 %collective-permute-start = (bf16[32,384]{1,0:T(8,128)(2,1)}, bf16[32,384]{1,0:T(8,128)(2,1)S(1)}, u32[]{:S(2)}, u32[]{:S(2)}) collective-permute-start(bf16[32,384]{1,0:T(8,128)(2,1)} %get-tuple-element.37.mine), channel_id=1, source_target_pairs={{0,1},{1,0},{2,3},{3,2},{4,5},{5,4},{6,7},{7,6},{8,9},{9,8},{10,11... | collective-permute-start | bytes 73736 | tf_op jit(solution)/shard_map/ppermute | solution.py:526
  5.7 0.7 %copy-start.10 = (bf16[32,384]{1,0:T(8,128)(2,1)S(1)}, bf16[32,384]{1,0:T(8,128)(2,1)}, u32[]{:S(2)}) copy-start(bf16[32,384]{1,0:T(8,128)(2,1)} %get-tuple-element.37.mine) | copy-start | bytes 73732
  7.9 7.2 %copy-start.2 = (bf16[15,32,32]{2,1,0:T(8,128)(2,1)S(1)}, bf16[15,32,32]{2,1,0:T(8,128)(2,1)}, u32[]{:S(2)}) copy-start(bf16[15,32,32]{2,1,0:T(8,128)(2,1)} %transfer.1) | copy-start | bytes 92164
  7.9 17.3 %all-to-all-start = ((bf16[8,40,256]{2,1,0:T(8,128)(2,1)}), bf16[8,40,256]{2,1,0:T(8,128)(2,1)S(1)}, u32[]{:S(2)}, u32[]{:S(2)}) async-start(bf16[8,40,256]{2,1,0:T(8,128)(2,1)} %get-tuple-element.40), calls=%async_computation | async-start | bytes 327680 | tf_op jit(solution)/shard_map/all_to_all | solution.py:592
  15.1 1.2 %copy-start.6 = (bf16[512,32,32]{0,2,1:T(8,128)(2,1)S(1)}, bf16[512,32,32]{0,2,1:T(8,128)(2,1)}, u32[]{:S(2)}) copy-start(bf16[512,32,32]{0,2,1:T(8,128)(2,1)} %param.16) | copy-start | bytes 3145732
  16.4 2.2 %copy-start = (bf16[2048,256]{1,0:T(8,128)(2,1)S(1)}, bf16[2048,256]{1,0:T(8,128)(2,1)}, u32[]{:S(2)}) copy-start(bf16[2048,256]{1,0:T(8,128)(2,1)} %emb.3) | copy-start | bytes 3145732
  16.4 2.2 %copy-start.3 = (s32[2048]{0:T(1024)S(1)}, s32[2048]{0:T(1024)}, u32[]{:S(2)}) copy-start(s32[2048]{0:T(1024)} %param.11) | copy-start | bytes 24580
  16.4 2.2 %copy-start.4 = (s32[8,32]{1,0:T(8,128)S(1)}, s32[8,32]{1,0:T(8,128)}, u32[]{:S(2)}) copy-start(s32[8,32]{1,0:T(8,128)} %skel.3) | copy-start | bytes 3076
  16.4 2.2 %copy-start.7 = (bf16[64,2048]{1,0:T(8,128)(2,1)S(1)}, bf16[64,2048]{1,0:T(8,128)(2,1)}, u32[]{:S(2)}) copy-start(bf16[64,2048]{1,0:T(8,128)(2,1)} %get-tuple-element.44.rhs_tree) | copy-start | bytes 786436
  26.2 9.9 %all-to-all-start.1 = ((bf16[4,40,256]{2,1,0:T(8,128)(2,1)}), bf16[4,40,256]{2,1,0:T(8,128)(2,1)S(1)}, u32[]{:S(2)}, u32[]{:S(2)}) async-start(bf16[4,40,256]{2,1,0:T(8,128)(2,1)} %get-tuple-element.50), calls=%async_computation.1 | async-start | bytes 163840 | tf_op jit(solution)/shard_map/all_to_all | solution.py:592
  37.1 17.4 %all-to-all-start.2 = ((bf16[8,40,256]{2,1,0:T(8,128)(2,1)}), bf16[8,40,256]{2,1,0:T(8,128)(2,1)S(1)}, u32[]{:S(2)}, u32[]{:S(2)}) async-start(bf16[8,40,256]{2,1,0:T(8,128)(2,1)} %get-tuple-element.55), calls=%async_computation.2 | async-start | bytes 327680 | tf_op jit(solution)/shard_map/all_to_all | solution.py:592
  48.6 0.7 %copy-start.5 = (s32[7,32]{1,0:T(8,128)S(1)}, s32[7,32]{1,0:T(8,128)}, u32[]{:S(2)}) copy-start(s32[7,32]{1,0:T(8,128)} %pick.1) | copy-start | bytes 2692
  48.6 0.9 %copy-start.8 = (f32[256,64]{1,0:T(8,128)S(1)}, f32[256,64]{1,0:T(8,128)}, u32[]{:S(2)}) copy-start(f32[256,64]{1,0:T(8,128)} %get-tuple-element.64.weights) | copy-start | bytes 196612
  49.6 1.6 %copy-start.1 = (bf16[2048,32]{0,1:T(8,128)(2,1)S(1)}, bf16[2048,32]{0,1:T(8,128)(2,1)}, u32[]{:S(2)}) copy-start(bf16[2048,32]{0,1:T(8,128)(2,1)} %param.12) | copy-start | bytes 393220
